TPU v7x, 32 devices: a whole 2x2x4 slice. The times are simulated.
32 devices in a mesh: dp: 8 (over z, x), cls: 4 (over y, core).
Axes of the slice: x: 2, y: 2, z: 4, core: 2. Of those that a mesh axis runs over, the one named last changes fastest.
Arguments:
- images: bfloat16 [4096, 128, 128], P('dp'), may hold values from -6 to 6
- references: bfloat16 [2304, 8192], P(('dp', 'cls')), may hold values from -0.0625 to 0.0625
- best_class: int32 [4096, 4], P('dp'), may hold values from 0 to 63, as said below
- best_rot: int32 [4096, 4], P('dp'), may hold values from 0 to 35
- prior: float32 [4096, 4], P('dp'), may hold values from 0.1 to 1
- precision: float32 [4096], P('dp'), may hold values from 0.5 to 200
Outputs:
- class_sums: float32 [2304, 8192], P(('dp', 'cls'))
Inputs may be any that keep to these rules, and one draw needn't show every extreme that they name: In each aligned block of 512 particles, the panels best_class * 36 + best_rot of at most 128 of the block's pairs lie among the 72 panels of one holder (panel // 72); one holder reaches exactly 128 in every block.
All inputs are finite; a program needn't handle non-finite values.
Results may differ from a plain program's by a relative error of at most 0.012.
The roundings to bfloat16 on the way count: a program that leaves them out, or rounds other values in their place, can miss the bound.
Values may be sent and summed in bfloat16 or wider, within the bound.
No kernel may reach another device: no remote copies, remote signals or barrier semaphores. Data moves between devices by JAX's collectives and lax.ppermute only.
A program may use at most 192 MiB of HBM per device.

v0:
```python
import math

import jax
import jax.numpy as jnp
from jax import lax
from jax.sharding import PartitionSpec as P

KWIN = 64
ROTS = 36
TOP = 4


neg_large = -1e30


def transform_tables(box_size, kwin_size):
    positions = jnp.arange(box_size, dtype=jnp.float32)
    frequencies = jnp.arange(kwin_size, dtype=jnp.float32) - float(kwin_size // 2)
    phase_x = 2.0 * math.pi * positions[:, None] * frequencies[None, :] / box_size
    x_table = (jnp.concatenate([jnp.cos(phase_x), -jnp.sin(phase_x)], axis=1) / box_size).astype(
        jnp.bfloat16
    )
    angle_y = 2.0 * math.pi * frequencies[:, None] * positions[None, :] / box_size
    cosine = jnp.cos(angle_y)
    sine_part = jnp.sin(angle_y)
    real_rows = jnp.stack([cosine, sine_part], axis=1)
    imag_rows = jnp.stack([-sine_part, cosine], axis=1)
    y_table = jnp.stack([real_rows, imag_rows], axis=0).astype(jnp.bfloat16)
    return (x_table, y_table)


def to_spectra(image_block, x_table, y_table):
    particle_count = image_block.shape[0]
    box_size = image_block.shape[1]
    flat_images = image_block.reshape(particle_count * box_size, box_size)
    half_transform = jnp.dot(flat_images, x_table, preferred_element_type=jnp.float32).astype(
        jnp.bfloat16
    )
    half_transform = half_transform.reshape(particle_count, box_size, 2, KWIN)
    spectrum = jnp.einsum(
        "pyck,oqcy->pkoq", half_transform, y_table, preferred_element_type=jnp.float32
    )
    return spectrum.reshape(particle_count, 2 * KWIN * KWIN).astype(jnp.bfloat16)


def on_device(images, references, best_class, best_rot, prior, precision):
    box_size = images.shape[1]
    pan_dev = references.shape[0]
    features = references.shape[1]
    cls_count = lax.axis_size("cls")
    group = lax.axis_index("cls")
    x_table, y_table = transform_tables(box_size, KWIN)
    spectrum = to_spectra(images, x_table, y_table)
    raw_scores = lax.dot_general(
        spectrum,
        lax.all_gather(references, "dp", axis=0, tiled=True),
        (((1,), (1,)), ((), ())),
        preferred_element_type=jnp.float32,
    )
    panel_ids = best_class * ROTS + best_rot
    owner_ids = panel_ids // pan_dev
    owned = owner_ids % cls_count == group
    local_ids = jnp.where(owned, owner_ids // cls_count * pan_dev + panel_ids % pan_dev, 0)
    picked = jnp.take_along_axis(raw_scores, local_ids, axis=1) * precision[:, None]
    masked = jnp.where(owned, picked, neg_large)
    peak_value = lax.pmax(jnp.max(masked, axis=1), "cls")
    partial_value = jnp.sum(
        jnp.where(owned, prior * jnp.exp(masked - peak_value[:, None]), 0.0), axis=1
    )
    denominator = lax.psum(partial_value, "cls")
    posterior = prior * jnp.exp(masked - peak_value[:, None]) / denominator[:, None]
    weight = jnp.where(owned, posterior, 0.0).astype(jnp.bfloat16)
    targets = jnp.arange(lax.axis_size("dp") * pan_dev)
    partial_sums = jnp.zeros((lax.axis_size("dp") * pan_dev, features), jnp.float32)
    for member in range(TOP):
        hit = (targets[:, None] == local_ids[:, member][None, :]) & owned[:, member][None, :]
        selector = jnp.where(hit, weight[:, member][None, :], 0.0)
        partial_sums = partial_sums + jnp.dot(
            selector, spectrum, preferred_element_type=jnp.float32
        )
    return lax.psum_scatter(
        partial_sums.astype(jnp.bfloat16), "dp", scatter_dimension=0, tiled=True
    ).astype(jnp.float32)


def solution(mesh):
    in_specs = (
        P("dp", None, None),
        P(("dp", "cls"), None),
        P("dp", None),
        P("dp", None),
        P("dp", None),
        P("dp"),
    )
    out_specs = P(("dp", "cls"), None)
    return jax.shard_map(
        on_device, mesh=mesh, in_specs=in_specs, out_specs=out_specs, check_vma=False
    )
```

profile of v0, /device:TPU:0, one launch (start us, length us, event | category | flops | bytes accessed | tf_op | source)
XLA Modules:
  0.0 417.2 jit_solution(12786692308508488045)
XLA Ops:
  6.5 0.7 all-gather.2.cloned.1.call-update
  7.3 0.0 reduce-scatter.2.cloned.1.call-start
  7.3 0.8 bitcast_or_fusion
  8.1 0.1 copy.27
  8.2 0.2 reshape.131
  8.4 0.2 fusion.43
  8.6 14.6 %fusion.2 = bf16[16,8,512,128]{3,1,2,0:T(8,128)(2,1)} fusion(bf16[65536,128]{1,0:T(8,128)(2,1)} %bitcast.36, f32[128,64]{0,1:T(8,128)S(1)} %get-tuple-element.25, f32[128,64]{0,1:T(8,128)S(1)} %get-tuple-element.24), kind=kOutput, calls=%fused_computation.6 | convolution fusion | flops 2155921408 | bytes 33619968 | tf_op jit(solution)/shard_map/dot_general | solution.py:36
  23.3 15.1 %copy.33 = bf16[16,8,512,128]{3,2,1,0:T(8,128)(2,1)} copy(bf16[16,8,512,128]{3,1,2,0:T(8,128)(2,1)} %fusion.2) | data formatting | bytes 33554432
  38.4 0.2 fusion.41
  38.7 11.1 %bitcast_convert_fusion = bf16[512,64,2,64]{0,3,2,1:T(8,128)(2,1)} fusion(bf16[512,128,2,64,1]{1,0,3,2,4:T(8,128)(2,1)} %bitcast.37, bf16[1,64,2,128]{3,1,2,0:T(8,128)(2,1)S(1)} %get-tuple-element.19, bf16[1,64,2,128]{3,1,2,0:T(8,128)(2,1)S(1)} %get-tuple-element.18), kind=kOutput, calls=%fused_computation.3 | convolution fusion | flops 2151809024 | bytes 25231360 | tf_op jit(solution)/shard_map/pyck,oqcy->pkoq/dot_general | solution.py:40
  49.8 100.5 %all-gather.2.cloned.1.call-done = bf16[576,8192]{1,0:T(8,128)(2,1)} async-done(((bf16[72,8192]{1,0:T(8,128)(2,1)}), bf16[576,8192]{1,0:T(8,128)(2,1)}) %all-gather.2.cloned.1.call-update) | async-done | bytes 9437200 | tf_op jit(solution)/shard_map/all_gather | solution.py:56
  150.3 10.0 %fusion.62 = f32[512,576]{0,1:T(8,128)S(1)} fusion(bf16[576,8192]{1,0:T(8,128)(2,1)} %all-gather.2.cloned.1.call-done, bf16[512,8192]{0,1:T(8,128)(2,1)} %bitcast.38), kind=kOutput, calls=%fused_computation.99 | convolution fusion | flops 4831838208 | bytes 19005440 | tf_op jit(solution)/shard_map/dot_general | solution.py:54
  160.4 16.8 %gather_fusion = f32[2048]{0:T(1024)S(1)} fusion(f32[512,576]{0,1:T(8,128)S(1)} %fusion.62, s32[2048]{0:T(1024)S(1)} %reshape.131), kind=kCustom, calls=%fused_computation | custom fusion | bytes 32768 | tf_op jit(solution)/shard_map/jit(take_along_axis)/gather | solution.py:64
  177.2 0.3 reshape.134
  177.4 0.1 copy.28
  177.6 6.2 %pmax.7 = f32[512]{0:T(512)S(1)} all-reduce(f32[512]{0:T(512)S(1)} %get-tuple-element.13), channel_id=1, replica_groups=mesh['dp'=8,'cls'=4] {'cls'}, use_global_device_ids=true, to_apply=%region_1.2 | all-reduce | flops 512 | bytes 4096 | tf_op jit(solution)/shard_map/pmax | solution.py:66
  183.8 6.3 %psum.7 = f32[512]{0:T(512)S(1)} all-reduce(f32[512]{0:T(512)S(1)} %select_reduce_fusion), channel_id=1, replica_groups=mesh['dp'=8,'cls'=4] {'cls'}, use_global_device_ids=true, to_apply=%region_3.4 | all-reduce | flops 512 | bytes 4096 | tf_op jit(solution)/shard_map/psum | solution.py:70
  190.1 12.7 %fusion.14 = f32[576,8192]{1,0:T(8,128)} fusion(bf16[512,8192]{0,1:T(8,128)(2,1)} %bitcast.39, s32[512]{0:T(512)S(1)} %bitcast.46, pred[512]{0:T(512)(128)(4,1)S(1)} %get-tuple-element.10, bf16[512]{0:T(512)(128)(2,1)S(1)} %get-tuple-element.6), kind=kOutput, calls=%fused_computation.19 | convolution fusion | flops 4832722944 | bytes 27266560 | tf_op jit(solution)/shard_map/dot_general | solution.py:78
  202.8 9.0 %fusion.16 = f32[576,8192]{1,0:T(8,128)} fusion(bf16[512,8192]{0,1:T(8,128)(2,1)S(1)} %bitcast.41, s32[512]{0:T(512)S(1)} %bitcast.45, pred[512]{0:T(512)(128)(4,1)S(1)} %get-tuple-element.11, bf16[512]{0:T(512)(128)(2,1)S(1)} %get-tuple-element.7), kind=kOutput, calls=%fused_computation.20 | convolution fusion | flops 4832722944 | bytes 27266560 | tf_op jit(solution)/shard_map/dot_general | solution.py:78
  211.8 9.1 %fusion.18 = f32[576,8192]{1,0:T(8,128)} fusion(bf16[512,8192]{0,1:T(8,128)(2,1)S(1)} %bitcast.42, s32[512]{0:T(512)S(1)} %bitcast.44, pred[512]{0:T(512)(128)(4,1)S(1)} %get-tuple-element.12, bf16[512]{0:T(512)(128)(2,1)S(1)} %get-tuple-element.8), kind=kOutput, calls=%fused_computation.21 | convolution fusion | flops 4832722944 | bytes 27266560 | tf_op jit(solution)/shard_map/dot_general | solution.py:78
  220.9 25.3 %add_convert_fusion = bf16[576,8192]{1,0:T(8,128)(2,1)} fusion(f32[576,8192]{1,0:T(8,128)} %fusion.14, f32[576,8192]{1,0:T(8,128)} %fusion.18, f32[576,8192]{1,0:T(8,128)} %fusion.16, bf16[512,8192]{0,1:T(8,128)(2,1)} %bitcast.40, s32[512]{0:T(512)S(1)} %bitcast.43, pred[512]{0:T(512)(128)(4,1)S(1)} %get-tuple-element.9, bf16[512]{0:T(512)(128)(2,1)S(1)} %get-tuple-element.5), kind=kOutput, calls=%fused_computation.2 | convolution fusion | flops 4851597312 | bytes 74452480 | tf_op jit(solution)/shard_map/dot_general | solution.py:78
  246.2 0.0 reduce-scatter.2.cloned.1.call-update
  246.2 161.3 %reduce-scatter.2.cloned.1.call-done = bf16[72,8192]{1,0:T(8,128)(2,1)} async-done(((bf16[576,8192]{1,0:T(8,128)(2,1)}), bf16[72,8192]{1,0:T(8,128)(2,1)}) %reduce-scatter.2.cloned.1.call-update) | async-done | bytes 1179664 | tf_op jit(solution)/shard_map/reduce_scatter | solution.py:81
  407.5 2.9 convert_element_type.37
  (17 shorter events, 0.2 us)
Async XLA Ops:
  6.5 143.8 %all-gather.2.cloned.1.call-start = ((), (), s32[]{:S(2)}) async-start(), calls=%async_computation.1 | async-start | bytes 10616832 | tf_op jit(solution)/shard_map/all_gather | solution.py:56
  7.3 400.2 %reduce-scatter.2.cloned.1.call-start = ((), (), s32[]{:S(2)}) async-start(), calls=%async_computation.2 | async-start | bytes 10616832 | tf_op jit(solution)/shard_map/reduce_scatter | solution.py:81
  160.4 17.2 %copy-start.2 = (f32[512]{0:T(512)S(1)}, f32[512]{0:T(512)}, u32[]{:S(2)}) copy-start(f32[512]{0:T(512)} %param.11) | copy-start | bytes 6148
  160.4 23.4 %copy-start.1 = (f32[512,4]{0,1:T(4,128)S(1)}, f32[512,4]{0,1:T(4,128)}, u32[]{:S(2)}) copy-start(f32[512,4]{0,1:T(4,128)} %param.10) | copy-start | bytes 24580
  190.1 12.7 %copy-start = (bf16[512,64,2,64]{0,3,2,1:T(8,128)(2,1)S(1)}, bf16[512,64,2,64]{0,3,2,1:T(8,128)(2,1)}, u32[]{:S(2)}) copy-start(bf16[512,64,2,64]{0,3,2,1:T(8,128)(2,1)} %bitcast_convert_fusion) | copy-start | bytes 25165828
Sparse Core Ops, SparseCore 0:
  9.5 140.7 all-gather.1
  246.3 161.1 reduce-scatter.1
where the time goes:
time: 418 us; the launch traced here: 417 us
  waiting for transfers between devices  263 us (63%)
  matrix products  91.8 us (22%)
  local copies, waits for them, and re-layouts  32.7 us (8%)
  between operations  13.5 us (3%)
  blocking collectives  12.4 us (3%)
    reduce_scatter x1, waiting for transfers between devices, on_device(): lax.psum_scatter(partial_sums.astype(jnp.bfloat16), 'dp', scatter_dimensi...  161 us
    all_gather x1, waiting for transfers between devices, on_device(): lax.all_gather(references, 'dp', axis=0, tiled=True)  101 us
    dot_general x4, matrix products, on_device(): jnp.dot(selector, spectrum, preferred_element_type=jnp.float32)  56 us
    gather x5, local copies, waits for them, and re-layouts, on_device(): jnp.take_along_axis(raw_scores, local_ids, axis=1) * precision[:, None]  17.5 us
    unnamed x7, local copies, waits for them, and re-layouts  15.1 us
    dot_general x1, matrix products, to_spectra(): jnp.dot(flat_images, x_table, preferred_element_type=jnp.float32)  14.6 us
    dot_general x1, matrix products, to_spectra(): jnp.einsum('pyck,oqcy->pkoq', half_transform, y_table, preferred_element_...  11.1 us
    dot_general x1, matrix products, on_device(): lax.dot_general(spectrum, lax.all_gather(references, 'dp', axis=0, tiled=...  10 us
  transfers between devices with their start and end apart: 2, of which 2 were waited for; matrix products, arithmetic and copies ran while one was open for 10% of the time, Pallas kernels for 0%

commit v1 on v0

v1 whole, which is shorter than its diff:
```python
import functools
import math

import numpy as np
import jax
import jax.numpy as jnp
from jax import lax
from jax.experimental import pallas as pl
from jax.experimental.pallas import tpu as pltpu
from jax.sharding import PartitionSpec as P

KWIN = 64
HALF = KWIN // 2
ROTS = 36
TOP = 4
LANES = 2 * KWIN
UNIQUE = (HALF + 1) * LANES
ROW_PAD = 72
VMEM_BYTES = 24 * 1024 * 1024
CUT = 17


def half_tables(box):
    positions = np.arange(box, dtype=np.float32)
    frequencies = np.arange(KWIN, dtype=np.float32) - float(HALF)
    phase_x = (2.0 * math.pi * positions[:, None] * frequencies[None, : HALF + 1] / box).astype(np.float32)
    x_rows = np.zeros((ROW_PAD, box), np.float32)
    x_rows[: HALF + 1] = np.cos(phase_x).T / box
    x_rows[HALF + 1 : 2 * HALF + 2] = -np.sin(phase_x).T / box
    angle = (2.0 * math.pi * positions[:, None] * frequencies[None, :] / box).astype(np.float32)
    cosine, sine = np.cos(angle), np.sin(angle)
    y_rows = np.zeros((2 * box, 2 * LANES), np.float32)
    y_rows[:box, :KWIN] = cosine
    y_rows[:box, KWIN:LANES] = -sine
    y_rows[box:, :KWIN] = sine
    y_rows[box:, KWIN:LANES] = cosine
    y_rows[:box, LANES : LANES + KWIN] = cosine[:, :1]
    y_rows[:box, LANES + KWIN :] = -sine[:, :1]
    y_rows[box:, LANES : LANES + KWIN] = -sine[:, :1]
    y_rows[box:, LANES + KWIN :] = -cosine[:, :1]
    return jnp.asarray(x_rows, jnp.bfloat16), jnp.asarray(y_rows, jnp.bfloat16)


def mirror_matrix():
    m = np.zeros((LANES, LANES), np.float32)
    for q in range(1, KWIN):
        m[KWIN - q, q] = 1.0
        m[LANES - q, KWIN + q] = -1.0
    return jnp.asarray(m, jnp.bfloat16)


def lane_q(shape):
    return lax.broadcasted_iota(jnp.int32, shape, 1) % KWIN


def full_spec(shape):
    return pl.BlockSpec(shape, lambda *_: (0,) * len(shape))


def params(**kw):
    return pltpu.CompilerParams(vmem_limit_bytes=VMEM_BYTES, **kw)


def group(k):
    return slice(k * LANES, (k + 1) * LANES)


def fold_kernel(r_ref, m_ref, *outs):
    rows = r_ref.shape[0]
    q = lane_q((rows, LANES))
    mirror = m_ref[...]
    flip = lambda v: jnp.dot(v, mirror, preferred_element_type=jnp.float32)

    def put(k, value):
        for out_ref, first, last in zip(outs, (0, CUT), (CUT, HALF + 1)):
            if first <= k < last:
                out_ref[:, group(k - first)] = value.astype(out_ref.dtype)

    put(0, r_ref[:, group(0)])
    centre = r_ref[:, group(HALF)]
    special = centre.astype(jnp.float32)
    special = special + jnp.where((q >= 1) & (q < HALF), flip(centre), 0.0)
    for k in range(1, HALF):
        other = r_ref[:, group(KWIN - k)]
        put(k, r_ref[:, group(k)].astype(jnp.float32) + flip(other))
        edge = pltpu.roll(other.astype(jnp.float32), KWIN - k, 1)
        special = jnp.where(q == KWIN - k, edge, special)
    put(HALF, special)


def widths():
    return CUT * LANES, UNIQUE - CUT * LANES


def fold(references, mirror):
    rows = references.shape[0]
    return pl.pallas_call(
        fold_kernel,
        out_shape=[jax.ShapeDtypeStruct((rows, w), jnp.bfloat16) for w in widths()],
        compiler_params=params(),
        name="fold",
    )(references, mirror)


def unfold_kernel(m_ref, *rest):
    terms, out_ref = rest[:-1], rest[-1]
    rows = out_ref.shape[0]
    q = lane_q((rows, LANES))
    mirror = m_ref[...]
    count = len(terms) // 2

    def total(k):
        chosen, at = (terms[:count], k) if k < CUT else (terms[count:], k - CUT)
        return sum(t[:, group(at)].astype(jnp.float32) for t in chosen)

    def flip(v):
        high = v.astype(jnp.bfloat16)
        low = (v - high.astype(jnp.float32)).astype(jnp.bfloat16)
        return jnp.dot(high, mirror, preferred_element_type=jnp.float32) + jnp.dot(
            low, mirror, preferred_element_type=jnp.float32
        )

    special = total(HALF)
    out_ref[:, group(0)] = total(0)
    out_ref[:, group(HALF)] = jnp.where(q <= HALF, special, flip(special))
    for k in range(1, HALF):
        value = total(k)
        out_ref[:, group(k)] = value
        edge = pltpu.roll(special, LANES - (KWIN - k), 1)
        out_ref[:, group(KWIN - k)] = jnp.where(q == 0, edge, flip(value))


def unfold(left, right, mirror):
    terms = list(left) + list(right)
    rows = terms[0].shape[0]
    return pl.pallas_call(
        unfold_kernel,
        out_shape=jax.ShapeDtypeStruct((rows, KWIN * LANES), jnp.float32),
        compiler_params=params(),
        name="unfold",
    )(mirror, *terms)


def dft_kernel(img_ref, x_ref, y_ref, *rest):
    out_ref, rows_scratch, lhs_scratch = rest[-3:]
    tile, box, _ = img_ref.shape
    x_rows = x_ref[...]
    step = 8
    for start in range(0, tile, step):
        pixels = img_ref[start : start + step].reshape(step * box, box)
        h = lax.dot_general(
            x_rows, pixels, (((1,), (1,)), ((), ())), preferred_element_type=jnp.float32
        )
        for i in range(step):
            at = (start + i) * ROW_PAD
            rows_scratch[at : at + ROW_PAD, :] = h[:, i * box : (i + 1) * box]
    for k in range(HALF + 1):
        for c in range(2):
            j = c * (HALF + 1) + k
            picked = rows_scratch[pl.ds(j, tile, stride=ROW_PAD), :]
            lhs_scratch[k * tile : (k + 1) * tile, c * box : (c + 1) * box] = picked.astype(jnp.bfloat16)
    y_rows = y_ref[...]
    q = lane_q((tile, LANES))
    special = jnp.zeros((tile, LANES), jnp.float32)
    batch = 11
    for k in range(HALF + 1):
        if k % batch == 0:
            many = jnp.dot(
                lhs_scratch[k * tile : (k + batch) * tile, :], y_rows, preferred_element_type=jnp.float32
            )
        both = many[(k % batch) * tile : (k % batch + 1) * tile]
        value = both[:, :LANES]
        if k < HALF:
            out_ref[:, group(k)] = value.astype(jnp.bfloat16)
        else:
            special = jnp.where(q <= HALF, value, special)
        if 0 < k < HALF:
            special = jnp.where(q == KWIN - k, both[:, LANES:], special)
    out_ref[:, group(HALF)] = special.astype(jnp.bfloat16)


def dft(images, x_rows, y_rows, tile, part=0, parts=1, earlier=None):
    count, box, _ = images.shape
    steps = count // (tile * parts)
    first = part * steps
    operands = [images, x_rows, y_rows]
    in_specs = [
        pl.BlockSpec((tile, box, box), lambda i: (first + i, 0, 0)),
        full_spec(x_rows.shape),
        full_spec(y_rows.shape),
    ]
    aliases = {}
    if earlier is not None:
        operands.append(earlier)
        in_specs.append(pl.BlockSpec(memory_space=pl.ANY))
        aliases = {3: 0}
    return pl.pallas_call(
        dft_kernel,
        grid=(steps,),
        in_specs=in_specs,
        out_specs=pl.BlockSpec((tile, UNIQUE), lambda i: (first + i, 0)),
        out_shape=jax.ShapeDtypeStruct((count, UNIQUE), jnp.bfloat16),
        scratch_shapes=[
            pltpu.VMEM((tile * ROW_PAD, box), jnp.float32),
            pltpu.VMEM(((HALF + 1) * tile, 2 * box), jnp.bfloat16),
        ],
        input_output_aliases=aliases,
        cost_estimate=pl.CostEstimate(
            flops=count // parts * (2 * box * box * ROW_PAD + 2 * (HALF + 1) * 2 * box * LANES * 2),
            bytes_accessed=2 * count // parts * (box * box + UNIQUE),
            transcendentals=0,
        ),
        compiler_params=params(),
        name="dft",
    )(*operands)


def stacked_rows(at, base_ref, rows, particles):
    parts = [
        lax.broadcasted_iota(jnp.int32, (rows, particles), 0) + base_ref[n] for n in at
    ]
    return jnp.concatenate(parts, axis=0) if len(parts) > 1 else parts[0]


def score_kernel(at, first, base_ref, spec_ref, panel_ref, before_ref, *rest):
    refs, out_ref = rest[:-1], rest[-1]
    particles = spec_ref.shape[0]
    rows, width = refs[0].shape
    block = refs[0][...] if len(refs) == 1 else jnp.concatenate([r[...] for r in refs], axis=0)
    s = lax.dot_general(
        block,
        spec_ref[:, first : first + width],
        (((1,), (1,)), ((), ())),
        preferred_element_type=jnp.float32,
    )
    row = stacked_rows(at, base_ref, rows, particles)
    for t in range(TOP):
        hit = row == panel_ref[t : t + 1, :]
        picked = jnp.sum(jnp.where(hit, s, 0.0), axis=0, keepdims=True)
        out_ref[t : t + 1, :] = before_ref[t : t + 1, :] + picked


def score(bases, at, piece, spectrum, panel, before, refs):
    rows, width = refs[0].shape
    particles = spectrum.shape[0]
    return pl.pallas_call(
        functools.partial(score_kernel, at, piece * CUT * LANES),
        in_specs=[pl.BlockSpec(memory_space=pltpu.SMEM)]
        + [pl.BlockSpec(memory_space=pltpu.VMEM)] * (3 + len(refs)),
        out_shape=jax.ShapeDtypeStruct(panel.shape, jnp.float32),
        cost_estimate=pl.CostEstimate(
            flops=2 * len(refs) * rows * particles * width * 2,
            bytes_accessed=2 * width * (particles + rows * len(refs)),
            transcendentals=0,
        ),
        compiler_params=params(),
        name="score",
    )(bases, spectrum, panel, before, *refs)


def weight_kernel(scores_ref, prior_ref, precision_ref, out_ref):
    value = jnp.sum(scores_ref[...], axis=0) * precision_ref[...]
    unscaled = prior_ref[...] * jnp.exp(value - jnp.max(value, axis=0, keepdims=True))
    weight = unscaled / jnp.sum(unscaled, axis=0, keepdims=True)
    out_ref[...] = weight.astype(jnp.bfloat16).astype(jnp.float32)


def weights_of(scores, prior, precision):
    return pl.pallas_call(
        weight_kernel,
        out_shape=jax.ShapeDtypeStruct(prior.shape, jnp.float32),
        compiler_params=params(),
        name="weights",
    )(scores, prior, precision)


def sums_kernel(at, first, base_ref, weight_ref, panel_ref, spec_ref, *outs):
    particles = spec_ref.shape[0]
    rows, width = outs[0].shape
    row = stacked_rows(at, base_ref, rows, particles)
    select = jnp.zeros(row.shape, jnp.float32)
    for t in range(TOP):
        select = select + jnp.where(row == panel_ref[t : t + 1, :], weight_ref[t : t + 1, :], 0.0)
    total = jnp.dot(
        select.astype(jnp.bfloat16),
        spec_ref[:, first : first + width],
        preferred_element_type=jnp.float32,
    )
    for n, out_ref in enumerate(outs):
        out_ref[...] = total[n * rows : (n + 1) * rows].astype(out_ref.dtype)


def sums(bases, at, piece, dtypes, weight, panel, spectrum, rows):
    particles = spectrum.shape[0]
    width = widths()[piece]
    return pl.pallas_call(
        functools.partial(sums_kernel, at, piece * CUT * LANES),
        in_specs=[pl.BlockSpec(memory_space=pltpu.SMEM)] + [pl.BlockSpec(memory_space=pltpu.VMEM)] * 3,
        out_shape=[jax.ShapeDtypeStruct((rows, width), d) for d in dtypes],
        cost_estimate=pl.CostEstimate(
            flops=2 * len(dtypes) * rows * particles * width * 2,
            bytes_accessed=2 * width * (particles + rows * len(dtypes)),
            transcendentals=0,
        ),
        compiler_params=params(),
        name="sums",
    )(bases, weight, panel, spectrum)


LINE = 4
GATHER_ORDER = ((0, 1, 2, 3), (1, 0, 1, 2), (2, 2, 3, 1), (3, 3, 0, 0))
SCATTER_ORDER = ((3, 0, 3, 0), (2, 3, 0, 1), (1, 2, 1, 2), (0, 1, 2, 3))


def block_places():
    table = np.zeros((2 * LINE, 16), np.int32)
    for place in range(2 * LINE):
        z, x = divmod(place, 2)
        gather = [order[z] for order in GATHER_ORDER]
        scatter = [order[z] for order in SCATTER_ORDER]
        table[place] = (
            [2 * g + x for g in gather]
            + [2 * g + 1 - x for g in gather]
            + [2 * g + x for g in scatter]
            + [2 * g + 1 - x for g in scatter]
        )
    return table


def along_z(hops):
    return [(2 * a + x, 2 * b + x) for a, b in hops for x in range(2)]


def move(value, hops):
    return lax.ppermute(value, "dp", along_z(hops))


def swap_x(value):
    return lax.ppermute(value, "dp", [(d, d ^ 1) for d in range(2 * LINE)])


def sum_of(terms):
    return functools.reduce(lambda a, b: a + b, terms)


def tie(*values):
    return lax.optimization_barrier(values)


def by_line(images, references, panel, prior, precision):
    rows = references.shape[0]
    cls_count = lax.axis_size("cls")
    mine = lax.axis_index("cls")
    place = lax.axis_index("dp")
    z = lax.shift_right_logical(place, 1)
    x_rows, y_rows = half_tables(images.shape[1])
    mirror = mirror_matrix()
    bases = (jnp.asarray(block_places())[place] * cls_count + mine) * rows
    here, there, keep, give = (range(4 * n, 4 * n + 4) for n in range(4))

    pieces = range(2)
    blocks = [[] for _ in pieces]
    own = fold(references, mirror)
    steps = []
    for p in pieces:
        u1 = move(own[p], ((0, 1), (1, 2), (2, 3)))
        d1 = move(own[p], ((1, 0), (2, 1), (3, 2)))
        steps.append((u1, d1, swap_x(own[p])))
    spectrum = dft(images, x_rows, y_rows, 64, 0, 2)
    (u1, d1, x1), (v1, w1, y1) = steps
    u1, d1, x1, spectrum = tie(u1, d1, x1, spectrum)
    v1, w1, y1 = tie(v1, w1, y1)
    steps = [(u1, d1, x1), (v1, w1, y1)]

    later = []
    for p in pieces:
        u1, d1, x1 = steps[p]
        u2 = move(u1, ((1, 2), (2, 3)))
        d2 = move(d1, ((1, 0), (2, 1)))
        s1 = jnp.where(z == 0, d1, u1)
        later.append([u2, d2, swap_x(s1)])
        blocks[p] += [own[p], x1, s1]
    spectrum = dft(images, x_rows, y_rows, 64, 1, 2, spectrum)
    *later[0], spectrum = tie(*later[0], spectrum)
    later[1] = tie(*later[1])

    last = []
    for p in pieces:
        u1, d1, x1 = steps[p]
        u2, d2, x2 = later[p]
        inner = jnp.where(z == 1, d2, u2)
        e3 = move(inner, ((2, 3), (1, 0)))
        s2 = jnp.where(z == 0, d2, jnp.where(z == 3, u2, d1))
        last.append([inner, e3, swap_x(s2)])
        blocks[p] += [x2, s2]
    order = (here[0], there[0], here[1], there[1], here[2])
    picked = jnp.zeros(panel.shape, jnp.float32)
    picked = score(bases, order, 0, spectrum, panel, picked, blocks[0])
    _, last[0][1], last[0][2], picked = tie(last[0][0], last[0][1], last[0][2], picked)
    picked = score(bases, order, 1, spectrum, panel, picked, blocks[1])
    last[1][1:] = tie(*last[1][1:])

    ends = []
    for p in pieces:
        inner, e3, x3 = last[p]
        s3 = jnp.where((z == 1) | (z == 2), inner, e3)
        ends.append(swap_x(s3))
        picked = score(bases, (there[2], here[3]), p, spectrum, panel, picked, [x3, s3])
    for p in pieces:
        picked = score(bases, (there[3],), p, spectrum, panel, picked, [ends[p]])

    scores = lax.all_gather(picked, "cls", axis=0, tiled=False)
    weight = weights_of(scores, prior, precision)

    narrow, wide = jnp.bfloat16, jnp.float32
    add = lambda *terms: sum_of([t.astype(wide) for t in terms]).astype(narrow)
    part = functools.partial(sums, bases, weight=weight, panel=panel, spectrum=spectrum, rows=rows)

    first = []
    for p in pieces:
        (g1,) = part((give[0],), p, [narrow])
        first.append(swap_x(g1))
    second = []
    for p in pieces:
        k1, g2 = part((keep[0], give[1]), p, [wide, narrow])
        r1, g2 = tie(first[p], g2)
        q1 = add(k1, r1)
        e2 = move(q1, ((0, 1), (3, 2)))
        second.append((q1, e2, swap_x(g2)))
    third = []
    for p in pieces:
        q1, e2, r2 = second[p]
        k2, g3 = part((keep[1], give[2]), p, [wide, narrow])
        e2, r2, g3 = tie(e2, r2, g3)
        q2 = add(k2, r2, e2)
        u3 = move(q2, ((0, 1), (1, 2)))
        d3 = move(q2, ((2, 1), (3, 2)))
        third.append((q1, u3, d3, swap_x(g3)))
    halves = []
    for p in pieces:
        q1, u3, d3, r3 = third[p]
        k3, g4 = part((keep[2], give[3]), p, [wide, narrow])
        u3, d3, r3, g4 = tie(u3, d3, r3, g4)
        q3 = add(k3, r3)
        up = add(jnp.where(z == 2, q1, q3), u3)
        down = add(jnp.where(z == 1, q1, q3), d3)
        u4 = move(up, ((0, 1), (1, 2), (2, 3)))
        d4 = move(down, ((1, 0), (2, 1), (3, 2)))
        r4 = swap_x(g4)
        (k4,) = part((keep[3],), p, [wide])
        halves.append([k4, r4, u4, d4])
    return unfold(halves[0], halves[1], mirror)


def by_collectives(images, references, panel, prior, precision):
    rows = references.shape[0]
    dp_count = lax.axis_size("dp")
    cls_count = lax.axis_size("cls")
    mine = lax.axis_index("cls")
    x_rows, y_rows = half_tables(images.shape[1])
    mirror = mirror_matrix()
    spectrum = dft(images, x_rows, y_rows, 64)
    bases = (jnp.arange(dp_count, dtype=jnp.int32) * cls_count + mine) * rows
    picked = jnp.zeros(panel.shape, jnp.float32)
    for p, own in enumerate(fold(references, mirror)):
        gathered = lax.all_gather(own, "dp", axis=0, tiled=False)
        for n in range(dp_count):
            picked = score(bases, (n,), p, spectrum, panel, picked, [gathered[n]])
    scores = lax.all_gather(picked, "cls", axis=0, tiled=False)
    weight = weights_of(scores, prior, precision)
    halves = []
    for p in range(2):
        partial = [
            sums(bases, (n,), p, [jnp.bfloat16], weight, panel, spectrum, rows)[0] for n in range(dp_count)
        ]
        halves.append([lax.psum_scatter(jnp.stack(partial), "dp", scatter_dimension=0, tiled=False)])
    return unfold(halves[0], halves[1], mirror)


def on_device(images, references, best_class, best_rot, prior, precision):
    panel = (best_class * ROTS + best_rot).T
    plan = by_line if lax.axis_size("dp") == 2 * LINE else by_collectives
    return plan(images, references, panel, prior.T, precision[None, :])


def solution(mesh):
    in_specs = (
        P("dp", None, None),
        P(("dp", "cls"), None),
        P("dp", None),
        P("dp", None),
        P("dp", None),
        P("dp"),
    )
    out_specs = P(("dp", "cls"), None)
    return jax.shard_map(on_device, mesh=mesh, in_specs=in_specs, out_specs=out_specs, check_vma=False)
```

time: 418 us -> 169 us (0.40)
  waiting for transfers between devices: 263 us -> 35.4 us
  matrix products: 91.8 us -> 0 us
  starting transfers between devices: 0.04 us -> 72.1 us
  Pallas kernels: 0 us -> 34.3 us
  local copies, waits for them, and re-layouts: 32.7 us -> 15.4 us
  between operations: 13.5 us -> 0.55 us
  blocking collectives: 12.4 us -> 5.19 us
    reduce_scatter x1 -> x0, waiting for transfers between devices: 161 us -> none  [on_device(): lax.psum_scatter(partial_sums.astype(jnp.bfloat16), 'dp', scatter_dimensi...]
    all_gather x1 -> x0, waiting for transfers between devices: 101 us -> none  [on_device(): lax.all_gather(references, 'dp', axis=0, tiled=True)]
    dot_general x7 -> x0, matrix products: 91.8 us -> none  [the longest x4 56 us: on_device(): jnp.dot(selector, spectrum, preferred_element_type=jnp.float32)]
    ppermute x0 -> x36, starting transfers between devices: none -> 72.1 us  [the longest x20 55.1 us: move(): return lax.ppermute(value, 'dp', along_z(hops))]
    ppermute x0 -> x36, waiting for transfers between devices: none -> 35.4 us  [the longest x16 25.8 us: swap_x(): return lax.ppermute(value, 'dp', [(d, d ^ 1) for d in range(2 * LINE)])]
    pallas_call x0 -> x21, Pallas kernels: none -> 34.3 us  [the longest x2 11.7 us: dft(): pl.pallas_call(dft_kernel, grid=(steps,), in_specs=in_specs, out_specs=pl...]
    gather x5 -> x0, local copies, waits for them, and re-layouts: 17.5 us -> none  [on_device(): jnp.take_along_axis(raw_scores, local_ids, axis=1) * precision[:, None]]
    psum x1 -> x0, blocking collectives: 6.29 us -> none  [on_device(): denominator = lax.psum(partial_value, 'cls')]
  transfers between devices with their start and end apart: 2 -> 36, of which waited for: 2 -> 9; matrix products, arithmetic and copies ran while one was open for 10% -> 3% of each run, Pallas kernels for 0% -> 17%
where the time goes in v1:
time: 169 us; the launch traced here: 168 us
  starting transfers between devices  72.1 us (43%)
  waiting for transfers between devices  35.4 us (21%)
  Pallas kernels  34.3 us (20%)
  local copies, waits for them, and re-layouts  15.4 us (9%)
  other arithmetic  5.21 us (3%)
  blocking collectives  5.19 us (3%)
    ppermute x20, starting transfers between devices, move(): return lax.ppermute(value, 'dp', along_z(hops))  55.1 us
    ppermute x16, waiting for transfers between devices, swap_x(): return lax.ppermute(value, 'dp', [(d, d ^ 1) for d in range(2 * LINE)])  25.8 us
    ppermute x16, starting transfers between devices, swap_x(): return lax.ppermute(value, 'dp', [(d, d ^ 1) for d in range(2 * LINE)])  17 us
    unnamed x32, local copies, waits for them, and re-layouts  15.4 us
    pallas_call x2, Pallas kernels, dft(): pl.pallas_call(dft_kernel, grid=(steps,), in_specs=in_specs, out_specs=pl...  11.7 us
    pallas_call x10, Pallas kernels, sums(): pl.pallas_call(functools.partial(sums_kernel, at, piece * CUT * LANES), i...  10.5 us
    ppermute x20, waiting for transfers between devices, move(): return lax.ppermute(value, 'dp', along_z(hops))  9.56 us
    pallas_call x6, Pallas kernels, score(): pl.pallas_call(functools.partial(score_kernel, at, piece * CUT * LANES),...  9.23 us
  transfers between devices with their start and end apart: 36, of which 9 were waited for; matrix products, arithmetic and copies ran while one was open for 3% of the time, Pallas kernels for 17%

profile of v1, /device:TPU:0, one launch (start us, length us, event | category | flops | bytes accessed | tf_op | source)
XLA Modules:
  0.0 168.1 jit_solution(6660930261916113000)
XLA Ops:
  2.6 4.9 %collective-permute-start.8 = (bf16[72,2048]{1,0:T(8,128)(2,1)S(1)}, bf16[72,2048]{1,0:T(8,128)(2,1)S(1)}, u32[]{:S(2)}, u32[]{:S(2)}) collective-permute-start(bf16[72,2048]{1,0:T(8,128)(2,1)S(1)} %get-tuple-element.66.rest_0_), channel_id=1, source_target_pairs={{0,8},{4,12},{8,16},{12,20},{16,24},{20,28},{1,9},{5,13},{9,17},{1... | collective-permute-start | bytes 884744 | tf_op jit(solution)/shard_map/ppermute | solution.py:335
  10.4 5.3 %collective-permute-start = (bf16[72,2176]{1,0:T(8,128)(2,1)S(1)}, bf16[72,2176]{1,0:T(8,128)(2,1)}, u32[]{:S(2)}, u32[]{:S(2)}) collective-permute-start(bf16[72,2176]{1,0:T(8,128)(2,1)S(1)} %get-tuple-element.56.rest_0_), channel_id=1, source_target_pairs={{0,8},{4,12},{8,16},{12,20},{16,24},{20,28},{1,9},{5,13},{9,17},{1... | collective-permute-start | bytes 940040 | tf_op jit(solution)/shard_map/ppermute | solution.py:335
  17.0 5.8 %copy-done.2 = bf16[512,128,128]{2,1,0:T(8,128)(2,1)S(1)} copy-done((bf16[512,128,128]{2,1,0:T(8,128)(2,1)S(1)}, bf16[512,128,128]{2,1,0:T(8,128)(2,1)}, u32[]{:S(2)}) %copy-start.2) | copy-done | bytes 16777240
  24.4 5.8 %dft.2.rest_0_ = bf16[512,4224]{1,0:T(8,128)(2,1)S(1)} custom-call(bf16[512,128,128]{2,1,0:T(8,128)(2,1)S(1)} %copy-done.2, bf16[72,128]{1,0:T(8,128)(2,1)S(1)} %copy-done.7, bf16[256,256]{1,0:T(8,128)(2,1)S(1)} %copy-done.4), custom_call_target="tpu_custom_call" | custom-call | flops 1711276032 | bytes 10551296 | tf_op jit(solution)/shard_map/dft/pallas_call | solution.py:197
  34.4 6.2 %collective-permute-done.2.rest_1_ = bf16[72,2176]{1,0:T(8,128)(2,1)S(1)} collective-permute-done((bf16[72,2176]{1,0:T(8,128)(2,1)S(1)}, bf16[72,2176]{1,0:T(8,128)(2,1)S(1)}, u32[]{:S(2)}, u32[]{:S(2)}) %collective-permute-start.2) | collective-permute-done | bytes 313376 | tf_op jit(solution)/shard_map/ppermute | solution.py:339
  42.6 5.9 %dft.3.spec_ref = bf16[512,4224]{1,0:T(8,128)(2,1)S(1)} custom-call(bf16[512,128,128]{2,1,0:T(8,128)(2,1)S(1)} %copy-done.2, bf16[72,128]{1,0:T(8,128)(2,1)S(1)} %copy-done.7, bf16[256,256]{1,0:T(8,128)(2,1)S(1)} %copy-done.4, bf16[512,4224]{1,0:T(8,128)(2,1)S(1)} %dft.2.rest_0_), custom_call_target="tpu_custom_call", output_to_operand_aliasing={{}: (3, {})} | custom-call | flops 1711276032 | bytes 10551296 | tf_op jit(solution)/shard_map/dft/pallas_call | solution.py:197
  48.5 2.0 %copy-done = bf16[512,4224]{1,0:T(8,128)(2,1)} copy-done((bf16[512,4224]{1,0:T(8,128)(2,1)}, bf16[512,4224]{1,0:T(8,128)(2,1)S(1)}, u32[]{:S(2)}) %copy-start) | copy-done | bytes 4325400
  54.7 4.9 %collective-permute-done.5.rest_3_ = bf16[72,2176]{1,0:T(8,128)(2,1)S(1)} collective-permute-done((bf16[72,2176]{1,0:T(8,128)(2,1)S(1)}, bf16[72,2176]{1,0:T(8,128)(2,1)S(1)}, u32[]{:S(2)}, u32[]{:S(2)}) %collective-permute-start.5) | collective-permute-done | bytes 313376 | tf_op jit(solution)/shard_map/ppermute | solution.py:339
  63.8 2.2 %copy-done.1 = bf16[512,4224]{1,0:T(8,128)(2,1)S(1)} copy-done((bf16[512,4224]{1,0:T(8,128)(2,1)S(1)}, bf16[512,4224]{1,0:T(8,128)(2,1)}, u32[]{:S(2)}) %copy-start.1) | copy-done | bytes 4325400
  67.0 1.8 %score.6.before_ref = f32[4,512]{1,0:T(4,128)S(1)} custom-call(s32[16]{0:T(128)S(1)} %multiply_bitcast_fusion.base_ref, bf16[512,4224]{1,0:T(8,128)(2,1)S(1)} %copy-done.1, s32[4,512]{1,0:T(4,128)S(1)} %add_bitcast_fusion.panel_ref, f32[4,512]{1,0:T(4,128)S(1)} %broadcast_in_dim.6.before_ref, bf16[72,2176]{1,0:T(8,128)(2,1)S(1)} %get-tuple-element.56.rest_0_, ...), custom_call_target="tpu_custom_call" | custom-call | flops 1604321280 | bytes 3794944 | tf_op jit(solution)/shard_map/score/pallas_call | solution.py:246
  68.9 3.7 %collective-permute-done.6 = bf16[72,2176]{1,0:T(8,128)(2,1)} collective-permute-done((bf16[72,2176]{1,0:T(8,128)(2,1)}, bf16[72,2176]{1,0:T(8,128)(2,1)}, u32[]{:S(2)}, u32[]{:S(2)}) %collective-permute-start.6) | collective-permute-done | bytes 313376 | tf_op jit(solution)/shard_map/ppermute | solution.py:335
  76.7 1.7 %score.7.before_ref = f32[4,512]{1,0:T(4,128)S(1)} custom-call(s32[16]{0:T(128)S(1)} %multiply_bitcast_fusion.base_ref, bf16[512,4224]{1,0:T(8,128)(2,1)S(1)} %copy-done.1, s32[4,512]{1,0:T(4,128)S(1)} %add_bitcast_fusion.panel_ref, f32[4,512]{1,0:T(4,128)S(1)} %score.6.before_ref, bf16[72,2048]{1,0:T(8,128)(2,1)S(1)} %get-tuple-element.66.rest_0_, ...), custom_call_target="tpu_custom_call" | custom-call | flops 1509949440 | bytes 3571712 | tf_op jit(solution)/shard_map/score/pallas_call | solution.py:246
  85.1 5.2 %all-gather.1.scores_ref = f32[4,4,512]{2,1,0:T(4,128)S(1)} all-gather(f32[1,4,512]{2,1,0:T(4,128)S(1)} %bitcast.9), channel_id=2, replica_groups=mesh['dp'=8,'cls'=4] {'cls'}, dimensions={0}, use_global_device_ids=true | all-gather | bytes 40960 | tf_op jit(solution)/shard_map/all_gather | solution.py:412
  98.8 2.4 %collective-permute-done.27 = bf16[72,2048]{1,0:T(8,128)(2,1)S(1)} collective-permute-done((bf16[72,2048]{1,0:T(8,128)(2,1)S(1)}, bf16[72,2048]{1,0:T(8,128)(2,1)S(1)}, u32[]{:S(2)}, u32[]{:S(2)}) %collective-permute-start.27) | collective-permute-done | bytes 294944 | tf_op jit(solution)/shard_map/ppermute | solution.py:339
  101.3 6.3 %collective-permute-start.28 = (bf16[72,2048]{1,0:T(8,128)(2,1)S(1)}, bf16[72,2048]{1,0:T(8,128)(2,1)S(1)}, u32[]{:S(2)}, u32[]{:S(2)}) collective-permute-start(bf16[72,2048]{1,0:T(8,128)(2,1)S(1)} %add_convert_fusion.9), channel_id=1, source_target_pairs={{0,8},{4,12},{24,16},{28,20},{1,9},{5,13},{25,17},{29,21},{2,10},{... | collective-permute-start | bytes 884744 | tf_op jit(solution)/shard_map/ppermute | solution.py:335
  108.7 5.6 %collective-permute-start.19 = (bf16[72,2176]{1,0:T(8,128)(2,1)S(1)}, bf16[72,2176]{1,0:T(8,128)(2,1)S(1)}, u32[]{:S(2)}, u32[]{:S(2)}) collective-permute-start(bf16[72,2176]{1,0:T(8,128)(2,1)S(1)} %add_convert_fusion.4), channel_id=1, source_target_pairs={{0,8},{4,12},{24,16},{28,20},{1,9},{5,13},{25,17},{29,21},{2,10},{... | collective-permute-start | bytes 940040 | tf_op jit(solution)/shard_map/ppermute | solution.py:335
  115.4 5.4 %collective-permute-start.30 = (bf16[72,2048]{1,0:T(8,128)(2,1)S(1)}, bf16[72,2048]{1,0:T(8,128)(2,1)S(1)}, u32[]{:S(2)}, u32[]{:S(2)}) collective-permute-start(bf16[72,2048]{1,0:T(8,128)(2,1)S(1)} %add_convert_fusion.8), channel_id=1, source_target_pairs={{0,8},{4,12},{8,16},{12,20},{1,9},{5,13},{9,17},{13,21},{2,10},{6,... | collective-permute-start | bytes 884744 | tf_op jit(solution)/shard_map/ppermute | solution.py:335
  122.4 4.3 %collective-permute-start.21 = (bf16[72,2176]{1,0:T(8,128)(2,1)S(1)}, bf16[72,2176]{1,0:T(8,128)(2,1)S(1)}, u32[]{:S(2)}, u32[]{:S(2)}) collective-permute-start(bf16[72,2176]{1,0:T(8,128)(2,1)S(1)} %add_convert_fusion.3), channel_id=1, source_target_pairs={{0,8},{4,12},{8,16},{12,20},{1,9},{5,13},{9,17},{13,21},{2,10},{6,... | collective-permute-start | bytes 940040 | tf_op jit(solution)/shard_map/ppermute | solution.py:335
  132.5 9.9 %collective-permute-done.32 = bf16[72,2048]{1,0:T(8,128)(2,1)S(1)} collective-permute-done((bf16[72,2048]{1,0:T(8,128)(2,1)S(1)}, bf16[72,2048]{1,0:T(8,128)(2,1)S(1)}, u32[]{:S(2)}, u32[]{:S(2)}) %collective-permute-start.32) | collective-permute-done | bytes 294944 | tf_op jit(solution)/shard_map/ppermute | solution.py:339
  144.7 5.7 %collective-permute-start.25 = (bf16[72,2176]{1,0:T(8,128)(2,1)S(1)}, bf16[72,2176]{1,0:T(8,128)(2,1)S(1)}, u32[]{:S(2)}, u32[]{:S(2)}) collective-permute-start(bf16[72,2176]{1,0:T(8,128)(2,1)S(1)} %get-tuple-element.108), channel_id=1, source_target_pairs={{0,8},{4,12},{8,16},{12,20},{16,24},{20,28},{1,9},{5,13},{9,17},{1... | collective-permute-start | bytes 940040 | tf_op jit(solution)/shard_map/ppermute | solution.py:335
  152.0 4.6 %collective-permute-start.34 = (bf16[72,2048]{1,0:T(8,128)(2,1)S(1)}, bf16[72,2048]{1,0:T(8,128)(2,1)S(1)}, u32[]{:S(2)}, u32[]{:S(2)}) collective-permute-start(bf16[72,2048]{1,0:T(8,128)(2,1)S(1)} %get-tuple-element.110), channel_id=1, source_target_pairs={{0,8},{4,12},{8,16},{12,20},{16,24},{20,28},{1,9},{5,13},{9,17},{1... | collective-permute-start | bytes 884744 | tf_op jit(solution)/shard_map/ppermute | solution.py:335
  160.0 1.7 %collective-permute-done.34.rest_6_ = bf16[72,2048]{1,0:T(8,128)(2,1)S(1)} collective-permute-done((bf16[72,2048]{1,0:T(8,128)(2,1)S(1)}, bf16[72,2048]{1,0:T(8,128)(2,1)S(1)}, u32[]{:S(2)}, u32[]{:S(2)}) %collective-permute-start.34) | collective-permute-done | bytes 294944 | tf_op jit(solution)/shard_map/ppermute | solution.py:335
  161.7 4.1 %collective-permute-done.35.rest_7_ = bf16[72,2048]{1,0:T(8,128)(2,1)S(1)} collective-permute-done((bf16[72,2048]{1,0:T(8,128)(2,1)S(1)}, bf16[72,2048]{1,0:T(8,128)(2,1)S(1)}, u32[]{:S(2)}, u32[]{:S(2)}) %collective-permute-start.35) | collective-permute-done | bytes 294944 | tf_op jit(solution)/shard_map/ppermute | solution.py:335
  165.8 2.3 %unfold.1 = f32[72,8192]{1,0:T(8,128)} custom-call(bf16[128,128]{1,0:T(8,128)(2,1)S(1)} %copy-done.6, f32[72,2176]{1,0:T(8,128)S(1)} %sums.10.rest_0_, bf16[72,2176]{1,0:T(8,128)(2,1)S(1)} %collective-permute-done.24.rest_1_, bf16[72,2176]{1,0:T(8,128)(2,1)S(1)} %collective-permute-done.25.rest_2_, bf16[72,2176]{1,0:T(8,128)(2,1)S(1)} %collective-permute-done.26.rest_3_, ...), custom_call_target="tpu_custom_call" | custom-call | tf_op jit(solution)/shard_map/unfold/pallas_call | solution.py:136
  (118 shorter events, 59.7 us)
Async XLA Ops:
  2.6 27.6 %collective-permute-start.8 = (bf16[72,2048]{1,0:T(8,128)(2,1)S(1)}, bf16[72,2048]{1,0:T(8,128)(2,1)S(1)}, u32[]{:S(2)}, u32[]{:S(2)}) collective-permute-start(bf16[72,2048]{1,0:T(8,128)(2,1)S(1)} %get-tuple-element.66.rest_0_), channel_id=1, source_target_pairs={{0,8},{4,12},{8,16},{12,20},{16,24},{20,28},{1,9},{5,13},{9,17},{1... | collective-permute-start | bytes 884744 | tf_op jit(solution)/shard_map/ppermute | solution.py:335
  7.5 23.3 %collective-permute-start.9 = (bf16[72,2048]{1,0:T(8,128)(2,1)S(1)}, bf16[72,2048]{1,0:T(8,128)(2,1)S(1)}, u32[]{:S(2)}, u32[]{:S(2)}) collective-permute-start(bf16[72,2048]{1,0:T(8,128)(2,1)S(1)} %get-tuple-element.66.rest_0_), channel_id=1, source_target_pairs={{8,0},{12,4},{16,8},{20,12},{24,16},{28,20},{9,1},{13,5},{17,9},{2... | collective-permute-start | bytes 884744 | tf_op jit(solution)/shard_map/ppermute | solution.py:335
  8.8 22.0 %collective-permute-start.10 = (bf16[72,2048]{1,0:T(8,128)(2,1)S(1)}, bf16[72,2048]{1,0:T(8,128)(2,1)S(1)}, u32[]{:S(2)}, u32[]{:S(2)}) collective-permute-start(bf16[72,2048]{1,0:T(8,128)(2,1)S(1)} %get-tuple-element.66.rest_0_), channel_id=1, source_target_pairs={{0,4},{4,0},{8,12},{12,8},{16,20},{20,16},{24,28},{28,24},{1,5},{5... | collective-permute-start | bytes 884744 | tf_op jit(solution)/shard_map/ppermute | solution.py:339
  10.4 22.4 %collective-permute-start = (bf16[72,2176]{1,0:T(8,128)(2,1)S(1)}, bf16[72,2176]{1,0:T(8,128)(2,1)}, u32[]{:S(2)}, u32[]{:S(2)}) collective-permute-start(bf16[72,2176]{1,0:T(8,128)(2,1)S(1)} %get-tuple-element.56.rest_0_), channel_id=1, source_target_pairs={{0,8},{4,12},{8,16},{12,20},{16,24},{20,28},{1,9},{5,13},{9,17},{1... | collective-permute-start | bytes 940040 | tf_op jit(solution)/shard_map/ppermute | solution.py:335
  15.7 18.7 %collective-permute-start.1 = (bf16[72,2176]{1,0:T(8,128)(2,1)S(1)}, bf16[72,2176]{1,0:T(8,128)(2,1)S(1)}, u32[]{:S(2)}, u32[]{:S(2)}) collective-permute-start(bf16[72,2176]{1,0:T(8,128)(2,1)S(1)} %get-tuple-element.56.rest_0_), channel_id=1, source_target_pairs={{8,0},{12,4},{16,8},{20,12},{24,16},{28,20},{9,1},{13,5},{17,9},{2... | collective-permute-start | bytes 940040 | tf_op jit(solution)/shard_map/ppermute | solution.py:335
  30.8 19.7 %collective-permute-start.11 = (bf16[72,2048]{1,0:T(8,128)(2,1)S(1)}, bf16[72,2048]{1,0:T(8,128)(2,1)S(1)}, u32[]{:S(2)}, u32[]{:S(2)}) collective-permute-start(bf16[72,2048]{1,0:T(8,128)(2,1)S(1)} %collective-permute-done.8), channel_id=1, source_target_pairs={{8,16},{12,20},{16,24},{20,28},{9,17},{13,21},{17,25},{21,29},{10,... | collective-permute-start | bytes 884744 | tf_op jit(solution)/shard_map/ppermute | solution.py:335
  31.5 19.6 %collective-permute-start.12 = (bf16[72,2048]{1,0:T(8,128)(2,1)S(1)}, bf16[72,2048]{1,0:T(8,128)(2,1)S(1)}, u32[]{:S(2)}, u32[]{:S(2)}) collective-permute-start(bf16[72,2048]{1,0:T(8,128)(2,1)S(1)} %collective-permute-done.9), channel_id=1, source_target_pairs={{8,0},{12,4},{16,8},{20,12},{9,1},{13,5},{17,9},{21,13},{10,2},{14... | collective-permute-start | bytes 884744 | tf_op jit(solution)/shard_map/ppermute | solution.py:335
  32.8 18.3 %collective-permute-start.13 = (bf16[72,2048]{1,0:T(8,128)(2,1)S(1)}, bf16[72,2048]{1,0:T(8,128)(2,1)S(1)}, u32[]{:S(2)}, u32[]{:S(2)}) collective-permute-start(bf16[72,2048]{1,0:T(8,128)(2,1)S(1)} %broadcast_select_fusion.5.rest_2_), channel_id=1, source_target_pairs={{0,4},{4,0},{8,12},{12,8},{16,20},{20,16},{24,28},{28,24},{1,5},{5... | collective-permute-start | bytes 884744 | tf_op jit(solution)/shard_map/ppermute | solution.py:339
  40.6 14.1 %collective-permute-start.3 = (bf16[72,2176]{1,0:T(8,128)(2,1)}, bf16[72,2176]{1,0:T(8,128)(2,1)S(1)}, u32[]{:S(2)}, u32[]{:S(2)}) collective-permute-start(bf16[72,2176]{1,0:T(8,128)(2,1)} %collective-permute-done), channel_id=1, source_target_pairs={{8,16},{12,20},{16,24},{20,28},{9,17},{13,21},{17,25},{21,29},{10,... | collective-permute-start | bytes 940040 | tf_op jit(solution)/shard_map/ppermute | solution.py:335
  41.3 13.5 %collective-permute-start.4 = (bf16[72,2176]{1,0:T(8,128)(2,1)S(1)}, bf16[72,2176]{1,0:T(8,128)(2,1)S(1)}, u32[]{:S(2)}, u32[]{:S(2)}) collective-permute-start(bf16[72,2176]{1,0:T(8,128)(2,1)S(1)} %collective-permute-done.1), channel_id=1, source_target_pairs={{8,0},{12,4},{16,8},{20,12},{9,1},{13,5},{17,9},{21,13},{10,2},{14... | collective-permute-start | bytes 940040 | tf_op jit(solution)/shard_map/ppermute | solution.py:335
  51.9 17.0 %collective-permute-start.14 = (bf16[72,2048]{1,0:T(8,128)(2,1)}, bf16[72,2048]{1,0:T(8,128)(2,1)}, u32[]{:S(2)}, u32[]{:S(2)}) collective-permute-start(bf16[72,2048]{1,0:T(8,128)(2,1)} %get-tuple-element.113), channel_id=1, source_target_pairs={{16,24},{20,28},{8,0},{12,4},{17,25},{21,29},{9,1},{13,5},{18,26},... | collective-permute-start | bytes 884744 | tf_op jit(solution)/shard_map/ppermute | solution.py:335
  53.2 15.7 %collective-permute-start.15 = (bf16[72,2048]{1,0:T(8,128)(2,1)S(1)}, bf16[72,2048]{1,0:T(8,128)(2,1)S(1)}, u32[]{:S(2)}, u32[]{:S(2)}) collective-permute-start(bf16[72,2048]{1,0:T(8,128)(2,1)S(1)} %get-tuple-element.114.rest_4_), channel_id=1, source_target_pairs={{0,4},{4,0},{8,12},{12,8},{16,20},{20,16},{24,28},{28,24},{1,5},{5... | collective-permute-start | bytes 884744 | tf_op jit(solution)/shard_map/ppermute | solution.py:339
  93.4 15.2 %collective-permute-start.18 = (bf16[72,2176]{1,0:T(8,128)(2,1)S(1)}, bf16[72,2176]{1,0:T(8,128)(2,1)S(1)}, u32[]{:S(2)}, u32[]{:S(2)}) collective-permute-start(bf16[72,2176]{1,0:T(8,128)(2,1)S(1)} %sums.13), channel_id=1, source_target_pairs={{0,4},{4,0},{8,12},{12,8},{16,20},{20,16},{24,28},{28,24},{1,5},{5... | collective-permute-start | bytes 940040 | tf_op jit(solution)/shard_map/ppermute | solution.py:339
  101.3 14.0 %collective-permute-start.28 = (bf16[72,2048]{1,0:T(8,128)(2,1)S(1)}, bf16[72,2048]{1,0:T(8,128)(2,1)S(1)}, u32[]{:S(2)}, u32[]{:S(2)}) collective-permute-start(bf16[72,2048]{1,0:T(8,128)(2,1)S(1)} %add_convert_fusion.9), channel_id=1, source_target_pairs={{0,8},{4,12},{24,16},{28,20},{1,9},{5,13},{25,17},{29,21},{2,10},{... | collective-permute-start | bytes 884744 | tf_op jit(solution)/shard_map/ppermute | solution.py:335
  108.7 12.2 %collective-permute-start.19 = (bf16[72,2176]{1,0:T(8,128)(2,1)S(1)}, bf16[72,2176]{1,0:T(8,128)(2,1)S(1)}, u32[]{:S(2)}, u32[]{:S(2)}) collective-permute-start(bf16[72,2176]{1,0:T(8,128)(2,1)S(1)} %add_convert_fusion.4), channel_id=1, source_target_pairs={{0,8},{4,12},{24,16},{28,20},{1,9},{5,13},{25,17},{29,21},{2,10},{... | collective-permute-start | bytes 940040 | tf_op jit(solution)/shard_map/ppermute | solution.py:335
  115.4 13.7 %collective-permute-start.30 = (bf16[72,2048]{1,0:T(8,128)(2,1)S(1)}, bf16[72,2048]{1,0:T(8,128)(2,1)S(1)}, u32[]{:S(2)}, u32[]{:S(2)}) collective-permute-start(bf16[72,2048]{1,0:T(8,128)(2,1)S(1)} %add_convert_fusion.8), channel_id=1, source_target_pairs={{0,8},{4,12},{8,16},{12,20},{1,9},{5,13},{9,17},{13,21},{2,10},{6,... | collective-permute-start | bytes 884744 | tf_op jit(solution)/shard_map/ppermute | solution.py:335
  122.4 20.9 %collective-permute-start.21 = (bf16[72,2176]{1,0:T(8,128)(2,1)S(1)}, bf16[72,2176]{1,0:T(8,128)(2,1)S(1)}, u32[]{:S(2)}, u32[]{:S(2)}) collective-permute-start(bf16[72,2176]{1,0:T(8,128)(2,1)S(1)} %add_convert_fusion.3), channel_id=1, source_target_pairs={{0,8},{4,12},{8,16},{12,20},{1,9},{5,13},{9,17},{13,21},{2,10},{6,... | collective-permute-start | bytes 940040 | tf_op jit(solution)/shard_map/ppermute | solution.py:335
  126.8 16.6 %collective-permute-start.22 = (bf16[72,2176]{1,0:T(8,128)(2,1)S(1)}, bf16[72,2176]{1,0:T(8,128)(2,1)S(1)}, u32[]{:S(2)}, u32[]{:S(2)}) collective-permute-start(bf16[72,2176]{1,0:T(8,128)(2,1)S(1)} %add_convert_fusion.3), channel_id=1, source_target_pairs={{16,8},{20,12},{24,16},{28,20},{17,9},{21,13},{25,17},{29,21},{18,... | collective-permute-start | bytes 940040 | tf_op jit(solution)/shard_map/ppermute | solution.py:335
  127.5 15.9 %collective-permute-start.23 = (bf16[72,2176]{1,0:T(8,128)(2,1)S(1)}, bf16[72,2176]{1,0:T(8,128)(2,1)S(1)}, u32[]{:S(2)}, u32[]{:S(2)}) collective-permute-start(bf16[72,2176]{1,0:T(8,128)(2,1)S(1)} %get-tuple-element.85), channel_id=1, source_target_pairs={{0,4},{4,0},{8,12},{12,8},{16,20},{20,16},{24,28},{28,24},{1,5},{5... | collective-permute-start | bytes 940040 | tf_op jit(solution)/shard_map/ppermute | solution.py:339
  129.2 13.2 %collective-permute-start.32 = (bf16[72,2048]{1,0:T(8,128)(2,1)S(1)}, bf16[72,2048]{1,0:T(8,128)(2,1)S(1)}, u32[]{:S(2)}, u32[]{:S(2)}) collective-permute-start(bf16[72,2048]{1,0:T(8,128)(2,1)S(1)} %get-tuple-element.100), channel_id=1, source_target_pairs={{0,4},{4,0},{8,12},{12,8},{16,20},{20,16},{24,28},{28,24},{1,5},{5... | collective-permute-start | bytes 884744 | tf_op jit(solution)/shard_map/ppermute | solution.py:339
  142.4 14.2 %collective-permute-start.33 = (bf16[72,2048]{1,0:T(8,128)(2,1)S(1)}, bf16[72,2048]{1,0:T(8,128)(2,1)S(1)}, u32[]{:S(2)}, u32[]{:S(2)}) collective-permute-start(bf16[72,2048]{1,0:T(8,128)(2,1)S(1)} %get-tuple-element.102), channel_id=1, source_target_pairs={{0,4},{4,0},{8,12},{12,8},{16,20},{20,16},{24,28},{28,24},{1,5},{5... | collective-permute-start | bytes 884744 | tf_op jit(solution)/shard_map/ppermute | solution.py:339
  143.4 22.5 %collective-permute-start.24 = (bf16[72,2176]{1,0:T(8,128)(2,1)S(1)}, bf16[72,2176]{1,0:T(8,128)(2,1)S(1)}, u32[]{:S(2)}, u32[]{:S(2)}) collective-permute-start(bf16[72,2176]{1,0:T(8,128)(2,1)S(1)} %get-tuple-element.87), channel_id=1, source_target_pairs={{0,4},{4,0},{8,12},{12,8},{16,20},{20,16},{24,28},{28,24},{1,5},{5... | collective-permute-start | bytes 940040 | tf_op jit(solution)/shard_map/ppermute | solution.py:339
  144.7 21.1 %collective-permute-start.25 = (bf16[72,2176]{1,0:T(8,128)(2,1)S(1)}, bf16[72,2176]{1,0:T(8,128)(2,1)S(1)}, u32[]{:S(2)}, u32[]{:S(2)}) collective-permute-start(bf16[72,2176]{1,0:T(8,128)(2,1)S(1)} %get-tuple-element.108), channel_id=1, source_target_pairs={{0,8},{4,12},{8,16},{12,20},{16,24},{20,28},{1,9},{5,13},{9,17},{1... | collective-permute-start | bytes 940040 | tf_op jit(solution)/shard_map/ppermute | solution.py:335
  150.5 15.3 %collective-permute-start.26 = (bf16[72,2176]{1,0:T(8,128)(2,1)S(1)}, bf16[72,2176]{1,0:T(8,128)(2,1)S(1)}, u32[]{:S(2)}, u32[]{:S(2)}) collective-permute-start(bf16[72,2176]{1,0:T(8,128)(2,1)S(1)} %get-tuple-element.107), channel_id=1, source_target_pairs={{8,0},{12,4},{16,8},{20,12},{24,16},{28,20},{9,1},{13,5},{17,9},{2... | collective-permute-start | bytes 940040 | tf_op jit(solution)/shard_map/ppermute | solution.py:335
  (28 other events, 208.0 us)

commit v2 on v0

v2 whole, which is shorter than its diff:
```python
import functools
import math

import numpy as np
import jax
import jax.numpy as jnp
from jax import lax
from jax.experimental import pallas as pl
from jax.experimental.pallas import tpu as pltpu
from jax.sharding import PartitionSpec as P

KWIN = 64
HALF = KWIN // 2
ROTS = 36
TOP = 4
LANES = 2 * KWIN
UNIQUE = (HALF + 1) * LANES
ROW_PAD = 72
CUT = 17
WIDTHS = (CUT * LANES, UNIQUE - CUT * LANES)


def half_tables(box):
    positions = np.arange(box, dtype=np.float32)
    frequencies = np.arange(KWIN, dtype=np.float32) - float(HALF)
    phase_x = (2.0 * math.pi * positions[:, None] * frequencies[None, : HALF + 1] / box).astype(np.float32)
    x_rows = np.zeros((ROW_PAD, box), np.float32)
    x_rows[: HALF + 1] = np.cos(phase_x).T / box
    x_rows[HALF + 1 : 2 * HALF + 2] = -np.sin(phase_x).T / box
    angle = (2.0 * math.pi * positions[:, None] * frequencies[None, :] / box).astype(np.float32)
    cosine, sine = np.cos(angle), np.sin(angle)
    y_rows = np.zeros((2 * box, 2 * LANES), np.float32)
    y_rows[:box, :KWIN] = cosine
    y_rows[:box, KWIN:LANES] = -sine
    y_rows[box:, :KWIN] = sine
    y_rows[box:, KWIN:LANES] = cosine
    y_rows[:box, LANES : LANES + KWIN] = cosine[:, :1]
    y_rows[:box, LANES + KWIN :] = -sine[:, :1]
    y_rows[box:, LANES : LANES + KWIN] = -sine[:, :1]
    y_rows[box:, LANES + KWIN :] = -cosine[:, :1]
    x_wide = np.concatenate([x_rows, np.zeros((ROW_PAD, 2 * LANES - box), np.float32)], axis=1)
    return jnp.asarray(np.concatenate([y_rows, x_wide]), jnp.bfloat16)


def mirror_matrix():
    row = lax.broadcasted_iota(jnp.int32, (LANES, LANES), 0)
    col = lax.broadcasted_iota(jnp.int32, (LANES, LANES), 1)
    value = jnp.where(col < KWIN, 1.0, -1.0)
    hit = (row % KWIN + col % KWIN == KWIN) & (row // KWIN == col // KWIN)
    return jnp.where(hit, value, 0.0).astype(jnp.bfloat16)


def lane_q(shape):
    return lax.broadcasted_iota(jnp.int32, shape, 1) % KWIN


def full_spec(shape):
    return pl.BlockSpec(shape, lambda *_: (0,) * len(shape))


def params(megabytes=24):
    return pltpu.CompilerParams(vmem_limit_bytes=megabytes * 1024 * 1024)


def group(k):
    return slice(k * LANES, (k + 1) * LANES)


def fold_kernel(r_ref, *outs):
    rows = r_ref.shape[0]
    q = lane_q((rows, LANES))
    mirror = mirror_matrix()
    flip = lambda v: jnp.dot(v, mirror, preferred_element_type=jnp.float32)

    def put(k, value):
        out_ref, at = (outs[0], k) if k < CUT else (outs[1], k - CUT)
        out_ref[:, group(at)] = value.astype(out_ref.dtype)

    put(0, r_ref[:, group(0)])
    centre = r_ref[:, group(HALF)]
    special = centre.astype(jnp.float32)
    special = special + jnp.where((q >= 1) & (q < HALF), flip(centre), 0.0)
    for k in range(1, HALF):
        other = r_ref[:, group(KWIN - k)]
        put(k, r_ref[:, group(k)].astype(jnp.float32) + flip(other))
        edge = pltpu.roll(other.astype(jnp.float32), KWIN - k, 1)
        special = jnp.where(q == KWIN - k, edge, special)
    put(HALF, special)


def fold(references):
    rows = references.shape[0]
    return pl.pallas_call(
        fold_kernel,
        out_shape=[jax.ShapeDtypeStruct((rows, width), jnp.bfloat16) for width in WIDTHS],
        compiler_params=params(),
        name="fold",
    )(references)


def unfold_kernel(*rest):
    terms, out_ref = rest[:-1], rest[-1]
    rows = out_ref.shape[0]
    q = lane_q((rows, LANES))
    mirror = mirror_matrix()
    count = len(terms) // 2

    def total(k):
        chosen, at = (terms[:count], k) if k < CUT else (terms[count:], k - CUT)
        return sum(t[:, group(at)].astype(jnp.float32) for t in chosen)

    def flip(v):
        high = v.astype(jnp.bfloat16)
        low = (v - high.astype(jnp.float32)).astype(jnp.bfloat16)
        return jnp.dot(high, mirror, preferred_element_type=jnp.float32) + jnp.dot(
            low, mirror, preferred_element_type=jnp.float32
        )

    special = total(HALF)
    out_ref[:, group(0)] = total(0)
    out_ref[:, group(HALF)] = jnp.where(q <= HALF, special, flip(special))
    for k in range(1, HALF):
        value = total(k)
        out_ref[:, group(k)] = value
        edge = pltpu.roll(special, LANES - (KWIN - k), 1)
        out_ref[:, group(KWIN - k)] = jnp.where(q == 0, edge, flip(value))


def unfold(left, right):
    terms = list(left) + list(right)
    rows = terms[0].shape[0]
    return pl.pallas_call(
        unfold_kernel,
        out_shape=jax.ShapeDtypeStruct((rows, KWIN * LANES), jnp.float32),
        compiler_params=params(),
        name="unfold",
    )(*terms)


def dft_kernel(tile, first, table_ref, img_ref, out_ref, pixel_scratch, rows_scratch, lhs_scratch, sems):
    count, box = out_ref.shape[0], img_ref.shape[1]
    tiles = count // tile

    def copy(n):
        return pltpu.make_async_copy(
            img_ref.at[pl.ds(first + n * tile, tile)], pixel_scratch.at[n], sems.at[n]
        )

    for n in range(tiles):
        copy(n).start()
    y_rows = table_ref[: 2 * box, :]
    x_rows = table_ref[2 * box :, :box]
    q = lane_q((tile, LANES))
    step, batch = 8, 11

    def one(n, carry):
        copy(n).wait()
        for start in range(0, tile, step):
            pixels = pixel_scratch[n, start : start + step].reshape(step * box, box)
            h = lax.dot_general(
                x_rows, pixels, (((1,), (1,)), ((), ())), preferred_element_type=jnp.float32
            )
            for i in range(step):
                at = (start + i) * ROW_PAD
                rows_scratch[at : at + ROW_PAD, :] = h[:, i * box : (i + 1) * box]
        for k in range(HALF + 1):
            for c in range(2):
                j = c * (HALF + 1) + k
                picked = rows_scratch[pl.ds(j, tile, stride=ROW_PAD), :]
                lhs_scratch[k * tile : (k + 1) * tile, c * box : (c + 1) * box] = picked.astype(jnp.bfloat16)
        here = pl.ds(pl.multiple_of(n * tile, tile), tile)
        special = jnp.zeros((tile, LANES), jnp.float32)
        for k in range(HALF + 1):
            if k % batch == 0:
                many = jnp.dot(
                    lhs_scratch[k * tile : (k + batch) * tile, :], y_rows, preferred_element_type=jnp.float32
                )
            both = many[(k % batch) * tile : (k % batch + 1) * tile]
            value = both[:, :LANES]
            if k < HALF:
                out_ref[here, group(k)] = value.astype(jnp.bfloat16)
            else:
                special = jnp.where(q <= HALF, value, special)
            if 0 < k < HALF:
                special = jnp.where(q == KWIN - k, both[:, LANES:], special)
        out_ref[here, group(HALF)] = special.astype(jnp.bfloat16)
        return carry

    lax.fori_loop(0, tiles, one, 0)


def dft(images, table, tile, part, parts):
    count, box = images.shape[0] // parts, images.shape[1]
    return pl.pallas_call(
        functools.partial(dft_kernel, tile, part * count),
        in_specs=[pl.BlockSpec(memory_space=pltpu.VMEM), pl.BlockSpec(memory_space=pl.ANY)],
        out_shape=jax.ShapeDtypeStruct((count, UNIQUE), jnp.bfloat16),
        scratch_shapes=[
            pltpu.VMEM((count // tile, tile, box, box), jnp.bfloat16),
            pltpu.VMEM((tile * ROW_PAD, box), jnp.float32),
            pltpu.VMEM(((HALF + 1) * tile, 2 * box), jnp.bfloat16),
            pltpu.SemaphoreType.DMA((count // tile,)),
        ],
        cost_estimate=pl.CostEstimate(
            flops=count * (2 * box * box * ROW_PAD + 2 * (HALF + 1) * 2 * box * LANES * 2),
            bytes_accessed=2 * count * (box * box + UNIQUE),
            transcendentals=0,
        ),
        compiler_params=params(46),
        name="dft",
    )(table, images)


def stacked_rows(at, base_ref, rows, particles):
    parts = [
        lax.broadcasted_iota(jnp.int32, (rows, particles), 0) + base_ref[n] for n in at
    ]
    return jnp.concatenate(parts, axis=0) if len(parts) > 1 else parts[0]


def stacked_rows(at, base_ref, rows, particles):
    parts = [
        lax.broadcasted_iota(jnp.int32, (rows, particles), 0) + base_ref[n] for n in at
    ]
    return jnp.concatenate(parts, axis=0) if len(parts) > 1 else parts[0]


def score_kernel(items, halves, base_ref, panel_ref, before_ref, *rest):
    specs, refs, out_ref = rest[:halves], list(rest[halves:-1]), rest[-1]
    rows = refs[0].shape[0]
    taken = []
    for at, first, width in items:
        blocks = [refs.pop(0)[...] for _ in at]
        taken.append((at, first, width, jnp.concatenate(blocks, axis=0) if len(blocks) > 1 else blocks[0]))
    edge = 0
    for spec_ref in specs:
        particles = spec_ref.shape[0]
        lanes = slice(edge, edge + particles)
        edge += particles
        picked = [before_ref[t : t + 1, lanes] for t in range(TOP)]
        for at, first, width, block in taken:
            s = lax.dot_general(
                block,
                spec_ref[:, first : first + width],
                (((1,), (1,)), ((), ())),
                preferred_element_type=jnp.float32,
            )
            row = stacked_rows(at, base_ref, rows, particles)
            for t in range(TOP):
                hit = row == panel_ref[t : t + 1, lanes]
                picked[t] = picked[t] + jnp.sum(jnp.where(hit, s, 0.0), axis=0, keepdims=True)
        for t in range(TOP):
            out_ref[t : t + 1, lanes] = picked[t]


def score(bases, spectra, panel, before, items):
    rows = items[0][2][0].shape[0]
    refs = [r for _, _, blocks in items for r in blocks]
    values = sum(r.shape[1] for r in refs) * rows
    shapes = [(at, first, blocks[0].shape[1]) for at, first, blocks in items]
    return pl.pallas_call(
        functools.partial(score_kernel, shapes, len(spectra)),
        in_specs=[pl.BlockSpec(memory_space=pltpu.SMEM)]
        + [pl.BlockSpec(memory_space=pltpu.VMEM)] * (2 + len(spectra) + len(refs)),
        out_shape=jax.ShapeDtypeStruct(panel.shape, jnp.float32),
        cost_estimate=pl.CostEstimate(
            flops=2 * values * panel.shape[1], bytes_accessed=2 * values, transcendentals=0
        ),
        compiler_params=params(),
        name="score",
    )(bases, panel, before, *spectra, *refs)


def weight_kernel(scores_ref, prior_ref, precision_ref, out_ref):
    value = jnp.sum(scores_ref[...], axis=0) * precision_ref[...]
    unscaled = prior_ref[...] * jnp.exp(value - jnp.max(value, axis=0, keepdims=True))
    weight = unscaled / jnp.sum(unscaled, axis=0, keepdims=True)
    out_ref[...] = weight.astype(jnp.bfloat16).astype(jnp.float32)


def weights_of(scores, prior, precision):
    return pl.pallas_call(
        weight_kernel,
        out_shape=jax.ShapeDtypeStruct(prior.shape, jnp.float32),
        compiler_params=params(),
        name="weights",
    )(scores, prior, precision)


def sums_kernel(items, halves, base_ref, weight_ref, panel_ref, *rest):
    specs, outs = rest[:halves], list(rest[halves:])
    particles = panel_ref.shape[1]
    for at, first in items:
        rows, width = outs[0].shape
        row = stacked_rows(at, base_ref, rows, particles)
        select = jnp.zeros(row.shape, jnp.float32)
        for t in range(TOP):
            select = select + jnp.where(row == panel_ref[t : t + 1, :], weight_ref[t : t + 1, :], 0.0)
        select = select.astype(jnp.bfloat16)
        total, edge = None, 0
        for spec_ref in specs:
            count = spec_ref.shape[0]
            term = jnp.dot(
                select[:, edge : edge + count],
                spec_ref[:, first : first + width],
                preferred_element_type=jnp.float32,
            )
            total = term if total is None else total + term
            edge += count
        for n in range(len(at)):
            out_ref = outs.pop(0)
            out_ref[...] = total[n * rows : (n + 1) * rows].astype(out_ref.dtype)


def sums(bases, weight, panel, spectra, rows, items, dtype):
    particles = panel.shape[1]
    shapes = [(rows, width) for at, _, width in items for _ in at]
    values = sum(a * b for a, b in shapes)
    return pl.pallas_call(
        functools.partial(sums_kernel, [(at, first) for at, first, _ in items], len(spectra)),
        in_specs=[pl.BlockSpec(memory_space=pltpu.SMEM)]
        + [pl.BlockSpec(memory_space=pltpu.VMEM)] * (2 + len(spectra)),
        out_shape=[jax.ShapeDtypeStruct(shape, dtype) for shape in shapes],
        cost_estimate=pl.CostEstimate(
            flops=2 * values * particles, bytes_accessed=4 * values, transcendentals=0
        ),
        compiler_params=params(),
        name="sums",
    )(bases, weight, panel, *spectra)


RING = (0, 2, 4, 6, 7, 5, 3, 1)


def ring_places():
    count = len(RING)
    table = np.zeros((count, count), np.int32)
    for at, place in enumerate(RING):
        table[place] = [RING[(at + d) % count] for d in range(count)]
    return table


def onward(value):
    return lax.ppermute(value, "dp", list(zip(RING, RING[1:] + RING[:1])))


def backward(value):
    return lax.ppermute(value, "dp", list(zip(RING[1:] + RING[:1], RING)))


def tie(*values):
    return lax.optimization_barrier(values)


def by_ring(images, references, panel, prior, precision):
    rows = references.shape[0]
    cls_count = lax.axis_size("cls")
    place, mine = lax.axis_index("dp"), lax.axis_index("cls")
    table = half_tables(images.shape[1])
    bases = (jnp.asarray(ring_places())[place] * cls_count + mine) * rows
    starts = (0, WIDTHS[0])

    own = fold(references)
    p1 = onward(own[0]), backward(own[1])
    q1 = onward(own[1]), backward(own[0])
    left = dft(images, table, 64, 0, 2)
    *p1, left, table = tie(*p1, left, table)
    p2 = onward(p1[0]), backward(p1[1])
    *q1, table = tie(*q1, table)
    q2 = onward(q1[0]), backward(q1[1])
    right = dft(images, table, 64, 1, 2)
    *p2, right = tie(*p2, right)
    p3 = onward(p2[0]), backward(p2[1])
    *q2, right = tie(*q2, right)
    q3 = onward(q2[0]), backward(q2[1])
    spectra = [left, right]
    picked = jnp.zeros(panel.shape, jnp.float32)
    near = [
        ((0, 7, 1), starts[0], [own[0], p1[0], q1[1]]),
        ((0, 7, 1), starts[1], [own[1], q1[0], p1[1]]),
        ((6, 2), starts[0], [p2[0], q2[1]]),
        ((6, 2), starts[1], [q2[0], p2[1]]),
    ]
    picked = score(bases, spectra, panel, picked, near)
    *p3, picked = tie(*p3, picked)
    p4 = onward(p3[0]), backward(p3[1])
    *q3, picked = tie(*q3, picked)
    middle = [((5, 3), starts[0], [p3[0], q3[1]]), ((5, 3), starts[1], [q3[0], p3[1]])]
    picked = score(bases, spectra, panel, picked, middle)
    *p4, picked = tie(*p4, picked)
    picked = score(bases, spectra, panel, picked, [((4,), starts[p], [p4[p]]) for p in range(2)])

    scores = lax.all_gather(picked, "cls", axis=0, tiled=False)
    weight = weights_of(scores, prior, precision)

    narrow, wide = jnp.bfloat16, jnp.float32
    part = functools.partial(sums, bases, weight, panel, spectra, rows)
    pieces = [(starts[p], WIDTHS[p]) for p in range(2)]
    far0, back0, far1, ahead1 = part([((4, 5), *pieces[0]), ((4, 3), *pieces[1])], narrow)
    p = onward(far0), backward(far1)
    q = onward(ahead1), backward(back0)
    rest = part([((3, 2, 6, 1, 7, 0), *pieces[0]), ((5, 2, 6, 1, 7, 0), *pieces[1])], wide)

    def pass_on(arrived, held):
        onto = [(h + a.astype(wide)).astype(narrow) for h, a in zip(held, arrived)]
        return onward(onto[0]), backward(onto[1])

    p = tie(*p)
    p = pass_on(p, (rest[0], rest[6]))
    q = pass_on(q, (rest[7], rest[2]))
    p = pass_on(p, (rest[1], rest[8]))
    q = pass_on(q, (rest[9], rest[4]))
    p = pass_on(p, (rest[3], rest[10]))
    return unfold([rest[5], p[0], q[1]], [rest[11], q[0], p[1]])


def by_collectives(images, references, panel, prior, precision):
    rows = references.shape[0]
    dp_count = lax.axis_size("dp")
    cls_count = lax.axis_size("cls")
    mine = lax.axis_index("cls")
    table = half_tables(images.shape[1])
    own = jnp.concatenate(fold(references), axis=1)
    gathered = lax.all_gather(own, "dp", axis=0, tiled=False)
    spectra = [dft(images, table, 64, part, 2) for part in range(2)]
    bases = (jnp.arange(dp_count, dtype=jnp.int32) * cls_count + mine) * rows
    picked = jnp.zeros(panel.shape, jnp.float32)
    items = [((n,), 0, [gathered[n]]) for n in range(dp_count)]
    for start in range(0, dp_count, 8):
        picked = score(bases, spectra, panel, picked, items[start : start + 8])
    scores = lax.all_gather(picked, "cls", axis=0, tiled=False)
    weight = weights_of(scores, prior, precision)
    partial = []
    for start in range(0, dp_count, 8):
        items = [((n,), 0, UNIQUE) for n in range(start, min(start + 8, dp_count))]
        partial += sums(bases, weight, panel, spectra, rows, items, jnp.bfloat16)
    half = lax.psum_scatter(jnp.stack(partial), "dp", scatter_dimension=0, tiled=False)
    return unfold([half[:, : WIDTHS[0]]], [half[:, WIDTHS[0] :]])


def on_device(images, references, best_class, best_rot, prior, precision):
    panel = (best_class * ROTS + best_rot).T
    plan = by_ring if lax.axis_size("dp") == len(RING) else by_collectives
    return plan(images, references, panel, prior.T, precision[None, :])


def solution(mesh):
    in_specs = (
        P("dp", None, None),
        P(("dp", "cls"), None),
        P("dp", None),
        P("dp", None),
        P("dp", None),
        P("dp"),
    )
    out_specs = P(("dp", "cls"), None)
    return jax.shard_map(on_device, mesh=mesh, in_specs=in_specs, out_specs=out_specs, check_vma=False)
```

time: 418 us -> 117 us (0.28)
  waiting for transfers between devices: 263 us -> 41.9 us
  matrix products: 91.8 us -> 0 us
  Pallas kernels: 0 us -> 30.4 us
  starting transfers between devices: 0.04 us -> 30.2 us
  local copies, waits for them, and re-layouts: 32.7 us -> 7.09 us
  between operations: 13.5 us -> 0.26 us
  blocking collectives: 12.4 us -> 5.19 us
    reduce_scatter x1 -> x0, waiting for transfers between devices: 161 us -> none  [on_device(): lax.psum_scatter(partial_sums.astype(jnp.bfloat16), 'dp', scatter_dimensi...]
    all_gather x1 -> x0, waiting for transfers between devices: 101 us -> none  [on_device(): lax.all_gather(references, 'dp', axis=0, tiled=True)]
    dot_general x7 -> x0, matrix products: 91.8 us -> none  [the longest x4 56 us: on_device(): jnp.dot(selector, spectrum, preferred_element_type=jnp.float32)]
    ppermute x0 -> x28, waiting for transfers between devices: none -> 41.9 us  [the longest x14 24.1 us: onward(): return lax.ppermute(value, 'dp', list(zip(RING, RING[1:] + RING[:1])))]
    pallas_call x0 -> x10, Pallas kernels: none -> 30.4 us  [the longest x2 14.8 us: dft(): pl.pallas_call(functools.partial(dft_kernel, tile, part * count), in_spec...]
    ppermute x0 -> x28, starting transfers between devices: none -> 30.2 us  [the longest x14 23.4 us: onward(): return lax.ppermute(value, 'dp', list(zip(RING, RING[1:] + RING[:1])))]
    gather x5 -> x0, local copies, waits for them, and re-layouts: 17.5 us -> none  [on_device(): jnp.take_along_axis(raw_scores, local_ids, axis=1) * precision[:, None]]
    unnamed x7 -> x26, local copies, waits for them, and re-layouts: 15.1 us -> 7.09 us
  transfers between devices with their start and end apart: 2 -> 28, of which waited for: 2 -> 11; matrix products, arithmetic and copies ran while one was open for 10% -> 1% of each run, Pallas kernels for 0% -> 21%
where the time goes in v2:
time: 117 us; the launch traced here: 116 us
  waiting for transfers between devices  41.9 us (36%)
  Pallas kernels  30.4 us (26%)
  starting transfers between devices  30.2 us (26%)
  local copies, waits for them, and re-layouts  7.09 us (6%)
  blocking collectives  5.19 us (4%)
  other arithmetic  1.37 us (1%)
    ppermute x14, waiting for transfers between devices, onward(): return lax.ppermute(value, 'dp', list(zip(RING, RING[1:] + RING[:1])))  24.1 us
    ppermute x14, starting transfers between devices, onward(): return lax.ppermute(value, 'dp', list(zip(RING, RING[1:] + RING[:1])))  23.4 us
    ppermute x14, waiting for transfers between devices, backward(): return lax.ppermute(value, 'dp', list(zip(RING[1:] + RING[:1], RING)))  17.8 us
    pallas_call x2, Pallas kernels, dft(): pl.pallas_call(functools.partial(dft_kernel, tile, part * count), in_spec...  14.8 us
    pallas_call x3, Pallas kernels, score(): pl.pallas_call(functools.partial(score_kernel, shapes, len(spectra)), in_...  8.59 us
    unnamed x26, local copies, waits for them, and re-layouts  7.09 us
    ppermute x14, starting transfers between devices, backward(): return lax.ppermute(value, 'dp', list(zip(RING[1:] + RING[:1], RING)))  6.77 us
    all_gather x1, blocking collectives, by_ring(): scores = lax.all_gather(picked, 'cls', axis=0, tiled=False)  5.19 us
  transfers between devices with their start and end apart: 28, of which 11 were waited for; matrix products, arithmetic and copies ran while one was open for 1% of the time, Pallas kernels for 21%

profile of v2, /device:TPU:0, one launch (start us, length us, event | category | flops | bytes accessed | tf_op | source)
XLA Modules:
  0.0 116.5 jit_solution(11213633568765309438)
XLA Ops:
  1.9 3.1 %collective-permute-start = (bf16[72,2176]{1,0:T(8,128)(2,1)S(1)}, bf16[72,2176]{1,0:T(8,128)(2,1)S(1)}, u32[]{:S(2)}, u32[]{:S(2)}) collective-permute-start(bf16[72,2176]{1,0:T(8,128)(2,1)S(1)} %get-tuple-element.47.rest_2_), channel_id=1, source_target_pairs={{0,8},{8,16},{16,24},{24,28},{28,20},{20,12},{12,4},{4,0},{1,9},{9... | collective-permute-start | bytes 940040 | tf_op jit(solution)/shard_map/ppermute | solution.py:344
  4.9 1.9 %collective-permute-start.5 = (bf16[72,2176]{1,0:T(8,128)(2,1)S(1)}, bf16[72,2176]{1,0:T(8,128)(2,1)S(1)}, u32[]{:S(2)}, u32[]{:S(2)}) collective-permute-start(bf16[72,2176]{1,0:T(8,128)(2,1)S(1)} %get-tuple-element.47.rest_2_), channel_id=1, source_target_pairs={{8,0},{16,8},{24,16},{28,24},{20,28},{12,20},{4,12},{0,4},{9,1},{1... | collective-permute-start | bytes 940040 | tf_op jit(solution)/shard_map/ppermute | solution.py:348
  7.9 7.4 %dft.2.rest_0_ = bf16[256,4224]{1,0:T(8,128)(2,1)S(1)} custom-call(bf16[328,256]{1,0:T(8,128)(2,1)S(1)} %copy-done.4, bf16[512,128,128]{2,1,0:T(8,128)(2,1)} %img_ref.3), custom_call_target="tpu_custom_call" | custom-call | flops 1711276032 | bytes 10551296 | tf_op jit(solution)/shard_map/dft/pallas_call | solution.py:194
  15.4 2.0 %collective-permute-start.2 = (bf16[72,2176]{1,0:T(8,128)(2,1)S(1)}, bf16[72,2176]{1,0:T(8,128)(2,1)}, u32[]{:S(2)}, u32[]{:S(2)}) collective-permute-start(bf16[72,2176]{1,0:T(8,128)(2,1)S(1)} %collective-permute-done.rest_3_), channel_id=1, source_target_pairs={{0,8},{8,16},{16,24},{24,28},{28,20},{20,12},{12,4},{4,0},{1,9},{9... | collective-permute-start | bytes 940040 | tf_op jit(solution)/shard_map/ppermute | solution.py:344
  17.4 2.1 %collective-permute-done.4.rest_6_ = bf16[72,2048]{1,0:T(8,128)(2,1)} collective-permute-done((bf16[72,2048]{1,0:T(8,128)(2,1)S(1)}, bf16[72,2048]{1,0:T(8,128)(2,1)}, u32[]{:S(2)}, u32[]{:S(2)}) %collective-permute-start.4) | collective-permute-done | bytes 294944 | tf_op jit(solution)/shard_map/ppermute | solution.py:344
  19.5 2.1 %collective-permute-done.5.rest_4_ = bf16[72,2176]{1,0:T(8,128)(2,1)S(1)} collective-permute-done((bf16[72,2176]{1,0:T(8,128)(2,1)S(1)}, bf16[72,2176]{1,0:T(8,128)(2,1)S(1)}, u32[]{:S(2)}, u32[]{:S(2)}) %collective-permute-start.5) | collective-permute-done | bytes 313376 | tf_op jit(solution)/shard_map/ppermute | solution.py:348
  23.6 7.4 %dft.3.rest_1_ = bf16[256,4224]{1,0:T(8,128)(2,1)S(1)} custom-call(bf16[328,256]{1,0:T(8,128)(2,1)S(1)} %copy-done.4, bf16[512,128,128]{2,1,0:T(8,128)(2,1)} %img_ref.3), custom_call_target="tpu_custom_call" | custom-call | flops 1711276032 | bytes 10551296 | tf_op jit(solution)/shard_map/dft/pallas_call | solution.py:194
  32.4 2.0 %collective-permute-start.6 = (bf16[72,2176]{1,0:T(8,128)(2,1)}, bf16[72,2176]{1,0:T(8,128)(2,1)S(1)}, u32[]{:S(2)}, u32[]{:S(2)}) collective-permute-start(bf16[72,2176]{1,0:T(8,128)(2,1)} %collective-permute-done.2.rest_8_), channel_id=1, source_target_pairs={{0,8},{8,16},{16,24},{24,28},{28,20},{20,12},{12,4},{4,0},{1,9},{9... | collective-permute-start | bytes 940040 | tf_op jit(solution)/shard_map/ppermute | solution.py:344
  40.7 4.2 %score.3.before_ref = f32[4,512]{1,0:T(4,128)S(1)} custom-call(s32[8]{0:T(128)S(1)} %multiply_bitcast_fusion.base_ref, s32[4,512]{1,0:T(4,128)S(1)} %add_bitcast_fusion.panel_ref, f32[4,512]{1,0:T(4,128)S(1)} %broadcast_in_dim.6.before_ref, bf16[256,4224]{1,0:T(8,128)(2,1)S(1)} %dft.2.rest_0_, bf16[256,4224]{1,0:T(8,128)(2,1)S(1)} %copy-done.1, ...), custom_call_target="tpu_custom_call" | custom-call | flops 1557135360 | bytes 3041280 | tf_op jit(solution)/shard_map/score/pallas_call | solution.py:261
  44.9 1.6 %collective-permute-start.10 = (bf16[72,2176]{1,0:T(8,128)(2,1)S(1)}, bf16[72,2176]{1,0:T(8,128)(2,1)S(1)}, u32[]{:S(2)}, u32[]{:S(2)}) collective-permute-start(bf16[72,2176]{1,0:T(8,128)(2,1)S(1)} %collective-permute-done.6.rest_2_), channel_id=1, source_target_pairs={{0,8},{8,16},{16,24},{24,28},{28,20},{20,12},{12,4},{4,0},{1,9},{9... | collective-permute-start | bytes 940040 | tf_op jit(solution)/shard_map/ppermute | solution.py:344
  47.0 2.5 %score.4.before_ref = f32[4,512]{1,0:T(4,128)S(1)} custom-call(s32[8]{0:T(128)S(1)} %multiply_bitcast_fusion.base_ref, s32[4,512]{1,0:T(4,128)S(1)} %add_bitcast_fusion.panel_ref, f32[4,512]{1,0:T(4,128)S(1)} %score.3.before_ref, bf16[256,4224]{1,0:T(8,128)(2,1)S(1)} %dft.2.rest_0_, bf16[256,4224]{1,0:T(8,128)(2,1)S(1)} %copy-done.1, ...), custom_call_target="tpu_custom_call" | custom-call | flops 622854144 | bytes 1216512 | tf_op jit(solution)/shard_map/score/pallas_call | solution.py:261
  49.6 3.9 %collective-permute-done.11.rest_3_ = bf16[72,2048]{1,0:T(8,128)(2,1)S(1)} collective-permute-done((bf16[72,2048]{1,0:T(8,128)(2,1)}, bf16[72,2048]{1,0:T(8,128)(2,1)S(1)}, u32[]{:S(2)}, u32[]{:S(2)}) %collective-permute-start.11) | collective-permute-done | bytes 294944 | tf_op jit(solution)/shard_map/ppermute | solution.py:348
  53.5 1.9 %score.5 = f32[4,512]{1,0:T(4,128)S(1)} custom-call(s32[8]{0:T(128)S(1)} %multiply_bitcast_fusion.base_ref, s32[4,512]{1,0:T(4,128)S(1)} %add_bitcast_fusion.panel_ref, f32[4,512]{1,0:T(4,128)S(1)} %score.4.before_ref, bf16[256,4224]{1,0:T(8,128)(2,1)S(1)} %dft.2.rest_0_, bf16[256,4224]{1,0:T(8,128)(2,1)S(1)} %copy-done.1, ...), custom_call_target="tpu_custom_call" | custom-call | flops 311427072 | bytes 608256 | tf_op jit(solution)/shard_map/score/pallas_call | solution.py:261
  55.4 5.2 %all-gather.1.scores_ref = f32[4,4,512]{2,1,0:T(4,128)S(1)} all-gather(f32[1,4,512]{2,1,0:T(4,128)S(1)} %bitcast.7), channel_id=2, replica_groups=mesh['dp'=8,'cls'=4] {'cls'}, dimensions={0}, use_global_device_ids=true | all-gather | bytes 40960 | tf_op jit(solution)/shard_map/all_gather | solution.py:393
  66.2 2.8 %sums.2 = (f32[72,2176]{1,0:T(8,128)S(1)}, f32[72,2176]{1,0:T(8,128)S(1)}, f32[72,2176]{1,0:T(8,128)S(1)}, f32[72,2176]{1,0:T(8,128)S(1)}, f32[72,2176]{1,0:T(8,...) custom-call(s32[8]{0:T(128)S(1)} %multiply_bitcast_fusion.base_ref, ...), custom_call_target="tpu_custom_call" | custom-call | flops 1868562432 | bytes 7299072 | tf_op jit(solution)/shard_map/sums/pallas_call | solution.py:319
  69.0 3.0 %collective-permute-done.22 = bf16[72,2048]{1,0:T(8,128)(2,1)S(1)} collective-permute-done((bf16[72,2048]{1,0:T(8,128)(2,1)S(1)}, bf16[72,2048]{1,0:T(8,128)(2,1)S(1)}, u32[]{:S(2)}, u32[]{:S(2)}) %collective-permute-start.22) | collective-permute-done | bytes 294944 | tf_op jit(solution)/shard_map/ppermute | solution.py:344
  73.7 5.0 %collective-permute-done.14 = bf16[72,2176]{1,0:T(8,128)(2,1)S(1)} collective-permute-done((bf16[72,2176]{1,0:T(8,128)(2,1)S(1)}, bf16[72,2176]{1,0:T(8,128)(2,1)S(1)}, u32[]{:S(2)}, u32[]{:S(2)}) %collective-permute-start.14) | collective-permute-done | bytes 313376 | tf_op jit(solution)/shard_map/ppermute | solution.py:344
  81.5 3.5 %collective-permute-done.23 = bf16[72,2048]{1,0:T(8,128)(2,1)S(1)} collective-permute-done((bf16[72,2048]{1,0:T(8,128)(2,1)S(1)}, bf16[72,2048]{1,0:T(8,128)(2,1)S(1)}, u32[]{:S(2)}, u32[]{:S(2)}) %collective-permute-start.23) | collective-permute-done | bytes 294944 | tf_op jit(solution)/shard_map/ppermute | solution.py:344
  86.7 2.0 %collective-permute-done.25 = bf16[72,2048]{1,0:T(8,128)(2,1)S(1)} collective-permute-done((bf16[72,2048]{1,0:T(8,128)(2,1)S(1)}, bf16[72,2048]{1,0:T(8,128)(2,1)S(1)}, u32[]{:S(2)}, u32[]{:S(2)}) %collective-permute-start.25) | collective-permute-done | bytes 294944 | tf_op jit(solution)/shard_map/ppermute | solution.py:348
  89.3 2.4 %collective-permute-done.16 = bf16[72,2176]{1,0:T(8,128)(2,1)S(1)} collective-permute-done((bf16[72,2176]{1,0:T(8,128)(2,1)S(1)}, bf16[72,2176]{1,0:T(8,128)(2,1)S(1)}, u32[]{:S(2)}, u32[]{:S(2)}) %collective-permute-start.16) | collective-permute-done | bytes 313376 | tf_op jit(solution)/shard_map/ppermute | solution.py:344
  93.4 2.0 %collective-permute-done.20 = bf16[72,2176]{1,0:T(8,128)(2,1)S(1)} collective-permute-done((bf16[72,2176]{1,0:T(8,128)(2,1)S(1)}, bf16[72,2176]{1,0:T(8,128)(2,1)S(1)}, u32[]{:S(2)}, u32[]{:S(2)}) %collective-permute-start.20) | collective-permute-done | bytes 313376 | tf_op jit(solution)/shard_map/ppermute | solution.py:348
  96.1 8.1 %collective-permute-done.17 = bf16[72,2176]{1,0:T(8,128)(2,1)S(1)} collective-permute-done((bf16[72,2176]{1,0:T(8,128)(2,1)S(1)}, bf16[72,2176]{1,0:T(8,128)(2,1)S(1)}, u32[]{:S(2)}, u32[]{:S(2)}) %collective-permute-start.17) | collective-permute-done | bytes 313376 | tf_op jit(solution)/shard_map/ppermute | solution.py:344
  106.5 7.7 %collective-permute-done.27.rest_5_ = bf16[72,2048]{1,0:T(8,128)(2,1)S(1)} collective-permute-done((bf16[72,2048]{1,0:T(8,128)(2,1)S(1)}, bf16[72,2048]{1,0:T(8,128)(2,1)S(1)}, u32[]{:S(2)}, u32[]{:S(2)}) %collective-permute-start.27) | collective-permute-done | bytes 294944 | tf_op jit(solution)/shard_map/ppermute | solution.py:348
  114.2 2.3 %unfold.1 = f32[72,8192]{1,0:T(8,128)} custom-call(f32[72,2176]{1,0:T(8,128)S(1)} %get-tuple-element.71.rest_0_, bf16[72,2176]{1,0:T(8,128)(2,1)S(1)} %collective-permute-done.18.rest_1_, bf16[72,2176]{1,0:T(8,128)(2,1)S(1)} %collective-permute-done.21.rest_2_, f32[72,2048]{1,0:T(8,128)S(1)} %get-tuple-element.81.rest_3_, ...), custom_call_target="tpu_custom_call" | custom-call | tf_op jit(solution)/shard_map/unfold/pallas_call | solution.py:132
  (82 shorter events, 30.0 us)
Async XLA Ops:
  1.9 13.5 %collective-permute-start = (bf16[72,2176]{1,0:T(8,128)(2,1)S(1)}, bf16[72,2176]{1,0:T(8,128)(2,1)S(1)}, u32[]{:S(2)}, u32[]{:S(2)}) collective-permute-start(bf16[72,2176]{1,0:T(8,128)(2,1)S(1)} %get-tuple-element.47.rest_2_), channel_id=1, source_target_pairs={{0,8},{8,16},{16,24},{24,28},{28,20},{20,12},{12,4},{4,0},{1,9},{9... | collective-permute-start | bytes 940040 | tf_op jit(solution)/shard_map/ppermute | solution.py:344
  4.9 10.4 %collective-permute-start.1 = (bf16[72,2048]{1,0:T(8,128)(2,1)S(1)}, bf16[72,2048]{1,0:T(8,128)(2,1)S(1)}, u32[]{:S(2)}, u32[]{:S(2)}) collective-permute-start(bf16[72,2048]{1,0:T(8,128)(2,1)S(1)} %get-tuple-element.48.rest_5_), channel_id=1, source_target_pairs={{8,0},{16,8},{24,16},{28,24},{20,28},{12,20},{4,12},{0,4},{9,1},{1... | collective-permute-start | bytes 884744 | tf_op jit(solution)/shard_map/ppermute | solution.py:348
  4.9 16.6 %collective-permute-start.5 = (bf16[72,2176]{1,0:T(8,128)(2,1)S(1)}, bf16[72,2176]{1,0:T(8,128)(2,1)S(1)}, u32[]{:S(2)}, u32[]{:S(2)}) collective-permute-start(bf16[72,2176]{1,0:T(8,128)(2,1)S(1)} %get-tuple-element.47.rest_2_), channel_id=1, source_target_pairs={{8,0},{16,8},{24,16},{28,24},{20,28},{12,20},{4,12},{0,4},{9,1},{1... | collective-permute-start | bytes 940040 | tf_op jit(solution)/shard_map/ppermute | solution.py:348
  6.9 12.6 %collective-permute-start.4 = (bf16[72,2048]{1,0:T(8,128)(2,1)S(1)}, bf16[72,2048]{1,0:T(8,128)(2,1)}, u32[]{:S(2)}, u32[]{:S(2)}) collective-permute-start(bf16[72,2048]{1,0:T(8,128)(2,1)S(1)} %get-tuple-element.48.rest_5_), channel_id=1, source_target_pairs={{0,8},{8,16},{16,24},{24,28},{28,20},{20,12},{12,4},{4,0},{1,9},{9... | collective-permute-start | bytes 884744 | tf_op jit(solution)/shard_map/ppermute | solution.py:344
  15.4 17.0 %collective-permute-start.2 = (bf16[72,2176]{1,0:T(8,128)(2,1)S(1)}, bf16[72,2176]{1,0:T(8,128)(2,1)}, u32[]{:S(2)}, u32[]{:S(2)}) collective-permute-start(bf16[72,2176]{1,0:T(8,128)(2,1)S(1)} %collective-permute-done.rest_3_), channel_id=1, source_target_pairs={{0,8},{8,16},{16,24},{24,28},{28,20},{20,12},{12,4},{4,0},{1,9},{9... | collective-permute-start | bytes 940040 | tf_op jit(solution)/shard_map/ppermute | solution.py:344
  17.4 14.9 %collective-permute-start.3 = (bf16[72,2048]{1,0:T(8,128)(2,1)S(1)}, bf16[72,2048]{1,0:T(8,128)(2,1)}, u32[]{:S(2)}, u32[]{:S(2)}) collective-permute-start(bf16[72,2048]{1,0:T(8,128)(2,1)S(1)} %collective-permute-done.1.rest_7_), channel_id=1, source_target_pairs={{8,0},{16,8},{24,16},{28,24},{20,28},{12,20},{4,12},{0,4},{9,1},{1... | collective-permute-start | bytes 884744 | tf_op jit(solution)/shard_map/ppermute | solution.py:348
  21.6 13.5 %collective-permute-start.8 = (bf16[72,2048]{1,0:T(8,128)(2,1)}, bf16[72,2048]{1,0:T(8,128)(2,1)}, u32[]{:S(2)}, u32[]{:S(2)}) collective-permute-start(bf16[72,2048]{1,0:T(8,128)(2,1)} %collective-permute-done.4.rest_6_), channel_id=1, source_target_pairs={{0,8},{8,16},{16,24},{24,28},{28,20},{20,12},{12,4},{4,0},{1,9},{9... | collective-permute-start | bytes 884744 | tf_op jit(solution)/shard_map/ppermute | solution.py:344
  23.2 11.9 %collective-permute-start.9 = (bf16[72,2176]{1,0:T(8,128)(2,1)S(1)}, bf16[72,2176]{1,0:T(8,128)(2,1)}, u32[]{:S(2)}, u32[]{:S(2)}) collective-permute-start(bf16[72,2176]{1,0:T(8,128)(2,1)S(1)} %collective-permute-done.5.rest_4_), channel_id=1, source_target_pairs={{8,0},{16,8},{24,16},{28,24},{20,28},{12,20},{4,12},{0,4},{9,1},{1... | collective-permute-start | bytes 940040 | tf_op jit(solution)/shard_map/ppermute | solution.py:348
  32.3 12.6 %collective-permute-start.7 = (bf16[72,2048]{1,0:T(8,128)(2,1)}, bf16[72,2048]{1,0:T(8,128)(2,1)}, u32[]{:S(2)}, u32[]{:S(2)}) collective-permute-start(bf16[72,2048]{1,0:T(8,128)(2,1)} %collective-permute-done.3.rest_11_), channel_id=1, source_target_pairs={{8,0},{16,8},{24,16},{28,24},{20,28},{12,20},{4,12},{0,4},{9,1},{1... | collective-permute-start | bytes 884744 | tf_op jit(solution)/shard_map/ppermute | solution.py:348
  32.4 12.6 %collective-permute-start.6 = (bf16[72,2176]{1,0:T(8,128)(2,1)}, bf16[72,2176]{1,0:T(8,128)(2,1)S(1)}, u32[]{:S(2)}, u32[]{:S(2)}) collective-permute-start(bf16[72,2176]{1,0:T(8,128)(2,1)} %collective-permute-done.2.rest_8_), channel_id=1, source_target_pairs={{0,8},{8,16},{16,24},{24,28},{28,20},{20,12},{12,4},{4,0},{1,9},{9... | collective-permute-start | bytes 940040 | tf_op jit(solution)/shard_map/ppermute | solution.py:344
  35.1 11.9 %collective-permute-start.12 = (bf16[72,2048]{1,0:T(8,128)(2,1)}, bf16[72,2048]{1,0:T(8,128)(2,1)S(1)}, u32[]{:S(2)}, u32[]{:S(2)}) collective-permute-start(bf16[72,2048]{1,0:T(8,128)(2,1)} %collective-permute-done.8.rest_10_), channel_id=1, source_target_pairs={{0,8},{8,16},{16,24},{24,28},{28,20},{20,12},{12,4},{4,0},{1,9},{9... | collective-permute-start | bytes 884744 | tf_op jit(solution)/shard_map/ppermute | solution.py:344
  36.7 10.3 %collective-permute-start.13 = (bf16[72,2176]{1,0:T(8,128)(2,1)}, bf16[72,2176]{1,0:T(8,128)(2,1)S(1)}, u32[]{:S(2)}, u32[]{:S(2)}) collective-permute-start(bf16[72,2176]{1,0:T(8,128)(2,1)} %collective-permute-done.9.rest_9_), channel_id=1, source_target_pairs={{8,0},{16,8},{24,16},{28,24},{20,28},{12,20},{4,12},{0,4},{9,1},{1... | collective-permute-start | bytes 940040 | tf_op jit(solution)/shard_map/ppermute | solution.py:348
  63.7 10.0 %collective-permute-start.15 = (bf16[72,2048]{1,0:T(8,128)(2,1)S(1)}, bf16[72,2048]{1,0:T(8,128)(2,1)S(1)}, u32[]{:S(2)}, u32[]{:S(2)}) collective-permute-start(bf16[72,2048]{1,0:T(8,128)(2,1)S(1)} %get-tuple-element.76), channel_id=1, source_target_pairs={{8,0},{16,8},{24,16},{28,24},{20,28},{12,20},{4,12},{0,4},{9,1},{1... | collective-permute-start | bytes 884744 | tf_op jit(solution)/shard_map/ppermute | solution.py:348
  64.2 14.5 %collective-permute-start.14 = (bf16[72,2176]{1,0:T(8,128)(2,1)S(1)}, bf16[72,2176]{1,0:T(8,128)(2,1)S(1)}, u32[]{:S(2)}, u32[]{:S(2)}) collective-permute-start(bf16[72,2176]{1,0:T(8,128)(2,1)S(1)} %get-tuple-element.75), channel_id=1, source_target_pairs={{0,8},{8,16},{16,24},{24,28},{28,20},{20,12},{12,4},{4,0},{1,9},{9... | collective-permute-start | bytes 940040 | tf_op jit(solution)/shard_map/ppermute | solution.py:344
  65.7 15.2 %collective-permute-start.19 = (bf16[72,2176]{1,0:T(8,128)(2,1)S(1)}, bf16[72,2176]{1,0:T(8,128)(2,1)S(1)}, u32[]{:S(2)}, u32[]{:S(2)}) collective-permute-start(bf16[72,2176]{1,0:T(8,128)(2,1)S(1)} %get-tuple-element.80), channel_id=1, source_target_pairs={{8,0},{16,8},{24,16},{28,24},{20,28},{12,20},{4,12},{0,4},{9,1},{1... | collective-permute-start | bytes 940040 | tf_op jit(solution)/shard_map/ppermute | solution.py:348
  72.0 13.0 %collective-permute-start.23 = (bf16[72,2048]{1,0:T(8,128)(2,1)S(1)}, bf16[72,2048]{1,0:T(8,128)(2,1)S(1)}, u32[]{:S(2)}, u32[]{:S(2)}) collective-permute-start(bf16[72,2048]{1,0:T(8,128)(2,1)S(1)} %add_convert_fusion.9), channel_id=1, source_target_pairs={{0,8},{8,16},{16,24},{24,28},{28,20},{20,12},{12,4},{4,0},{1,9},{9... | collective-permute-start | bytes 884744 | tf_op jit(solution)/shard_map/ppermute | solution.py:344
  78.7 10.0 %collective-permute-start.25 = (bf16[72,2048]{1,0:T(8,128)(2,1)S(1)}, bf16[72,2048]{1,0:T(8,128)(2,1)S(1)}, u32[]{:S(2)}, u32[]{:S(2)}) collective-permute-start(bf16[72,2048]{1,0:T(8,128)(2,1)S(1)} %add_convert_fusion.7), channel_id=1, source_target_pairs={{8,0},{16,8},{24,16},{28,24},{20,28},{12,20},{4,12},{0,4},{9,1},{1... | collective-permute-start | bytes 884744 | tf_op jit(solution)/shard_map/ppermute | solution.py:348
  79.3 12.4 %collective-permute-start.16 = (bf16[72,2176]{1,0:T(8,128)(2,1)S(1)}, bf16[72,2176]{1,0:T(8,128)(2,1)S(1)}, u32[]{:S(2)}, u32[]{:S(2)}) collective-permute-start(bf16[72,2176]{1,0:T(8,128)(2,1)S(1)} %add_convert_fusion.4), channel_id=1, source_target_pairs={{0,8},{8,16},{16,24},{24,28},{28,20},{20,12},{12,4},{4,0},{1,9},{9... | collective-permute-start | bytes 940040 | tf_op jit(solution)/shard_map/ppermute | solution.py:344
  81.0 14.4 %collective-permute-start.20 = (bf16[72,2176]{1,0:T(8,128)(2,1)S(1)}, bf16[72,2176]{1,0:T(8,128)(2,1)S(1)}, u32[]{:S(2)}, u32[]{:S(2)}) collective-permute-start(bf16[72,2176]{1,0:T(8,128)(2,1)S(1)} %add_convert_fusion.1), channel_id=1, source_target_pairs={{8,0},{16,8},{24,16},{28,24},{20,28},{12,20},{4,12},{0,4},{9,1},{1... | collective-permute-start | bytes 940040 | tf_op jit(solution)/shard_map/ppermute | solution.py:348
  85.1 21.4 %collective-permute-start.24 = (bf16[72,2048]{1,0:T(8,128)(2,1)S(1)}, bf16[72,2048]{1,0:T(8,128)(2,1)S(1)}, u32[]{:S(2)}, u32[]{:S(2)}) collective-permute-start(bf16[72,2048]{1,0:T(8,128)(2,1)S(1)} %add_convert_fusion.8), channel_id=1, source_target_pairs={{0,8},{8,16},{16,24},{24,28},{28,20},{20,12},{12,4},{4,0},{1,9},{9... | collective-permute-start | bytes 884744 | tf_op jit(solution)/shard_map/ppermute | solution.py:344
  88.8 17.1 %collective-permute-start.26 = (bf16[72,2048]{1,0:T(8,128)(2,1)S(1)}, bf16[72,2048]{1,0:T(8,128)(2,1)S(1)}, u32[]{:S(2)}, u32[]{:S(2)}) collective-permute-start(bf16[72,2048]{1,0:T(8,128)(2,1)S(1)} %add_convert_fusion.6), channel_id=1, source_target_pairs={{8,0},{16,8},{24,16},{28,24},{20,28},{12,20},{4,12},{0,4},{9,1},{1... | collective-permute-start | bytes 884744 | tf_op jit(solution)/shard_map/ppermute | solution.py:348
  91.8 12.4 %collective-permute-start.17 = (bf16[72,2176]{1,0:T(8,128)(2,1)S(1)}, bf16[72,2176]{1,0:T(8,128)(2,1)S(1)}, u32[]{:S(2)}, u32[]{:S(2)}) collective-permute-start(bf16[72,2176]{1,0:T(8,128)(2,1)S(1)} %add_convert_fusion.3), channel_id=1, source_target_pairs={{0,8},{8,16},{16,24},{24,28},{28,20},{20,12},{12,4},{4,0},{1,9},{9... | collective-permute-start | bytes 940040 | tf_op jit(solution)/shard_map/ppermute | solution.py:344
  95.5 10.9 %collective-permute-start.21 = (bf16[72,2176]{1,0:T(8,128)(2,1)S(1)}, bf16[72,2176]{1,0:T(8,128)(2,1)S(1)}, u32[]{:S(2)}, u32[]{:S(2)}) collective-permute-start(bf16[72,2176]{1,0:T(8,128)(2,1)S(1)} %add_convert_fusion), channel_id=1, source_target_pairs={{8,0},{16,8},{24,16},{28,24},{20,28},{12,20},{4,12},{0,4},{9,1},{1... | collective-permute-start | bytes 940040 | tf_op jit(solution)/shard_map/ppermute | solution.py:348
  104.3 9.9 %collective-permute-start.18 = (bf16[72,2176]{1,0:T(8,128)(2,1)S(1)}, bf16[72,2176]{1,0:T(8,128)(2,1)S(1)}, u32[]{:S(2)}, u32[]{:S(2)}) collective-permute-start(bf16[72,2176]{1,0:T(8,128)(2,1)S(1)} %add_convert_fusion.2), channel_id=1, source_target_pairs={{0,8},{8,16},{16,24},{24,28},{28,20},{20,12},{12,4},{4,0},{1,9},{9... | collective-permute-start | bytes 940040 | tf_op jit(solution)/shard_map/ppermute | solution.py:344
  (17 other events, 141.3 us)

commit v3 on v2

--- a/solution.py
+++ b/solution.py
@@ -58,7 +58,7 @@
     return pl.BlockSpec(shape, lambda *_: (0,) * len(shape))
 
 
-def params(megabytes=24):
+def params(megabytes=16):
     return pltpu.CompilerParams(vmem_limit_bytes=megabytes * 1024 * 1024)
 
 
@@ -99,11 +99,17 @@
 
 
 def unfold_kernel(*rest):
-    terms, out_ref = rest[:-1], rest[-1]
+    terms, (result_ref, out_ref, sems) = rest[:-3], rest[-3:]
     rows = out_ref.shape[0]
     q = lane_q((rows, LANES))
     mirror = mirror_matrix()
     count = len(terms) // 2
+    chunk = 8
+    width = chunk * LANES
+
+    def copy(n):
+        lanes = pl.ds(n * width, width)
+        return pltpu.make_async_copy(out_ref.at[:, lanes], result_ref.at[:, lanes], sems.at[n])
 
     def total(k):
         chosen, at = (terms[:count], k) if k < CUT else (terms[count:], k - CUT)
@@ -124,6 +130,13 @@
         out_ref[:, group(k)] = value
         edge = pltpu.roll(special, LANES - (KWIN - k), 1)
         out_ref[:, group(KWIN - k)] = jnp.where(q == 0, edge, flip(value))
+        if (k + 1) % chunk == 0:
+            copy(k // chunk).start()
+        if k % chunk == 0:
+            copy((KWIN - k) // chunk).start()
+    copy(HALF // chunk).start()
+    for n in range(KWIN // chunk):
+        copy(n).wait()
 
 
 def unfold(left, right):
@@ -131,15 +144,22 @@
     rows = terms[0].shape[0]
     return pl.pallas_call(
         unfold_kernel,
+        in_specs=[pl.BlockSpec(memory_space=pltpu.VMEM)] * len(terms),
+        out_specs=pl.BlockSpec(memory_space=pl.ANY),
         out_shape=jax.ShapeDtypeStruct((rows, KWIN * LANES), jnp.float32),
+        scratch_shapes=[
+            pltpu.VMEM((rows, KWIN * LANES), jnp.float32),
+            pltpu.SemaphoreType.DMA((KWIN // 8,)),
+        ],
         compiler_params=params(),
         name="unfold",
     )(*terms)
 
 
-def dft_kernel(tile, first, table_ref, img_ref, out_ref, pixel_scratch, rows_scratch, lhs_scratch, sems):
-    count, box = out_ref.shape[0], img_ref.shape[1]
-    tiles = count // tile
+def dft_kernel(tile, first, table_ref, img_ref, *rest):
+    out_ref, pixel_scratch, rows_scratch, lhs_scratch, sems = rest[-5:]
+    tiles, box = pixel_scratch.shape[0], img_ref.shape[1]
+    kept = out_ref.shape[0] - tiles * tile
 
     def copy(n):
         return pltpu.make_async_copy(
@@ -148,6 +168,8 @@
 
     for n in range(tiles):
         copy(n).start()
+    if kept:
+        out_ref[:kept] = rest[0][...]
     y_rows = table_ref[: 2 * box, :]
     x_rows = table_ref[2 * box :, :box]
     q = lane_q((tile, LANES))
@@ -168,7 +190,7 @@
                 j = c * (HALF + 1) + k
                 picked = rows_scratch[pl.ds(j, tile, stride=ROW_PAD), :]
                 lhs_scratch[k * tile : (k + 1) * tile, c * box : (c + 1) * box] = picked.astype(jnp.bfloat16)
-        here = pl.ds(pl.multiple_of(n * tile, tile), tile)
+        here = pl.ds(pl.multiple_of(kept + n * tile, tile), tile)
         special = jnp.zeros((tile, LANES), jnp.float32)
         for k in range(HALF + 1):
             if k % batch == 0:
@@ -189,12 +211,14 @@
     lax.fori_loop(0, tiles, one, 0)
 
 
-def dft(images, table, tile, part, parts):
-    count, box = images.shape[0] // parts, images.shape[1]
-    return pl.pallas_call(
-        functools.partial(dft_kernel, tile, part * count),
-        in_specs=[pl.BlockSpec(memory_space=pltpu.VMEM), pl.BlockSpec(memory_space=pl.ANY)],
-        out_shape=jax.ShapeDtypeStruct((count, UNIQUE), jnp.bfloat16),
+def dft(images, table, tile, first, count, before=()):
+    box = images.shape[1]
+    total = count + sum(b.shape[0] for b in before)
+    return pl.pallas_call(
+        functools.partial(dft_kernel, tile, first),
+        in_specs=[pl.BlockSpec(memory_space=pltpu.VMEM), pl.BlockSpec(memory_space=pl.ANY)]
+        + [pl.BlockSpec(memory_space=pltpu.VMEM)] * len(before),
+        out_shape=jax.ShapeDtypeStruct((total, UNIQUE), jnp.bfloat16),
         scratch_shapes=[
             pltpu.VMEM((count // tile, tile, box, box), jnp.bfloat16),
             pltpu.VMEM((tile * ROW_PAD, box), jnp.float32),
@@ -208,7 +232,7 @@
         ),
         compiler_params=params(46),
         name="dft",
-    )(table, images)
+    )(table, images, *before)
 
 
 def stacked_rows(at, base_ref, rows, particles):
@@ -271,8 +295,12 @@
     )(bases, panel, before, *spectra, *refs)
 
 
-def weight_kernel(scores_ref, prior_ref, precision_ref, out_ref):
-    value = jnp.sum(scores_ref[...], axis=0) * precision_ref[...]
+def weight_kernel(*rest):
+    (prior_ref, precision_ref, out_ref), scores = rest[-3:], rest[:-3]
+    total = scores[0][...]
+    for ref in scores[1:]:
+        total = total + ref[...]
+    value = total * precision_ref[...]
     unscaled = prior_ref[...] * jnp.exp(value - jnp.max(value, axis=0, keepdims=True))
     weight = unscaled / jnp.sum(unscaled, axis=0, keepdims=True)
     out_ref[...] = weight.astype(jnp.bfloat16).astype(jnp.float32)
@@ -284,7 +312,7 @@
         out_shape=jax.ShapeDtypeStruct(prior.shape, jnp.float32),
         compiler_params=params(),
         name="weights",
-    )(scores, prior, precision)
+    )(*scores, prior, precision)
 
 
 def sums_kernel(items, halves, base_ref, weight_ref, panel_ref, *rest):
@@ -363,17 +391,22 @@
     own = fold(references)
     p1 = onward(own[0]), backward(own[1])
     q1 = onward(own[1]), backward(own[0])
-    left = dft(images, table, 64, 0, 2)
+    half = images.shape[0] // 2
+    left = dft(images, table, 64, 0, half)
     *p1, left, table = tie(*p1, left, table)
     p2 = onward(p1[0]), backward(p1[1])
     *q1, table = tie(*q1, table)
     q2 = onward(q1[0]), backward(q1[1])
-    right = dft(images, table, 64, 1, 2)
-    *p2, right = tie(*p2, right)
+    right = dft(images, table, 64, half, half // 2)
+    *p2, right, table = tie(*p2, right, table)
     p3 = onward(p2[0]), backward(p2[1])
-    *q2, right = tie(*q2, right)
+    *q2, table = tie(*q2, table)
     q3 = onward(q2[0]), backward(q2[1])
+    right = dft(images, table, 64, half + half // 2, half // 2, [right])
     spectra = [left, right]
+    *p3, right = tie(*p3, right)
+    spectra = [left, right]
+    p4 = onward(p3[0]), backward(p3[1])
     picked = jnp.zeros(panel.shape, jnp.float32)
     near = [
         ((0, 7, 1), starts[0], [own[0], p1[0], q1[1]]),
@@ -382,15 +415,14 @@
         ((6, 2), starts[1], [q2[0], p2[1]]),
     ]
     picked = score(bases, spectra, panel, picked, near)
-    *p3, picked = tie(*p3, picked)
-    p4 = onward(p3[0]), backward(p3[1])
     *q3, picked = tie(*q3, picked)
     middle = [((5, 3), starts[0], [p3[0], q3[1]]), ((5, 3), starts[1], [q3[0], p3[1]])]
     picked = score(bases, spectra, panel, picked, middle)
     *p4, picked = tie(*p4, picked)
     picked = score(bases, spectra, panel, picked, [((4,), starts[p], [p4[p]]) for p in range(2)])
 
-    scores = lax.all_gather(picked, "cls", axis=0, tiled=False)
+    turns = [[(c, c ^ n) for c in range(cls_count)] for n in range(1, cls_count)]
+    scores = [picked] + [lax.ppermute(picked, "cls", turn) for turn in turns]
     weight = weights_of(scores, prior, precision)
 
     narrow, wide = jnp.bfloat16, jnp.float32
@@ -422,14 +454,15 @@
     table = half_tables(images.shape[1])
     own = jnp.concatenate(fold(references), axis=1)
     gathered = lax.all_gather(own, "dp", axis=0, tiled=False)
-    spectra = [dft(images, table, 64, part, 2) for part in range(2)]
+    half = images.shape[0] // 2
+    spectra = [dft(images, table, 64, part * half, half) for part in range(2)]
     bases = (jnp.arange(dp_count, dtype=jnp.int32) * cls_count + mine) * rows
     picked = jnp.zeros(panel.shape, jnp.float32)
     items = [((n,), 0, [gathered[n]]) for n in range(dp_count)]
     for start in range(0, dp_count, 8):
         picked = score(bases, spectra, panel, picked, items[start : start + 8])
     scores = lax.all_gather(picked, "cls", axis=0, tiled=False)
-    weight = weights_of(scores, prior, precision)
+    weight = weights_of([scores[n] for n in range(cls_count)], prior, precision)
     partial = []
     for start in range(0, dp_count, 8):
         items = [((n,), 0, UNIQUE) for n in range(start, min(start + 8, dp_count))]

time: 117 us -> 114 us (0.974)
  blocking collectives: 5.19 us -> 0 us
  local copies, waits for them, and re-layouts: 7.09 us -> 2.95 us
  waiting for transfers between devices: 41.9 us -> 45.1 us
  starting transfers between devices: 30.2 us -> 32.4 us
  Pallas kernels: 30.4 us -> 31.6 us
    all_gather x1 -> x0, blocking collectives: 5.19 us -> none  [by_ring(): scores = lax.all_gather(picked, 'cls', axis=0, tiled=False)]
    unnamed x26 -> x34, local copies, waits for them, and re-layouts: 7.09 us -> 2.95 us
    ppermute x14, starting transfers between devices: 23.4 us -> 25.6 us  [onward(): return lax.ppermute(value, 'dp', list(zip(RING, RING[1:] + RING[:1])))]
    ppermute x14, starting transfers between devices: 6.77 us -> 4.85 us  [backward(): return lax.ppermute(value, 'dp', list(zip(RING[1:] + RING[:1], RING)))]
    ppermute x0 -> x3, starting transfers between devices: none -> 1.92 us  [by_ring(): scores = [picked] + [lax.ppermute(picked, 'cls', turn) for turn in turns]]
    ppermute x0 -> x3, waiting for transfers between devices: none -> 1.87 us  [by_ring(): scores = [picked] + [lax.ppermute(picked, 'cls', turn) for turn in turns]]
    ppermute x14, waiting for transfers between devices: 24.1 us -> 25.3 us  [onward(): return lax.ppermute(value, 'dp', list(zip(RING, RING[1:] + RING[:1])))]
    pallas_call x3 -> x4, Pallas kernels: 17 us -> 18.2 us  [the longest x3 16.3 us: dft(): pl.pallas_call(functools.partial(dft_kernel, tile, first), in_specs=[pl.B...]
  transfers between devices with their start and end apart: 28 -> 31, of which waited for: 11 -> 16; matrix products, arithmetic and copies ran while one was open for 1% -> 1% of each run, Pallas kernels for 21% -> 23%
where the time goes in v3:
time: 114 us
  waiting for transfers between devices  45.1 us (40%)
  starting transfers between devices  32.4 us (28%)
  Pallas kernels  31.6 us (28%)
  local copies, waits for them, and re-layouts  2.95 us (3%)
  other arithmetic  1.43 us (1%)
    ppermute x14, starting transfers between devices, onward(): return lax.ppermute(value, 'dp', list(zip(RING, RING[1:] + RING[:1])))  25.6 us
    ppermute x14, waiting for transfers between devices, onward(): return lax.ppermute(value, 'dp', list(zip(RING, RING[1:] + RING[:1])))  25.3 us
    ppermute x14, waiting for transfers between devices, backward(): return lax.ppermute(value, 'dp', list(zip(RING[1:] + RING[:1], RING)))  18 us
    pallas_call x3, Pallas kernels, dft(): pl.pallas_call(functools.partial(dft_kernel, tile, first), in_specs=[pl.B...  16.3 us
    pallas_call x3, Pallas kernels, score(): pl.pallas_call(functools.partial(score_kernel, shapes, len(spectra)), in_...  8.64 us
    ppermute x14, starting transfers between devices, backward(): return lax.ppermute(value, 'dp', list(zip(RING[1:] + RING[:1], RING)))  4.85 us
    pallas_call x2, Pallas kernels, sums(): pl.pallas_call(functools.partial(sums_kernel, [(at, first) for at, first,...  4.16 us
    unnamed x34, local copies, waits for them, and re-layouts  2.95 us
  transfers between devices with their start and end apart: 31, of which 16 were waited for; matrix products, arithmetic and copies ran while one was open for 1% of the time, Pallas kernels for 23%

profile of v3, /device:TPU:0, one launch (start us, length us, event | category | flops | bytes accessed | tf_op | source)
XLA Modules:
  0.0 114.1 jit_solution(9732446477644704688)
XLA Ops:
  1.9 3.1 %collective-permute-start = (bf16[72,2176]{1,0:T(8,128)(2,1)S(1)}, bf16[72,2176]{1,0:T(8,128)(2,1)S(1)}, u32[]{:S(2)}, u32[]{:S(2)}) collective-permute-start(bf16[72,2176]{1,0:T(8,128)(2,1)S(1)} %get-tuple-element.48.rest_2_), channel_id=1, source_target_pairs={{0,8},{8,16},{16,24},{24,28},{28,20},{20,12},{12,4},{4,0},{1,9},{9... | collective-permute-start | bytes 940040 | tf_op jit(solution)/shard_map/ppermute | solution.py:372
  4.9 2.0 %collective-permute-start.4 = (bf16[72,2048]{1,0:T(8,128)(2,1)S(1)}, bf16[72,2048]{1,0:T(8,128)(2,1)}, u32[]{:S(2)}, u32[]{:S(2)}) collective-permute-start(bf16[72,2048]{1,0:T(8,128)(2,1)S(1)} %get-tuple-element.49.rest_5_), channel_id=1, source_target_pairs={{0,8},{8,16},{16,24},{24,28},{28,20},{20,12},{12,4},{4,0},{1,9},{9... | collective-permute-start | bytes 884744 | tf_op jit(solution)/shard_map/ppermute | solution.py:372
  7.9 7.4 %dft.3.rest_0_ = bf16[256,4224]{1,0:T(8,128)(2,1)S(1)} custom-call(bf16[328,256]{1,0:T(8,128)(2,1)S(1)} %copy-done, bf16[512,128,128]{2,1,0:T(8,128)(2,1)} %img_ref.5), custom_call_target="tpu_custom_call" | custom-call | flops 1711276032 | bytes 10551296 | tf_op jit(solution)/shard_map/dft/pallas_call | solution.py:217
  15.4 2.1 %collective-permute-start.2 = (bf16[72,2176]{1,0:T(8,128)(2,1)S(1)}, bf16[72,2176]{1,0:T(8,128)(2,1)}, u32[]{:S(2)}, u32[]{:S(2)}) collective-permute-start(bf16[72,2176]{1,0:T(8,128)(2,1)S(1)} %collective-permute-done.rest_3_), channel_id=1, source_target_pairs={{0,8},{8,16},{16,24},{24,28},{28,20},{20,12},{12,4},{4,0},{1,9},{9... | collective-permute-start | bytes 940040 | tf_op jit(solution)/shard_map/ppermute | solution.py:372
  17.5 2.1 %collective-permute-done.4.rest_6_ = bf16[72,2048]{1,0:T(8,128)(2,1)} collective-permute-done((bf16[72,2048]{1,0:T(8,128)(2,1)S(1)}, bf16[72,2048]{1,0:T(8,128)(2,1)}, u32[]{:S(2)}, u32[]{:S(2)}) %collective-permute-start.4) | collective-permute-done | bytes 294944 | tf_op jit(solution)/shard_map/ppermute | solution.py:372
  19.5 2.2 %collective-permute-done.5.rest_4_ = bf16[72,2176]{1,0:T(8,128)(2,1)} collective-permute-done((bf16[72,2176]{1,0:T(8,128)(2,1)S(1)}, bf16[72,2176]{1,0:T(8,128)(2,1)}, u32[]{:S(2)}, u32[]{:S(2)}) %collective-permute-start.5) | collective-permute-done | bytes 313376 | tf_op jit(solution)/shard_map/ppermute | solution.py:376
  21.7 2.0 %collective-permute-start.8 = (bf16[72,2048]{1,0:T(8,128)(2,1)}, bf16[72,2048]{1,0:T(8,128)(2,1)}, u32[]{:S(2)}, u32[]{:S(2)}) collective-permute-start(bf16[72,2048]{1,0:T(8,128)(2,1)} %collective-permute-done.4.rest_6_), channel_id=1, source_target_pairs={{0,8},{8,16},{16,24},{24,28},{28,20},{20,12},{12,4},{4,0},{1,9},{9... | collective-permute-start | bytes 884744 | tf_op jit(solution)/shard_map/ppermute | solution.py:372
  23.7 4.5 %dft.4.rest_0_ = bf16[128,4224]{1,0:T(8,128)(2,1)S(1)} custom-call(bf16[328,256]{1,0:T(8,128)(2,1)S(1)} %copy-done, bf16[512,128,128]{2,1,0:T(8,128)(2,1)} %img_ref.5), custom_call_target="tpu_custom_call" | custom-call | flops 855638016 | bytes 5275648 | tf_op jit(solution)/shard_map/dft/pallas_call | solution.py:217
  32.5 2.2 %collective-permute-done.9.rest_9_ = bf16[72,2176]{1,0:T(8,128)(2,1)} collective-permute-done((bf16[72,2176]{1,0:T(8,128)(2,1)}, bf16[72,2176]{1,0:T(8,128)(2,1)}, u32[]{:S(2)}, u32[]{:S(2)}) %collective-permute-start.9) | collective-permute-done | bytes 313376 | tf_op jit(solution)/shard_map/ppermute | solution.py:376
  36.8 4.5 %dft.5.rest_1_ = bf16[256,4224]{1,0:T(8,128)(2,1)S(1)} custom-call(bf16[328,256]{1,0:T(8,128)(2,1)S(1)} %copy-done.1, bf16[512,128,128]{2,1,0:T(8,128)(2,1)} %img_ref.5, bf16[128,4224]{1,0:T(8,128)(2,1)S(1)} %dft.4.rest_0_), custom_call_target="tpu_custom_call" | custom-call | flops 855638016 | bytes 5275648 | tf_op jit(solution)/shard_map/dft/pallas_call | solution.py:217
  41.3 2.0 %collective-permute-start.10 = (bf16[72,2176]{1,0:T(8,128)(2,1)}, bf16[72,2176]{1,0:T(8,128)(2,1)S(1)}, u32[]{:S(2)}, u32[]{:S(2)}) collective-permute-start(bf16[72,2176]{1,0:T(8,128)(2,1)} %collective-permute-done.6.rest_2_), channel_id=1, source_target_pairs={{0,8},{8,16},{16,24},{24,28},{28,20},{20,12},{12,4},{4,0},{1,9},{9... | collective-permute-start | bytes 940040 | tf_op jit(solution)/shard_map/ppermute | solution.py:372
  44.1 4.2 %score.3.before_ref = f32[4,512]{1,0:T(4,128)S(1)} custom-call(s32[8]{0:T(128)S(1)} %multiply_bitcast_fusion.base_ref, s32[4,512]{1,0:T(4,128)S(1)} %add_bitcast_fusion.panel_ref, f32[4,512]{1,0:T(4,128)S(1)} %broadcast_in_dim.6.before_ref, bf16[256,4224]{1,0:T(8,128)(2,1)S(1)} %dft.3.rest_0_, bf16[256,4224]{1,0:T(8,128)(2,1)S(1)} %dft.5.rest_1_, ...), custom_call_target="tpu_custom_call" | custom-call | flops 1557135360 | bytes 3041280 | tf_op jit(solution)/shard_map/score/pallas_call | solution.py:285
  48.3 2.5 %score.4.before_ref = f32[4,512]{1,0:T(4,128)S(1)} custom-call(s32[8]{0:T(128)S(1)} %multiply_bitcast_fusion.base_ref, s32[4,512]{1,0:T(4,128)S(1)} %add_bitcast_fusion.panel_ref, f32[4,512]{1,0:T(4,128)S(1)} %score.3.before_ref, bf16[256,4224]{1,0:T(8,128)(2,1)S(1)} %dft.3.rest_0_, bf16[256,4224]{1,0:T(8,128)(2,1)S(1)} %dft.5.rest_1_, ...), custom_call_target="tpu_custom_call" | custom-call | flops 622854144 | bytes 1216512 | tf_op jit(solution)/shard_map/score/pallas_call | solution.py:285
  52.5 1.9 %score.5.rest_0_ = f32[4,512]{1,0:T(4,128)S(1)} custom-call(s32[8]{0:T(128)S(1)} %multiply_bitcast_fusion.base_ref, s32[4,512]{1,0:T(4,128)S(1)} %add_bitcast_fusion.panel_ref, f32[4,512]{1,0:T(4,128)S(1)} %score.4.before_ref, bf16[256,4224]{1,0:T(8,128)(2,1)S(1)} %dft.3.rest_0_, bf16[256,4224]{1,0:T(8,128)(2,1)S(1)} %dft.5.rest_1_, ...), custom_call_target="tpu_custom_call" | custom-call | flops 311427072 | bytes 608256 | tf_op jit(solution)/shard_map/score/pallas_call | solution.py:285
  63.8 2.8 %sums.2 = (f32[72,2176]{1,0:T(8,128)S(1)}, f32[72,2176]{1,0:T(8,128)S(1)}, f32[72,2176]{1,0:T(8,128)S(1)}, f32[72,2176]{1,0:T(8,128)S(1)}, f32[72,2176]{1,0:T(8,...) custom-call(s32[8]{0:T(128)S(1)} %multiply_bitcast_fusion.base_ref, ...), custom_call_target="tpu_custom_call" | custom-call | flops 1868562432 | bytes 7299072 | tf_op jit(solution)/shard_map/sums/pallas_call | solution.py:347
  66.6 3.0 %collective-permute-done.25 = bf16[72,2048]{1,0:T(8,128)(2,1)S(1)} collective-permute-done((bf16[72,2048]{1,0:T(8,128)(2,1)S(1)}, bf16[72,2048]{1,0:T(8,128)(2,1)S(1)}, u32[]{:S(2)}, u32[]{:S(2)}) %collective-permute-start.25) | collective-permute-done | bytes 294944 | tf_op jit(solution)/shard_map/ppermute | solution.py:372
  71.3 5.0 %collective-permute-done.17 = bf16[72,2176]{1,0:T(8,128)(2,1)S(1)} collective-permute-done((bf16[72,2176]{1,0:T(8,128)(2,1)S(1)}, bf16[72,2176]{1,0:T(8,128)(2,1)S(1)}, u32[]{:S(2)}, u32[]{:S(2)}) %collective-permute-start.17) | collective-permute-done | bytes 313376 | tf_op jit(solution)/shard_map/ppermute | solution.py:372
  79.3 3.3 %collective-permute-done.26 = bf16[72,2048]{1,0:T(8,128)(2,1)S(1)} collective-permute-done((bf16[72,2048]{1,0:T(8,128)(2,1)S(1)}, bf16[72,2048]{1,0:T(8,128)(2,1)S(1)}, u32[]{:S(2)}, u32[]{:S(2)}) %collective-permute-start.26) | collective-permute-done | bytes 294944 | tf_op jit(solution)/shard_map/ppermute | solution.py:372
  84.3 2.0 %collective-permute-done.28 = bf16[72,2048]{1,0:T(8,128)(2,1)S(1)} collective-permute-done((bf16[72,2048]{1,0:T(8,128)(2,1)S(1)}, bf16[72,2048]{1,0:T(8,128)(2,1)S(1)}, u32[]{:S(2)}, u32[]{:S(2)}) %collective-permute-start.28) | collective-permute-done | bytes 294944 | tf_op jit(solution)/shard_map/ppermute | solution.py:376
  87.1 2.3 %collective-permute-done.19 = bf16[72,2176]{1,0:T(8,128)(2,1)S(1)} collective-permute-done((bf16[72,2176]{1,0:T(8,128)(2,1)S(1)}, bf16[72,2176]{1,0:T(8,128)(2,1)S(1)}, u32[]{:S(2)}, u32[]{:S(2)}) %collective-permute-start.19) | collective-permute-done | bytes 313376 | tf_op jit(solution)/shard_map/ppermute | solution.py:372
  91.1 2.0 %collective-permute-done.23 = bf16[72,2176]{1,0:T(8,128)(2,1)S(1)} collective-permute-done((bf16[72,2176]{1,0:T(8,128)(2,1)S(1)}, bf16[72,2176]{1,0:T(8,128)(2,1)S(1)}, u32[]{:S(2)}, u32[]{:S(2)}) %collective-permute-start.23) | collective-permute-done | bytes 313376 | tf_op jit(solution)/shard_map/ppermute | solution.py:376
  93.8 8.1 %collective-permute-done.20 = bf16[72,2176]{1,0:T(8,128)(2,1)S(1)} collective-permute-done((bf16[72,2176]{1,0:T(8,128)(2,1)S(1)}, bf16[72,2176]{1,0:T(8,128)(2,1)S(1)}, u32[]{:S(2)}, u32[]{:S(2)}) %collective-permute-start.20) | collective-permute-done | bytes 313376 | tf_op jit(solution)/shard_map/ppermute | solution.py:372
  104.3 7.8 %collective-permute-done.30.rest_5_ = bf16[72,2048]{1,0:T(8,128)(2,1)S(1)} collective-permute-done((bf16[72,2048]{1,0:T(8,128)(2,1)S(1)}, bf16[72,2048]{1,0:T(8,128)(2,1)S(1)}, u32[]{:S(2)}, u32[]{:S(2)}) %collective-permute-start.30) | collective-permute-done | bytes 294944 | tf_op jit(solution)/shard_map/ppermute | solution.py:376
  112.0 1.9 %unfold.1 = f32[72,8192]{1,0:T(8,128)} custom-call(f32[72,2176]{1,0:T(8,128)S(1)} %get-tuple-element.73.rest_0_, bf16[72,2176]{1,0:T(8,128)(2,1)S(1)} %collective-permute-done.21.rest_1_, bf16[72,2176]{1,0:T(8,128)(2,1)S(1)} %collective-permute-done.24.rest_2_, f32[72,2048]{1,0:T(8,128)S(1)} %get-tuple-element.83.rest_3_, ...), custom_call_target="tpu_custom_call" | custom-call | tf_op jit(solution)/shard_map/unfold/pallas_call | solution.py:145
  (96 shorter events, 32.7 us)
Async XLA Ops:
  1.9 13.5 %collective-permute-start = (bf16[72,2176]{1,0:T(8,128)(2,1)S(1)}, bf16[72,2176]{1,0:T(8,128)(2,1)S(1)}, u32[]{:S(2)}, u32[]{:S(2)}) collective-permute-start(bf16[72,2176]{1,0:T(8,128)(2,1)S(1)} %get-tuple-element.48.rest_2_), channel_id=1, source_target_pairs={{0,8},{8,16},{16,24},{24,28},{28,20},{20,12},{12,4},{4,0},{1,9},{9... | collective-permute-start | bytes 940040 | tf_op jit(solution)/shard_map/ppermute | solution.py:372
  4.9 10.4 %collective-permute-start.1 = (bf16[72,2048]{1,0:T(8,128)(2,1)S(1)}, bf16[72,2048]{1,0:T(8,128)(2,1)S(1)}, u32[]{:S(2)}, u32[]{:S(2)}) collective-permute-start(bf16[72,2048]{1,0:T(8,128)(2,1)S(1)} %get-tuple-element.49.rest_5_), channel_id=1, source_target_pairs={{8,0},{16,8},{24,16},{28,24},{20,28},{12,20},{4,12},{0,4},{9,1},{1... | collective-permute-start | bytes 884744 | tf_op jit(solution)/shard_map/ppermute | solution.py:376
  4.9 14.6 %collective-permute-start.4 = (bf16[72,2048]{1,0:T(8,128)(2,1)S(1)}, bf16[72,2048]{1,0:T(8,128)(2,1)}, u32[]{:S(2)}, u32[]{:S(2)}) collective-permute-start(bf16[72,2048]{1,0:T(8,128)(2,1)S(1)} %get-tuple-element.49.rest_5_), channel_id=1, source_target_pairs={{0,8},{8,16},{16,24},{24,28},{28,20},{20,12},{12,4},{4,0},{1,9},{9... | collective-permute-start | bytes 884744 | tf_op jit(solution)/shard_map/ppermute | solution.py:372
  7.0 14.7 %collective-permute-start.5 = (bf16[72,2176]{1,0:T(8,128)(2,1)S(1)}, bf16[72,2176]{1,0:T(8,128)(2,1)}, u32[]{:S(2)}, u32[]{:S(2)}) collective-permute-start(bf16[72,2176]{1,0:T(8,128)(2,1)S(1)} %get-tuple-element.48.rest_2_), channel_id=1, source_target_pairs={{8,0},{16,8},{24,16},{28,24},{20,28},{12,20},{4,12},{0,4},{9,1},{1... | collective-permute-start | bytes 940040 | tf_op jit(solution)/shard_map/ppermute | solution.py:376
  15.4 12.9 %collective-permute-start.2 = (bf16[72,2176]{1,0:T(8,128)(2,1)S(1)}, bf16[72,2176]{1,0:T(8,128)(2,1)}, u32[]{:S(2)}, u32[]{:S(2)}) collective-permute-start(bf16[72,2176]{1,0:T(8,128)(2,1)S(1)} %collective-permute-done.rest_3_), channel_id=1, source_target_pairs={{0,8},{8,16},{16,24},{24,28},{28,20},{20,12},{12,4},{4,0},{1,9},{9... | collective-permute-start | bytes 940040 | tf_op jit(solution)/shard_map/ppermute | solution.py:372
  17.4 10.8 %collective-permute-start.3 = (bf16[72,2048]{1,0:T(8,128)(2,1)S(1)}, bf16[72,2048]{1,0:T(8,128)(2,1)S(1)}, u32[]{:S(2)}, u32[]{:S(2)}) collective-permute-start(bf16[72,2048]{1,0:T(8,128)(2,1)S(1)} %collective-permute-done.1.rest_7_), channel_id=1, source_target_pairs={{8,0},{16,8},{24,16},{28,24},{20,28},{12,20},{4,12},{0,4},{9,1},{1... | collective-permute-start | bytes 884744 | tf_op jit(solution)/shard_map/ppermute | solution.py:376
  21.7 13.0 %collective-permute-start.9 = (bf16[72,2176]{1,0:T(8,128)(2,1)}, bf16[72,2176]{1,0:T(8,128)(2,1)}, u32[]{:S(2)}, u32[]{:S(2)}) collective-permute-start(bf16[72,2176]{1,0:T(8,128)(2,1)} %collective-permute-done.5.rest_4_), channel_id=1, source_target_pairs={{8,0},{16,8},{24,16},{28,24},{20,28},{12,20},{4,12},{0,4},{9,1},{1... | collective-permute-start | bytes 940040 | tf_op jit(solution)/shard_map/ppermute | solution.py:376
  21.7 10.8 %collective-permute-start.8 = (bf16[72,2048]{1,0:T(8,128)(2,1)}, bf16[72,2048]{1,0:T(8,128)(2,1)}, u32[]{:S(2)}, u32[]{:S(2)}) collective-permute-start(bf16[72,2048]{1,0:T(8,128)(2,1)} %collective-permute-done.4.rest_6_), channel_id=1, source_target_pairs={{0,8},{8,16},{16,24},{24,28},{28,20},{20,12},{12,4},{4,0},{1,9},{9... | collective-permute-start | bytes 884744 | tf_op jit(solution)/shard_map/ppermute | solution.py:372
  28.9 12.3 %collective-permute-start.6 = (bf16[72,2176]{1,0:T(8,128)(2,1)}, bf16[72,2176]{1,0:T(8,128)(2,1)}, u32[]{:S(2)}, u32[]{:S(2)}) collective-permute-start(bf16[72,2176]{1,0:T(8,128)(2,1)} %collective-permute-done.2.rest_8_), channel_id=1, source_target_pairs={{0,8},{8,16},{16,24},{24,28},{28,20},{20,12},{12,4},{4,0},{1,9},{9... | collective-permute-start | bytes 940040 | tf_op jit(solution)/shard_map/ppermute | solution.py:372
  30.5 10.7 %collective-permute-start.7 = (bf16[72,2048]{1,0:T(8,128)(2,1)}, bf16[72,2048]{1,0:T(8,128)(2,1)S(1)}, u32[]{:S(2)}, u32[]{:S(2)}) collective-permute-start(bf16[72,2048]{1,0:T(8,128)(2,1)} %copy-done.11), channel_id=1, source_target_pairs={{8,0},{16,8},{24,16},{28,24},{20,28},{12,20},{4,12},{0,4},{9,1},{1... | collective-permute-start | bytes 884744 | tf_op jit(solution)/shard_map/ppermute | solution.py:376
  34.7 13.6 %collective-permute-start.12 = (bf16[72,2048]{1,0:T(8,128)(2,1)}, bf16[72,2048]{1,0:T(8,128)(2,1)S(1)}, u32[]{:S(2)}, u32[]{:S(2)}) collective-permute-start(bf16[72,2048]{1,0:T(8,128)(2,1)} %collective-permute-done.8.rest_10_), channel_id=1, source_target_pairs={{0,8},{8,16},{16,24},{24,28},{28,20},{20,12},{12,4},{4,0},{1,9},{9... | collective-permute-start | bytes 884744 | tf_op jit(solution)/shard_map/ppermute | solution.py:372
  36.3 12.0 %collective-permute-start.13 = (bf16[72,2176]{1,0:T(8,128)(2,1)}, bf16[72,2176]{1,0:T(8,128)(2,1)S(1)}, u32[]{:S(2)}, u32[]{:S(2)}) collective-permute-start(bf16[72,2176]{1,0:T(8,128)(2,1)} %collective-permute-done.9.rest_9_), channel_id=1, source_target_pairs={{8,0},{16,8},{24,16},{28,24},{20,28},{12,20},{4,12},{0,4},{9,1},{1... | collective-permute-start | bytes 940040 | tf_op jit(solution)/shard_map/ppermute | solution.py:376
  41.3 11.2 %collective-permute-start.11 = (bf16[72,2048]{1,0:T(8,128)(2,1)S(1)}, bf16[72,2048]{1,0:T(8,128)(2,1)S(1)}, u32[]{:S(2)}, u32[]{:S(2)}) collective-permute-start(bf16[72,2048]{1,0:T(8,128)(2,1)S(1)} %collective-permute-done.7.rest_5_), channel_id=1, source_target_pairs={{8,0},{16,8},{24,16},{28,24},{20,28},{12,20},{4,12},{0,4},{9,1},{1... | collective-permute-start | bytes 884744 | tf_op jit(solution)/shard_map/ppermute | solution.py:376
  41.3 11.2 %collective-permute-start.10 = (bf16[72,2176]{1,0:T(8,128)(2,1)}, bf16[72,2176]{1,0:T(8,128)(2,1)S(1)}, u32[]{:S(2)}, u32[]{:S(2)}) collective-permute-start(bf16[72,2176]{1,0:T(8,128)(2,1)} %collective-permute-done.6.rest_2_), channel_id=1, source_target_pairs={{0,8},{8,16},{16,24},{24,28},{28,20},{20,12},{12,4},{4,0},{1,9},{9... | collective-permute-start | bytes 940040 | tf_op jit(solution)/shard_map/ppermute | solution.py:372
  61.8 14.5 %collective-permute-start.17 = (bf16[72,2176]{1,0:T(8,128)(2,1)S(1)}, bf16[72,2176]{1,0:T(8,128)(2,1)S(1)}, u32[]{:S(2)}, u32[]{:S(2)}) collective-permute-start(bf16[72,2176]{1,0:T(8,128)(2,1)S(1)} %get-tuple-element.77), channel_id=1, source_target_pairs={{0,8},{8,16},{16,24},{24,28},{28,20},{20,12},{12,4},{4,0},{1,9},{9... | collective-permute-start | bytes 940040 | tf_op jit(solution)/shard_map/ppermute | solution.py:372
  63.4 15.2 %collective-permute-start.22 = (bf16[72,2176]{1,0:T(8,128)(2,1)S(1)}, bf16[72,2176]{1,0:T(8,128)(2,1)S(1)}, u32[]{:S(2)}, u32[]{:S(2)}) collective-permute-start(bf16[72,2176]{1,0:T(8,128)(2,1)S(1)} %get-tuple-element.82), channel_id=1, source_target_pairs={{8,0},{16,8},{24,16},{28,24},{20,28},{12,20},{4,12},{0,4},{9,1},{1... | collective-permute-start | bytes 940040 | tf_op jit(solution)/shard_map/ppermute | solution.py:376
  69.7 13.0 %collective-permute-start.26 = (bf16[72,2048]{1,0:T(8,128)(2,1)S(1)}, bf16[72,2048]{1,0:T(8,128)(2,1)S(1)}, u32[]{:S(2)}, u32[]{:S(2)}) collective-permute-start(bf16[72,2048]{1,0:T(8,128)(2,1)S(1)} %add_convert_fusion.9), channel_id=1, source_target_pairs={{0,8},{8,16},{16,24},{24,28},{28,20},{20,12},{12,4},{4,0},{1,9},{9... | collective-permute-start | bytes 884744 | tf_op jit(solution)/shard_map/ppermute | solution.py:372
  77.1 12.3 %collective-permute-start.19 = (bf16[72,2176]{1,0:T(8,128)(2,1)S(1)}, bf16[72,2176]{1,0:T(8,128)(2,1)S(1)}, u32[]{:S(2)}, u32[]{:S(2)}) collective-permute-start(bf16[72,2176]{1,0:T(8,128)(2,1)S(1)} %add_convert_fusion.4), channel_id=1, source_target_pairs={{0,8},{8,16},{16,24},{24,28},{28,20},{20,12},{12,4},{4,0},{1,9},{9... | collective-permute-start | bytes 940040 | tf_op jit(solution)/shard_map/ppermute | solution.py:372
  78.7 14.4 %collective-permute-start.23 = (bf16[72,2176]{1,0:T(8,128)(2,1)S(1)}, bf16[72,2176]{1,0:T(8,128)(2,1)S(1)}, u32[]{:S(2)}, u32[]{:S(2)}) collective-permute-start(bf16[72,2176]{1,0:T(8,128)(2,1)S(1)} %add_convert_fusion.1), channel_id=1, source_target_pairs={{8,0},{16,8},{24,16},{28,24},{20,28},{12,20},{4,12},{0,4},{9,1},{1... | collective-permute-start | bytes 940040 | tf_op jit(solution)/shard_map/ppermute | solution.py:376
  82.7 21.5 %collective-permute-start.27 = (bf16[72,2048]{1,0:T(8,128)(2,1)S(1)}, bf16[72,2048]{1,0:T(8,128)(2,1)S(1)}, u32[]{:S(2)}, u32[]{:S(2)}) collective-permute-start(bf16[72,2048]{1,0:T(8,128)(2,1)S(1)} %add_convert_fusion.8), channel_id=1, source_target_pairs={{0,8},{8,16},{16,24},{24,28},{28,20},{20,12},{12,4},{4,0},{1,9},{9... | collective-permute-start | bytes 884744 | tf_op jit(solution)/shard_map/ppermute | solution.py:372
  86.5 17.2 %collective-permute-start.29 = (bf16[72,2048]{1,0:T(8,128)(2,1)S(1)}, bf16[72,2048]{1,0:T(8,128)(2,1)S(1)}, u32[]{:S(2)}, u32[]{:S(2)}) collective-permute-start(bf16[72,2048]{1,0:T(8,128)(2,1)S(1)} %add_convert_fusion.6), channel_id=1, source_target_pairs={{8,0},{16,8},{24,16},{28,24},{20,28},{12,20},{4,12},{0,4},{9,1},{1... | collective-permute-start | bytes 884744 | tf_op jit(solution)/shard_map/ppermute | solution.py:376
  89.4 12.5 %collective-permute-start.20 = (bf16[72,2176]{1,0:T(8,128)(2,1)S(1)}, bf16[72,2176]{1,0:T(8,128)(2,1)S(1)}, u32[]{:S(2)}, u32[]{:S(2)}) collective-permute-start(bf16[72,2176]{1,0:T(8,128)(2,1)S(1)} %add_convert_fusion.3), channel_id=1, source_target_pairs={{0,8},{8,16},{16,24},{24,28},{28,20},{20,12},{12,4},{4,0},{1,9},{9... | collective-permute-start | bytes 940040 | tf_op jit(solution)/shard_map/ppermute | solution.py:372
  93.2 11.1 %collective-permute-start.24 = (bf16[72,2176]{1,0:T(8,128)(2,1)S(1)}, bf16[72,2176]{1,0:T(8,128)(2,1)S(1)}, u32[]{:S(2)}, u32[]{:S(2)}) collective-permute-start(bf16[72,2176]{1,0:T(8,128)(2,1)S(1)} %add_convert_fusion), channel_id=1, source_target_pairs={{8,0},{16,8},{24,16},{28,24},{20,28},{12,20},{4,12},{0,4},{9,1},{1... | collective-permute-start | bytes 940040 | tf_op jit(solution)/shard_map/ppermute | solution.py:376
  102.0 10.0 %collective-permute-start.21 = (bf16[72,2176]{1,0:T(8,128)(2,1)S(1)}, bf16[72,2176]{1,0:T(8,128)(2,1)S(1)}, u32[]{:S(2)}, u32[]{:S(2)}) collective-permute-start(bf16[72,2176]{1,0:T(8,128)(2,1)S(1)} %add_convert_fusion.2), channel_id=1, source_target_pairs={{0,8},{8,16},{16,24},{24,28},{28,20},{20,12},{12,4},{4,0},{1,9},{9... | collective-permute-start | bytes 940040 | tf_op jit(solution)/shard_map/ppermute | solution.py:372
  (24 other events, 235.6 us)

commit v4 on v3

--- a/solution.py
+++ b/solution.py
@@ -115,21 +115,26 @@
         chosen, at = (terms[:count], k) if k < CUT else (terms[count:], k - CUT)
         return sum(t[:, group(at)].astype(jnp.float32) for t in chosen)
 
+    twice = jnp.concatenate([mirror, mirror], axis=0)
+
     def flip(v):
         high = v.astype(jnp.bfloat16)
         low = (v - high.astype(jnp.float32)).astype(jnp.bfloat16)
-        return jnp.dot(high, mirror, preferred_element_type=jnp.float32) + jnp.dot(
-            low, mirror, preferred_element_type=jnp.float32
+        return jnp.dot(
+            jnp.concatenate([high, low], axis=1), twice, preferred_element_type=jnp.float32
         )
 
     special = total(HALF)
     out_ref[:, group(0)] = total(0)
     out_ref[:, group(HALF)] = jnp.where(q <= HALF, special, flip(special))
     for k in range(1, HALF):
-        value = total(k)
-        out_ref[:, group(k)] = value
+        if k % chunk == 1:
+            values = [total(n) for n in range(k, min(k + chunk, HALF))]
+            flipped = flip(jnp.concatenate(values, axis=0))
+        at = (k - 1) % chunk
+        out_ref[:, group(k)] = values[at]
         edge = pltpu.roll(special, LANES - (KWIN - k), 1)
-        out_ref[:, group(KWIN - k)] = jnp.where(q == 0, edge, flip(value))
+        out_ref[:, group(KWIN - k)] = jnp.where(q == 0, edge, flipped[at * rows : (at + 1) * rows])
         if (k + 1) % chunk == 0:
             copy(k // chunk).start()
         if k % chunk == 0:
@@ -221,7 +226,7 @@
         out_shape=jax.ShapeDtypeStruct((total, UNIQUE), jnp.bfloat16),
         scratch_shapes=[
             pltpu.VMEM((count // tile, tile, box, box), jnp.bfloat16),
-            pltpu.VMEM((tile * ROW_PAD, box), jnp.float32),
+            pltpu.VMEM(((tile + 1) * ROW_PAD, box), jnp.float32),
             pltpu.VMEM(((HALF + 1) * tile, 2 * box), jnp.bfloat16),
             pltpu.SemaphoreType.DMA((count // tile,)),
         ],
@@ -295,29 +300,24 @@
     )(bases, panel, before, *spectra, *refs)
 
 
-def weight_kernel(*rest):
-    (prior_ref, precision_ref, out_ref), scores = rest[-3:], rest[:-3]
-    total = scores[0][...]
-    for ref in scores[1:]:
+def softmax(score_refs, prior_ref, precision_ref):
+    total = score_refs[0][...]
+    for ref in score_refs[1:]:
         total = total + ref[...]
     value = total * precision_ref[...]
     unscaled = prior_ref[...] * jnp.exp(value - jnp.max(value, axis=0, keepdims=True))
     weight = unscaled / jnp.sum(unscaled, axis=0, keepdims=True)
-    out_ref[...] = weight.astype(jnp.bfloat16).astype(jnp.float32)
-
-
-def weights_of(scores, prior, precision):
-    return pl.pallas_call(
-        weight_kernel,
-        out_shape=jax.ShapeDtypeStruct(prior.shape, jnp.float32),
-        compiler_params=params(),
-        name="weights",
-    )(*scores, prior, precision)
-
-
-def sums_kernel(items, halves, base_ref, weight_ref, panel_ref, *rest):
-    specs, outs = rest[:halves], list(rest[halves:])
+    return weight.astype(jnp.bfloat16).astype(jnp.float32)
+
+
+def sums_kernel(items, halves, count, base_ref, panel_ref, *rest):
+    specs, given, outs = rest[:halves], rest[halves : halves + count], list(rest[halves + count :])
     particles = panel_ref.shape[1]
+    if count == 1:
+        weight_ref = given[0]
+    else:
+        weight_ref = outs.pop(0)
+        weight_ref[...] = softmax(given[:-2], *given[-2:])
     for at, first in items:
         rows, width = outs[0].shape
         row = stacked_rows(at, base_ref, rows, particles)
@@ -342,19 +342,23 @@
 
 def sums(bases, weight, panel, spectra, rows, items, dtype):
     particles = panel.shape[1]
+    given = list(weight) if isinstance(weight, (list, tuple)) else [weight]
     shapes = [(rows, width) for at, _, width in items for _ in at]
     values = sum(a * b for a, b in shapes)
+    out_shape = [jax.ShapeDtypeStruct(shape, dtype) for shape in shapes]
+    if len(given) > 1:
+        out_shape = [jax.ShapeDtypeStruct(panel.shape, jnp.float32)] + out_shape
     return pl.pallas_call(
-        functools.partial(sums_kernel, [(at, first) for at, first, _ in items], len(spectra)),
+        functools.partial(sums_kernel, [(at, first) for at, first, _ in items], len(spectra), len(given)),
         in_specs=[pl.BlockSpec(memory_space=pltpu.SMEM)]
-        + [pl.BlockSpec(memory_space=pltpu.VMEM)] * (2 + len(spectra)),
-        out_shape=[jax.ShapeDtypeStruct(shape, dtype) for shape in shapes],
+        + [pl.BlockSpec(memory_space=pltpu.VMEM)] * (1 + len(spectra) + len(given)),
+        out_shape=out_shape,
         cost_estimate=pl.CostEstimate(
             flops=2 * values * particles, bytes_accessed=4 * values, transcendentals=0
         ),
         compiler_params=params(),
         name="sums",
-    )(bases, weight, panel, *spectra)
+    )(bases, panel, *spectra, *given)
 
 
 RING = (0, 2, 4, 6, 7, 5, 3, 1)
@@ -422,28 +426,39 @@
     picked = score(bases, spectra, panel, picked, [((4,), starts[p], [p4[p]]) for p in range(2)])
 
     turns = [[(c, c ^ n) for c in range(cls_count)] for n in range(1, cls_count)]
-    scores = [picked] + [lax.ppermute(picked, "cls", turn) for turn in turns]
-    weight = weights_of(scores, prior, precision)
+    weight = [picked] + [lax.ppermute(picked, "cls", turn) for turn in turns] + [prior, precision]
 
     narrow, wide = jnp.bfloat16, jnp.float32
-    part = functools.partial(sums, bases, weight, panel, spectra, rows)
     pieces = [(starts[p], WIDTHS[p]) for p in range(2)]
-    far0, back0, far1, ahead1 = part([((4, 5), *pieces[0]), ((4, 3), *pieces[1])], narrow)
-    p = onward(far0), backward(far1)
-    q = onward(ahead1), backward(back0)
-    rest = part([((3, 2, 6, 1, 7, 0), *pieces[0]), ((5, 2, 6, 1, 7, 0), *pieces[1])], wide)
+
+    def part(places, dtype):
+        items = [(at, *piece) for at, piece in zip(zip(*places), pieces)]
+        return sums(bases, weight, panel, spectra, rows, items, dtype)
 
     def pass_on(arrived, held):
         onto = [(h + a.astype(wide)).astype(narrow) for h, a in zip(held, arrived)]
         return onward(onto[0]), backward(onto[1])
 
-    p = tie(*p)
-    p = pass_on(p, (rest[0], rest[6]))
-    q = pass_on(q, (rest[7], rest[2]))
-    p = pass_on(p, (rest[1], rest[8]))
-    q = pass_on(q, (rest[9], rest[4]))
-    p = pass_on(p, (rest[3], rest[10]))
-    return unfold([rest[5], p[0], q[1]], [rest[11], q[0], p[1]])
+    weight, far0, back0, far1, ahead1 = part([(4, 4), (5, 3)], narrow)
+    p = onward(far0), backward(far1)
+    q = onward(ahead1), backward(back0)
+    held = list(part([(3, 5)], wide))
+    *p, weight, held[0], held[1] = tie(*p, weight, *held)
+    p = pass_on(p, held)
+    held = list(part([(6, 2)], wide))
+    *q, weight, held[0], held[1] = tie(*q, weight, *held)
+    q = pass_on(q, held[::-1])
+    held = list(part([(2, 6)], wide))
+    *p, weight, held[0], held[1] = tie(*p, weight, *held)
+    p = pass_on(p, held)
+    held = list(part([(7, 1)], wide))
+    *q, weight, held[0], held[1] = tie(*q, weight, *held)
+    q = pass_on(q, held[::-1])
+    held = list(part([(1, 7)], wide))
+    *p, weight, held[0], held[1] = tie(*p, weight, *held)
+    p = pass_on(p, held)
+    kept = part([(0, 0)], wide)
+    return unfold([kept[0], p[0], q[1]], [kept[1], q[0], p[1]])
 
 
 def by_collectives(images, references, panel, prior, precision):
@@ -462,11 +477,13 @@
     for start in range(0, dp_count, 8):
         picked = score(bases, spectra, panel, picked, items[start : start + 8])
     scores = lax.all_gather(picked, "cls", axis=0, tiled=False)
-    weight = weights_of([scores[n] for n in range(cls_count)], prior, precision)
+    weight = [scores[n] for n in range(cls_count)] + [prior, precision]
     partial = []
     for start in range(0, dp_count, 8):
         items = [((n,), 0, UNIQUE) for n in range(start, min(start + 8, dp_count))]
-        partial += sums(bases, weight, panel, spectra, rows, items, jnp.bfloat16)
+        made = sums(bases, weight, panel, spectra, rows, items, jnp.bfloat16)
+        weight, made = (made[0], made[1:]) if start == 0 else (weight, made)
+        partial += made
     half = lax.psum_scatter(jnp.stack(partial), "dp", scatter_dimension=0, tiled=False)
     return unfold([half[:, : WIDTHS[0]]], [half[:, WIDTHS[0] :]])
 

time: 114 us -> 112 us (0.982)
  waiting for transfers between devices: 45.1 us -> 38.7 us
  Pallas kernels: 31.6 us -> 37.1 us
    ppermute x14, waiting for transfers between devices: 25.3 us -> 8.51 us  [onward(): return lax.ppermute(value, 'dp', list(zip(RING, RING[1:] + RING[:1])))]
    ppermute x14, waiting for transfers between devices: 18 us -> 27.4 us  [backward(): return lax.ppermute(value, 'dp', list(zip(RING[1:] + RING[:1], RING)))]
    pallas_call x2 -> x7, Pallas kernels: 4.16 us -> 9.61 us  [sums(): pl.pallas_call(functools.partial(sums_kernel, [(at, first) for at, first,...]
    unnamed x34 -> x30, local copies, waits for them, and re-layouts: 2.95 us -> 2.26 us
  transfers between devices with their start and end apart: 31 -> 31, of which waited for: 16 -> 17; matrix products, arithmetic and copies ran while one was open for 1% -> 1% of each run, Pallas kernels for 23% -> 28%
where the time goes in v4:
time: 112 us
  waiting for transfers between devices  38.7 us (35%)
  Pallas kernels  37.1 us (33%)
  starting transfers between devices  32.3 us (29%)
  local copies, waits for them, and re-layouts  2.26 us (2%)
  other arithmetic  1.31 us (1%)
    ppermute x14, waiting for transfers between devices, backward(): return lax.ppermute(value, 'dp', list(zip(RING[1:] + RING[:1], RING)))  27.4 us
    ppermute x14, starting transfers between devices, onward(): return lax.ppermute(value, 'dp', list(zip(RING, RING[1:] + RING[:1])))  25.4 us
    pallas_call x3, Pallas kernels, dft(): pl.pallas_call(functools.partial(dft_kernel, tile, first), in_specs=[pl.B...  16.3 us
    pallas_call x7, Pallas kernels, sums(): pl.pallas_call(functools.partial(sums_kernel, [(at, first) for at, first,...  9.61 us
    pallas_call x3, Pallas kernels, score(): pl.pallas_call(functools.partial(score_kernel, shapes, len(spectra)), in_...  8.73 us
    ppermute x14, waiting for transfers between devices, onward(): return lax.ppermute(value, 'dp', list(zip(RING, RING[1:] + RING[:1])))  8.51 us
    ppermute x14, starting transfers between devices, backward(): return lax.ppermute(value, 'dp', list(zip(RING[1:] + RING[:1], RING)))  4.97 us
    ppermute x3, waiting for transfers between devices, by_ring(): lax.ppermute(picked, 'cls', turn)  2.8 us
  transfers between devices with their start and end apart: 31, of which 17 were waited for; matrix products, arithmetic and copies ran while one was open for 1% of the time, Pallas kernels for 28%

profile of v4, /device:TPU:0, one launch (start us, length us, event | category | flops | bytes accessed | tf_op | source)
XLA Modules:
  0.0 112.2 jit_solution(7730298864100328151)
XLA Ops:
  1.9 3.1 %collective-permute-start = (bf16[72,2176]{1,0:T(8,128)(2,1)S(1)}, bf16[72,2176]{1,0:T(8,128)(2,1)S(1)}, u32[]{:S(2)}, u32[]{:S(2)}) collective-permute-start(bf16[72,2176]{1,0:T(8,128)(2,1)S(1)} %get-tuple-element.72.rest_2_), channel_id=1, source_target_pairs={{0,8},{8,16},{16,24},{24,28},{28,20},{20,12},{12,4},{4,0},{1,9},{9... | collective-permute-start | bytes 940040 | tf_op jit(solution)/shard_map/ppermute | solution.py:376
  4.9 2.0 %collective-permute-start.4 = (bf16[72,2048]{1,0:T(8,128)(2,1)S(1)}, bf16[72,2048]{1,0:T(8,128)(2,1)}, u32[]{:S(2)}, u32[]{:S(2)}) collective-permute-start(bf16[72,2048]{1,0:T(8,128)(2,1)S(1)} %get-tuple-element.73.rest_5_), channel_id=1, source_target_pairs={{0,8},{8,16},{16,24},{24,28},{28,20},{20,12},{12,4},{4,0},{1,9},{9... | collective-permute-start | bytes 884744 | tf_op jit(solution)/shard_map/ppermute | solution.py:376
  7.9 7.4 %dft.3.rest_0_ = bf16[256,4224]{1,0:T(8,128)(2,1)S(1)} custom-call(bf16[328,256]{1,0:T(8,128)(2,1)S(1)} %copy-done, bf16[512,128,128]{2,1,0:T(8,128)(2,1)} %img_ref.5), custom_call_target="tpu_custom_call" | custom-call | flops 1711276032 | bytes 10551296 | tf_op jit(solution)/shard_map/dft/pallas_call | solution.py:222
  15.4 2.1 %collective-permute-start.2 = (bf16[72,2176]{1,0:T(8,128)(2,1)S(1)}, bf16[72,2176]{1,0:T(8,128)(2,1)}, u32[]{:S(2)}, u32[]{:S(2)}) collective-permute-start(bf16[72,2176]{1,0:T(8,128)(2,1)S(1)} %collective-permute-done.rest_3_), channel_id=1, source_target_pairs={{0,8},{8,16},{16,24},{24,28},{28,20},{20,12},{12,4},{4,0},{1,9},{9... | collective-permute-start | bytes 940040 | tf_op jit(solution)/shard_map/ppermute | solution.py:376
  17.4 2.1 %collective-permute-done.4.rest_6_ = bf16[72,2048]{1,0:T(8,128)(2,1)} collective-permute-done((bf16[72,2048]{1,0:T(8,128)(2,1)S(1)}, bf16[72,2048]{1,0:T(8,128)(2,1)}, u32[]{:S(2)}, u32[]{:S(2)}) %collective-permute-start.4) | collective-permute-done | bytes 294944 | tf_op jit(solution)/shard_map/ppermute | solution.py:376
  19.5 2.2 %collective-permute-done.5.rest_4_ = bf16[72,2176]{1,0:T(8,128)(2,1)} collective-permute-done((bf16[72,2176]{1,0:T(8,128)(2,1)S(1)}, bf16[72,2176]{1,0:T(8,128)(2,1)}, u32[]{:S(2)}, u32[]{:S(2)}) %collective-permute-start.5) | collective-permute-done | bytes 313376 | tf_op jit(solution)/shard_map/ppermute | solution.py:380
  21.7 2.0 %collective-permute-start.8 = (bf16[72,2048]{1,0:T(8,128)(2,1)}, bf16[72,2048]{1,0:T(8,128)(2,1)}, u32[]{:S(2)}, u32[]{:S(2)}) collective-permute-start(bf16[72,2048]{1,0:T(8,128)(2,1)} %collective-permute-done.4.rest_6_), channel_id=1, source_target_pairs={{0,8},{8,16},{16,24},{24,28},{28,20},{20,12},{12,4},{4,0},{1,9},{9... | collective-permute-start | bytes 884744 | tf_op jit(solution)/shard_map/ppermute | solution.py:376
  23.7 4.5 %dft.4.rest_0_ = bf16[128,4224]{1,0:T(8,128)(2,1)S(1)} custom-call(bf16[328,256]{1,0:T(8,128)(2,1)S(1)} %copy-done, bf16[512,128,128]{2,1,0:T(8,128)(2,1)} %img_ref.5), custom_call_target="tpu_custom_call" | custom-call | flops 855638016 | bytes 5275648 | tf_op jit(solution)/shard_map/dft/pallas_call | solution.py:222
  28.2 1.6 %collective-permute-start.6 = (bf16[72,2176]{1,0:T(8,128)(2,1)}, bf16[72,2176]{1,0:T(8,128)(2,1)}, u32[]{:S(2)}, u32[]{:S(2)}) collective-permute-start(bf16[72,2176]{1,0:T(8,128)(2,1)} %collective-permute-done.2.rest_8_), channel_id=1, source_target_pairs={{0,8},{8,16},{16,24},{24,28},{28,20},{20,12},{12,4},{4,0},{1,9},{9... | collective-permute-start | bytes 940040 | tf_op jit(solution)/shard_map/ppermute | solution.py:376
  30.4 2.2 %collective-permute-done.8.rest_10_ = bf16[72,2048]{1,0:T(8,128)(2,1)} collective-permute-done((bf16[72,2048]{1,0:T(8,128)(2,1)}, bf16[72,2048]{1,0:T(8,128)(2,1)}, u32[]{:S(2)}, u32[]{:S(2)}) %collective-permute-start.8) | collective-permute-done | bytes 294944 | tf_op jit(solution)/shard_map/ppermute | solution.py:376
  32.5 2.2 %collective-permute-done.9.rest_9_ = bf16[72,2176]{1,0:T(8,128)(2,1)} collective-permute-done((bf16[72,2176]{1,0:T(8,128)(2,1)}, bf16[72,2176]{1,0:T(8,128)(2,1)}, u32[]{:S(2)}, u32[]{:S(2)}) %collective-permute-start.9) | collective-permute-done | bytes 313376 | tf_op jit(solution)/shard_map/ppermute | solution.py:380
  36.8 4.5 %dft.5.rest_1_ = bf16[256,4224]{1,0:T(8,128)(2,1)S(1)} custom-call(bf16[328,256]{1,0:T(8,128)(2,1)S(1)} %copy-done.1, bf16[512,128,128]{2,1,0:T(8,128)(2,1)} %img_ref.5, bf16[128,4224]{1,0:T(8,128)(2,1)S(1)} %dft.4.rest_0_), custom_call_target="tpu_custom_call" | custom-call | flops 855638016 | bytes 5275648 | tf_op jit(solution)/shard_map/dft/pallas_call | solution.py:222
  44.1 4.3 %score.3.before_ref = f32[4,512]{1,0:T(4,128)S(1)} custom-call(s32[8]{0:T(128)S(1)} %multiply_bitcast_fusion.base_ref, s32[4,512]{1,0:T(4,128)S(1)} %add_bitcast_fusion.panel_ref, f32[4,512]{1,0:T(4,128)S(1)} %broadcast_in_dim.6.before_ref, bf16[256,4224]{1,0:T(8,128)(2,1)S(1)} %dft.3.rest_0_, bf16[256,4224]{1,0:T(8,128)(2,1)S(1)} %dft.5.rest_1_, ...), custom_call_target="tpu_custom_call" | custom-call | flops 1557135360 | bytes 3041280 | tf_op jit(solution)/shard_map/score/pallas_call | solution.py:290
  48.4 2.5 %score.4.before_ref = f32[4,512]{1,0:T(4,128)S(1)} custom-call(s32[8]{0:T(128)S(1)} %multiply_bitcast_fusion.base_ref, s32[4,512]{1,0:T(4,128)S(1)} %add_bitcast_fusion.panel_ref, f32[4,512]{1,0:T(4,128)S(1)} %score.3.before_ref, bf16[256,4224]{1,0:T(8,128)(2,1)S(1)} %dft.3.rest_0_, bf16[256,4224]{1,0:T(8,128)(2,1)S(1)} %dft.5.rest_1_, ...), custom_call_target="tpu_custom_call" | custom-call | flops 622854144 | bytes 1216512 | tf_op jit(solution)/shard_map/score/pallas_call | solution.py:290
  52.5 1.9 %score.5.rest_2_ = f32[4,512]{1,0:T(4,128)S(1)} custom-call(s32[8]{0:T(128)S(1)} %multiply_bitcast_fusion.base_ref, s32[4,512]{1,0:T(4,128)S(1)} %add_bitcast_fusion.panel_ref, f32[4,512]{1,0:T(4,128)S(1)} %score.4.before_ref, bf16[256,4224]{1,0:T(8,128)(2,1)S(1)} %dft.3.rest_0_, bf16[256,4224]{1,0:T(8,128)(2,1)S(1)} %dft.5.rest_1_, ...), custom_call_target="tpu_custom_call" | custom-call | flops 311427072 | bytes 608256 | tf_op jit(solution)/shard_map/score/pallas_call | solution.py:290
  56.4 1.9 %collective-permute-done.15.rest_4_ = f32[4,512]{1,0:T(4,128)S(1)} collective-permute-done((f32[4,512]{1,0:T(4,128)S(1)}, f32[4,512]{1,0:T(4,128)S(1)}, u32[]{:S(2)}, u32[]{:S(2)}) %collective-permute-start.15) | collective-permute-done | bytes 8224 | tf_op jit(solution)/shard_map/ppermute | solution.py:429
  60.6 1.6 %collective-permute-start.17 = (bf16[72,2176]{1,0:T(8,128)(2,1)S(1)}, bf16[72,2176]{1,0:T(8,128)(2,1)S(1)}, u32[]{:S(2)}, u32[]{:S(2)}) collective-permute-start(bf16[72,2176]{1,0:T(8,128)(2,1)S(1)} %get-tuple-element.97), channel_id=1, source_target_pairs={{0,8},{8,16},{16,24},{24,28},{28,20},{20,12},{12,4},{4,0},{1,9},{9... | collective-permute-start | bytes 940040 | tf_op jit(solution)/shard_map/ppermute | solution.py:376
  66.1 6.0 %collective-permute-done.18 = bf16[72,2048]{1,0:T(8,128)(2,1)S(1)} collective-permute-done((bf16[72,2048]{1,0:T(8,128)(2,1)S(1)}, bf16[72,2048]{1,0:T(8,128)(2,1)S(1)}, u32[]{:S(2)}, u32[]{:S(2)}) %collective-permute-start.18) | collective-permute-done | bytes 294944 | tf_op jit(solution)/shard_map/ppermute | solution.py:380
  82.5 2.7 %collective-permute-done.20 = bf16[72,2048]{1,0:T(8,128)(2,1)S(1)} collective-permute-done((bf16[72,2048]{1,0:T(8,128)(2,1)S(1)}, bf16[72,2048]{1,0:T(8,128)(2,1)S(1)}, u32[]{:S(2)}, u32[]{:S(2)}) %collective-permute-start.20) | collective-permute-done | bytes 294944 | tf_op jit(solution)/shard_map/ppermute | solution.py:380
  92.6 1.6 %collective-permute-start.29 = (bf16[72,2048]{1,0:T(8,128)(2,1)S(1)}, bf16[72,2048]{1,0:T(8,128)(2,1)S(1)}, u32[]{:S(2)}, u32[]{:S(2)}) collective-permute-start(bf16[72,2048]{1,0:T(8,128)(2,1)S(1)} %add_convert_fusion.6), channel_id=1, source_target_pairs={{0,8},{8,16},{16,24},{24,28},{28,20},{20,12},{12,4},{4,0},{1,9},{9... | collective-permute-start | bytes 884744 | tf_op jit(solution)/shard_map/ppermute | solution.py:376
  95.5 2.7 %collective-permute-done.24 = bf16[72,2048]{1,0:T(8,128)(2,1)S(1)} collective-permute-done((bf16[72,2048]{1,0:T(8,128)(2,1)S(1)}, bf16[72,2048]{1,0:T(8,128)(2,1)S(1)}, u32[]{:S(2)}, u32[]{:S(2)}) %collective-permute-start.24) | collective-permute-done | bytes 294944 | tf_op jit(solution)/shard_map/ppermute | solution.py:380
  98.3 1.6 %collective-permute-start.27 = (bf16[72,2176]{1,0:T(8,128)(2,1)S(1)}, bf16[72,2176]{1,0:T(8,128)(2,1)S(1)}, u32[]{:S(2)}, u32[]{:S(2)}) collective-permute-start(bf16[72,2176]{1,0:T(8,128)(2,1)S(1)} %add_convert_fusion.1), channel_id=1, source_target_pairs={{0,8},{8,16},{16,24},{24,28},{28,20},{20,12},{12,4},{4,0},{1,9},{9... | collective-permute-start | bytes 940040 | tf_op jit(solution)/shard_map/ppermute | solution.py:376
  104.9 5.2 %collective-permute-done.30.rest_5_ = bf16[72,2048]{1,0:T(8,128)(2,1)S(1)} collective-permute-done((bf16[72,2048]{1,0:T(8,128)(2,1)S(1)}, bf16[72,2048]{1,0:T(8,128)(2,1)S(1)}, u32[]{:S(2)}, u32[]{:S(2)}) %collective-permute-start.30) | collective-permute-done | bytes 294944 | tf_op jit(solution)/shard_map/ppermute | solution.py:380
  110.2 1.8 %unfold.1 = f32[72,8192]{1,0:T(8,128)} custom-call(f32[72,2176]{1,0:T(8,128)S(1)} %get-tuple-element.129.rest_0_, bf16[72,2176]{1,0:T(8,128)(2,1)S(1)} %collective-permute-done.27.rest_1_, bf16[72,2176]{1,0:T(8,128)(2,1)S(1)} %collective-permute-done.28.rest_2_, f32[72,2048]{1,0:T(8,128)S(1)} %get-tuple-element.134.rest_3_, ...), custom_call_target="tpu_custom_call" | custom-call | tf_op jit(solution)/shard_map/unfold/pallas_call | solution.py:150
  (96 shorter events, 41.9 us)
Async XLA Ops:
  1.9 13.5 %collective-permute-start = (bf16[72,2176]{1,0:T(8,128)(2,1)S(1)}, bf16[72,2176]{1,0:T(8,128)(2,1)S(1)}, u32[]{:S(2)}, u32[]{:S(2)}) collective-permute-start(bf16[72,2176]{1,0:T(8,128)(2,1)S(1)} %get-tuple-element.72.rest_2_), channel_id=1, source_target_pairs={{0,8},{8,16},{16,24},{24,28},{28,20},{20,12},{12,4},{4,0},{1,9},{9... | collective-permute-start | bytes 940040 | tf_op jit(solution)/shard_map/ppermute | solution.py:376
  4.9 14.6 %collective-permute-start.4 = (bf16[72,2048]{1,0:T(8,128)(2,1)S(1)}, bf16[72,2048]{1,0:T(8,128)(2,1)}, u32[]{:S(2)}, u32[]{:S(2)}) collective-permute-start(bf16[72,2048]{1,0:T(8,128)(2,1)S(1)} %get-tuple-element.73.rest_5_), channel_id=1, source_target_pairs={{0,8},{8,16},{16,24},{24,28},{28,20},{20,12},{12,4},{4,0},{1,9},{9... | collective-permute-start | bytes 884744 | tf_op jit(solution)/shard_map/ppermute | solution.py:376
  7.0 14.7 %collective-permute-start.5 = (bf16[72,2176]{1,0:T(8,128)(2,1)S(1)}, bf16[72,2176]{1,0:T(8,128)(2,1)}, u32[]{:S(2)}, u32[]{:S(2)}) collective-permute-start(bf16[72,2176]{1,0:T(8,128)(2,1)S(1)} %get-tuple-element.72.rest_2_), channel_id=1, source_target_pairs={{8,0},{16,8},{24,16},{28,24},{20,28},{12,20},{4,12},{0,4},{9,1},{1... | collective-permute-start | bytes 940040 | tf_op jit(solution)/shard_map/ppermute | solution.py:380
  15.4 12.9 %collective-permute-start.2 = (bf16[72,2176]{1,0:T(8,128)(2,1)S(1)}, bf16[72,2176]{1,0:T(8,128)(2,1)}, u32[]{:S(2)}, u32[]{:S(2)}) collective-permute-start(bf16[72,2176]{1,0:T(8,128)(2,1)S(1)} %collective-permute-done.rest_3_), channel_id=1, source_target_pairs={{0,8},{8,16},{16,24},{24,28},{28,20},{20,12},{12,4},{4,0},{1,9},{9... | collective-permute-start | bytes 940040 | tf_op jit(solution)/shard_map/ppermute | solution.py:376
  17.4 10.8 %collective-permute-start.3 = (bf16[72,2048]{1,0:T(8,128)(2,1)S(1)}, bf16[72,2048]{1,0:T(8,128)(2,1)}, u32[]{:S(2)}, u32[]{:S(2)}) collective-permute-start(bf16[72,2048]{1,0:T(8,128)(2,1)S(1)} %collective-permute-done.1.rest_7_), channel_id=1, source_target_pairs={{8,0},{16,8},{24,16},{28,24},{20,28},{12,20},{4,12},{0,4},{9,1},{1... | collective-permute-start | bytes 884744 | tf_op jit(solution)/shard_map/ppermute | solution.py:380
  21.7 13.0 %collective-permute-start.9 = (bf16[72,2176]{1,0:T(8,128)(2,1)}, bf16[72,2176]{1,0:T(8,128)(2,1)}, u32[]{:S(2)}, u32[]{:S(2)}) collective-permute-start(bf16[72,2176]{1,0:T(8,128)(2,1)} %collective-permute-done.5.rest_4_), channel_id=1, source_target_pairs={{8,0},{16,8},{24,16},{28,24},{20,28},{12,20},{4,12},{0,4},{9,1},{1... | collective-permute-start | bytes 940040 | tf_op jit(solution)/shard_map/ppermute | solution.py:380
  21.7 10.8 %collective-permute-start.8 = (bf16[72,2048]{1,0:T(8,128)(2,1)}, bf16[72,2048]{1,0:T(8,128)(2,1)}, u32[]{:S(2)}, u32[]{:S(2)}) collective-permute-start(bf16[72,2048]{1,0:T(8,128)(2,1)} %collective-permute-done.4.rest_6_), channel_id=1, source_target_pairs={{0,8},{8,16},{16,24},{24,28},{28,20},{20,12},{12,4},{4,0},{1,9},{9... | collective-permute-start | bytes 884744 | tf_op jit(solution)/shard_map/ppermute | solution.py:376
  28.2 13.0 %collective-permute-start.6 = (bf16[72,2176]{1,0:T(8,128)(2,1)}, bf16[72,2176]{1,0:T(8,128)(2,1)}, u32[]{:S(2)}, u32[]{:S(2)}) collective-permute-start(bf16[72,2176]{1,0:T(8,128)(2,1)} %collective-permute-done.2.rest_8_), channel_id=1, source_target_pairs={{0,8},{8,16},{16,24},{24,28},{28,20},{20,12},{12,4},{4,0},{1,9},{9... | collective-permute-start | bytes 940040 | tf_op jit(solution)/shard_map/ppermute | solution.py:376
  29.9 11.4 %collective-permute-start.7 = (bf16[72,2048]{1,0:T(8,128)(2,1)}, bf16[72,2048]{1,0:T(8,128)(2,1)S(1)}, u32[]{:S(2)}, u32[]{:S(2)}) collective-permute-start(bf16[72,2048]{1,0:T(8,128)(2,1)} %collective-permute-done.3.rest_11_), channel_id=1, source_target_pairs={{8,0},{16,8},{24,16},{28,24},{20,28},{12,20},{4,12},{0,4},{9,1},{1... | collective-permute-start | bytes 884744 | tf_op jit(solution)/shard_map/ppermute | solution.py:380
  34.7 13.6 %collective-permute-start.12 = (bf16[72,2048]{1,0:T(8,128)(2,1)}, bf16[72,2048]{1,0:T(8,128)(2,1)S(1)}, u32[]{:S(2)}, u32[]{:S(2)}) collective-permute-start(bf16[72,2048]{1,0:T(8,128)(2,1)} %collective-permute-done.8.rest_10_), channel_id=1, source_target_pairs={{0,8},{8,16},{16,24},{24,28},{28,20},{20,12},{12,4},{4,0},{1,9},{9... | collective-permute-start | bytes 884744 | tf_op jit(solution)/shard_map/ppermute | solution.py:376
  36.3 12.1 %collective-permute-start.13 = (bf16[72,2176]{1,0:T(8,128)(2,1)}, bf16[72,2176]{1,0:T(8,128)(2,1)S(1)}, u32[]{:S(2)}, u32[]{:S(2)}) collective-permute-start(bf16[72,2176]{1,0:T(8,128)(2,1)} %collective-permute-done.9.rest_9_), channel_id=1, source_target_pairs={{8,0},{16,8},{24,16},{28,24},{20,28},{12,20},{4,12},{0,4},{9,1},{1... | collective-permute-start | bytes 940040 | tf_op jit(solution)/shard_map/ppermute | solution.py:380
  41.3 11.2 %collective-permute-start.10 = (bf16[72,2176]{1,0:T(8,128)(2,1)}, bf16[72,2176]{1,0:T(8,128)(2,1)S(1)}, u32[]{:S(2)}, u32[]{:S(2)}) collective-permute-start(bf16[72,2176]{1,0:T(8,128)(2,1)} %collective-permute-done.6.rest_2_), channel_id=1, source_target_pairs={{0,8},{8,16},{16,24},{24,28},{28,20},{20,12},{12,4},{4,0},{1,9},{9... | collective-permute-start | bytes 940040 | tf_op jit(solution)/shard_map/ppermute | solution.py:376
  60.6 11.5 %collective-permute-start.17 = (bf16[72,2176]{1,0:T(8,128)(2,1)S(1)}, bf16[72,2176]{1,0:T(8,128)(2,1)S(1)}, u32[]{:S(2)}, u32[]{:S(2)}) collective-permute-start(bf16[72,2176]{1,0:T(8,128)(2,1)S(1)} %get-tuple-element.97), channel_id=1, source_target_pairs={{0,8},{8,16},{16,24},{24,28},{28,20},{20,12},{12,4},{4,0},{1,9},{9... | collective-permute-start | bytes 940040 | tf_op jit(solution)/shard_map/ppermute | solution.py:376
  62.7 14.5 %collective-permute-start.21 = (bf16[72,2048]{1,0:T(8,128)(2,1)S(1)}, bf16[72,2048]{1,0:T(8,128)(2,1)S(1)}, u32[]{:S(2)}, u32[]{:S(2)}) collective-permute-start(bf16[72,2048]{1,0:T(8,128)(2,1)S(1)} %get-tuple-element.106), channel_id=1, source_target_pairs={{0,8},{8,16},{16,24},{24,28},{28,20},{20,12},{12,4},{4,0},{1,9},{9... | collective-permute-start | bytes 884744 | tf_op jit(solution)/shard_map/ppermute | solution.py:376
  64.3 14.6 %collective-permute-start.22 = (bf16[72,2176]{1,0:T(8,128)(2,1)S(1)}, bf16[72,2176]{1,0:T(8,128)(2,1)S(1)}, u32[]{:S(2)}, u32[]{:S(2)}) collective-permute-start(bf16[72,2176]{1,0:T(8,128)(2,1)S(1)} %get-tuple-element.107), channel_id=1, source_target_pairs={{8,0},{16,8},{24,16},{28,24},{20,28},{12,20},{4,12},{0,4},{9,1},{1... | collective-permute-start | bytes 940040 | tf_op jit(solution)/shard_map/ppermute | solution.py:380
  72.2 13.0 %collective-permute-start.19 = (bf16[72,2176]{1,0:T(8,128)(2,1)S(1)}, bf16[72,2176]{1,0:T(8,128)(2,1)S(1)}, u32[]{:S(2)}, u32[]{:S(2)}) collective-permute-start(bf16[72,2176]{1,0:T(8,128)(2,1)S(1)} %add_convert_fusion.4), channel_id=1, source_target_pairs={{0,8},{8,16},{16,24},{24,28},{28,20},{20,12},{12,4},{4,0},{1,9},{9... | collective-permute-start | bytes 940040 | tf_op jit(solution)/shard_map/ppermute | solution.py:376
  73.9 11.3 %collective-permute-start.20 = (bf16[72,2048]{1,0:T(8,128)(2,1)S(1)}, bf16[72,2048]{1,0:T(8,128)(2,1)S(1)}, u32[]{:S(2)}, u32[]{:S(2)}) collective-permute-start(bf16[72,2048]{1,0:T(8,128)(2,1)S(1)} %add_convert_fusion.9), channel_id=1, source_target_pairs={{8,0},{16,8},{24,16},{28,24},{20,28},{12,20},{4,12},{0,4},{9,1},{1... | collective-permute-start | bytes 884744 | tf_op jit(solution)/shard_map/ppermute | solution.py:380
  78.9 11.4 %collective-permute-start.25 = (bf16[72,2048]{1,0:T(8,128)(2,1)S(1)}, bf16[72,2048]{1,0:T(8,128)(2,1)S(1)}, u32[]{:S(2)}, u32[]{:S(2)}) collective-permute-start(bf16[72,2048]{1,0:T(8,128)(2,1)S(1)} %add_convert_fusion.7), channel_id=1, source_target_pairs={{0,8},{8,16},{16,24},{24,28},{28,20},{20,12},{12,4},{4,0},{1,9},{9... | collective-permute-start | bytes 884744 | tf_op jit(solution)/shard_map/ppermute | solution.py:376
  80.6 11.3 %collective-permute-start.26 = (bf16[72,2176]{1,0:T(8,128)(2,1)S(1)}, bf16[72,2176]{1,0:T(8,128)(2,1)S(1)}, u32[]{:S(2)}, u32[]{:S(2)}) collective-permute-start(bf16[72,2176]{1,0:T(8,128)(2,1)S(1)} %add_convert_fusion.2), channel_id=1, source_target_pairs={{8,0},{16,8},{24,16},{28,24},{20,28},{12,20},{4,12},{0,4},{9,1},{1... | collective-permute-start | bytes 940040 | tf_op jit(solution)/shard_map/ppermute | solution.py:380
  85.3 13.0 %collective-permute-start.23 = (bf16[72,2176]{1,0:T(8,128)(2,1)S(1)}, bf16[72,2176]{1,0:T(8,128)(2,1)S(1)}, u32[]{:S(2)}, u32[]{:S(2)}) collective-permute-start(bf16[72,2176]{1,0:T(8,128)(2,1)S(1)} %add_convert_fusion.3), channel_id=1, source_target_pairs={{0,8},{8,16},{16,24},{24,28},{28,20},{20,12},{12,4},{4,0},{1,9},{9... | collective-permute-start | bytes 940040 | tf_op jit(solution)/shard_map/ppermute | solution.py:376
  87.0 11.3 %collective-permute-start.24 = (bf16[72,2048]{1,0:T(8,128)(2,1)S(1)}, bf16[72,2048]{1,0:T(8,128)(2,1)S(1)}, u32[]{:S(2)}, u32[]{:S(2)}) collective-permute-start(bf16[72,2048]{1,0:T(8,128)(2,1)S(1)} %add_convert_fusion.8), channel_id=1, source_target_pairs={{8,0},{16,8},{24,16},{28,24},{20,28},{12,20},{4,12},{0,4},{9,1},{1... | collective-permute-start | bytes 884744 | tf_op jit(solution)/shard_map/ppermute | solution.py:380
  92.0 13.0 %collective-permute-start.28 = (bf16[72,2176]{1,0:T(8,128)(2,1)S(1)}, bf16[72,2176]{1,0:T(8,128)(2,1)S(1)}, u32[]{:S(2)}, u32[]{:S(2)}) collective-permute-start(bf16[72,2176]{1,0:T(8,128)(2,1)S(1)} %add_convert_fusion), channel_id=1, source_target_pairs={{8,0},{16,8},{24,16},{28,24},{20,28},{12,20},{4,12},{0,4},{9,1},{1... | collective-permute-start | bytes 940040 | tf_op jit(solution)/shard_map/ppermute | solution.py:380
  92.6 10.8 %collective-permute-start.29 = (bf16[72,2048]{1,0:T(8,128)(2,1)S(1)}, bf16[72,2048]{1,0:T(8,128)(2,1)S(1)}, u32[]{:S(2)}, u32[]{:S(2)}) collective-permute-start(bf16[72,2048]{1,0:T(8,128)(2,1)S(1)} %add_convert_fusion.6), channel_id=1, source_target_pairs={{0,8},{8,16},{16,24},{24,28},{28,20},{20,12},{12,4},{4,0},{1,9},{9... | collective-permute-start | bytes 884744 | tf_op jit(solution)/shard_map/ppermute | solution.py:376
  98.3 11.9 %collective-permute-start.27 = (bf16[72,2176]{1,0:T(8,128)(2,1)S(1)}, bf16[72,2176]{1,0:T(8,128)(2,1)S(1)}, u32[]{:S(2)}, u32[]{:S(2)}) collective-permute-start(bf16[72,2176]{1,0:T(8,128)(2,1)S(1)} %add_convert_fusion.1), channel_id=1, source_target_pairs={{0,8},{8,16},{16,24},{24,28},{28,20},{20,12},{12,4},{4,0},{1,9},{9... | collective-permute-start | bytes 940040 | tf_op jit(solution)/shard_map/ppermute | solution.py:376
  (22 other events, 226.6 us)

commit v5 on v4

--- a/solution.py
+++ b/solution.py
@@ -422,10 +422,11 @@
     *q3, picked = tie(*q3, picked)
     middle = [((5, 3), starts[0], [p3[0], q3[1]]), ((5, 3), starts[1], [q3[0], p3[1]])]
     picked = score(bases, spectra, panel, picked, middle)
-    *p4, picked = tie(*p4, picked)
-    picked = score(bases, spectra, panel, picked, [((4,), starts[p], [p4[p]]) for p in range(2)])
-
-    turns = [[(c, c ^ n) for c in range(cls_count)] for n in range(1, cls_count)]
+    for piece in range(2):
+        arrived, picked = tie(p4[piece], picked)
+        picked = score(bases, spectra, panel, picked, [((4,), starts[piece], [arrived])])
+
+    turns = [[(c, c ^ n) for c in range(cls_count)] for n in range(cls_count - 1, 0, -1)]
     weight = [picked] + [lax.ppermute(picked, "cls", turn) for turn in turns] + [prior, precision]
 
     narrow, wide = jnp.bfloat16, jnp.float32

time: 112 us -> 112 us (level)
  waiting for transfers between devices: 38.7 us -> 37.1 us
    ppermute x14, waiting for transfers between devices: 27.4 us -> 26.2 us  [backward(): return lax.ppermute(value, 'dp', list(zip(RING[1:] + RING[:1], RING)))]
    pallas_call x3 -> x4, Pallas kernels: 8.73 us -> 9.54 us  [score(): pl.pallas_call(functools.partial(score_kernel, shapes, len(spectra)), in_...]
  transfers between devices with their start and end apart: 31 -> 31, of which waited for: 17 -> 17; matrix products, arithmetic and copies ran while one was open for 1% -> 1% of each run, Pallas kernels for 28% -> 29%
where the time goes in v5:
time: 112 us; the launch traced here: 111 us
  Pallas kernels  37.9 us (34%)
  waiting for transfers between devices  37.1 us (33%)
  starting transfers between devices  32.3 us (29%)
  local copies, waits for them, and re-layouts  2.26 us (2%)
  other arithmetic  1.31 us (1%)
    ppermute x14, waiting for transfers between devices, backward(): return lax.ppermute(value, 'dp', list(zip(RING[1:] + RING[:1], RING)))  26.2 us
    ppermute x14, starting transfers between devices, onward(): return lax.ppermute(value, 'dp', list(zip(RING, RING[1:] + RING[:1])))  25.9 us
    pallas_call x3, Pallas kernels, dft(): pl.pallas_call(functools.partial(dft_kernel, tile, first), in_specs=[pl.B...  16.3 us
    pallas_call x7, Pallas kernels, sums(): pl.pallas_call(functools.partial(sums_kernel, [(at, first) for at, first,...  9.62 us
    pallas_call x4, Pallas kernels, score(): pl.pallas_call(functools.partial(score_kernel, shapes, len(spectra)), in_...  9.54 us
    ppermute x14, waiting for transfers between devices, onward(): return lax.ppermute(value, 'dp', list(zip(RING, RING[1:] + RING[:1])))  8.82 us
    ppermute x14, starting transfers between devices, backward(): return lax.ppermute(value, 'dp', list(zip(RING[1:] + RING[:1], RING)))  4.44 us
    unnamed x30, local copies, waits for them, and re-layouts  2.26 us
  transfers between devices with their start and end apart: 31, of which 17 were waited for; matrix products, arithmetic and copies ran while one was open for 1% of the time, Pallas kernels for 29%

profile of v5, /device:TPU:0, one launch (start us, length us, event | category | flops | bytes accessed | tf_op | source)
XLA Modules:
  0.0 111.4 jit_solution(10624194195612453473)
XLA Ops:
  1.9 3.1 %collective-permute-start = (bf16[72,2176]{1,0:T(8,128)(2,1)S(1)}, bf16[72,2176]{1,0:T(8,128)(2,1)S(1)}, u32[]{:S(2)}, u32[]{:S(2)}) collective-permute-start(bf16[72,2176]{1,0:T(8,128)(2,1)S(1)} %get-tuple-element.73.rest_2_), channel_id=1, source_target_pairs={{0,8},{8,16},{16,24},{24,28},{28,20},{20,12},{12,4},{4,0},{1,9},{9... | collective-permute-start | bytes 940040 | tf_op jit(solution)/shard_map/ppermute | solution.py:376
  4.9 2.0 %collective-permute-start.4 = (bf16[72,2048]{1,0:T(8,128)(2,1)S(1)}, bf16[72,2048]{1,0:T(8,128)(2,1)}, u32[]{:S(2)}, u32[]{:S(2)}) collective-permute-start(bf16[72,2048]{1,0:T(8,128)(2,1)S(1)} %get-tuple-element.74.rest_5_), channel_id=1, source_target_pairs={{0,8},{8,16},{16,24},{24,28},{28,20},{20,12},{12,4},{4,0},{1,9},{9... | collective-permute-start | bytes 884744 | tf_op jit(solution)/shard_map/ppermute | solution.py:376
  7.9 7.4 %dft.3.rest_0_ = bf16[256,4224]{1,0:T(8,128)(2,1)S(1)} custom-call(bf16[328,256]{1,0:T(8,128)(2,1)S(1)} %copy-done, bf16[512,128,128]{2,1,0:T(8,128)(2,1)} %img_ref.5), custom_call_target="tpu_custom_call" | custom-call | flops 1711276032 | bytes 10551296 | tf_op jit(solution)/shard_map/dft/pallas_call | solution.py:222
  15.4 2.1 %collective-permute-start.2 = (bf16[72,2176]{1,0:T(8,128)(2,1)S(1)}, bf16[72,2176]{1,0:T(8,128)(2,1)}, u32[]{:S(2)}, u32[]{:S(2)}) collective-permute-start(bf16[72,2176]{1,0:T(8,128)(2,1)S(1)} %collective-permute-done.rest_3_), channel_id=1, source_target_pairs={{0,8},{8,16},{16,24},{24,28},{28,20},{20,12},{12,4},{4,0},{1,9},{9... | collective-permute-start | bytes 940040 | tf_op jit(solution)/shard_map/ppermute | solution.py:376
  17.4 2.1 %collective-permute-done.4.rest_6_ = bf16[72,2048]{1,0:T(8,128)(2,1)} collective-permute-done((bf16[72,2048]{1,0:T(8,128)(2,1)S(1)}, bf16[72,2048]{1,0:T(8,128)(2,1)}, u32[]{:S(2)}, u32[]{:S(2)}) %collective-permute-start.4) | collective-permute-done | bytes 294944 | tf_op jit(solution)/shard_map/ppermute | solution.py:376
  19.5 2.2 %collective-permute-done.5.rest_4_ = bf16[72,2176]{1,0:T(8,128)(2,1)} collective-permute-done((bf16[72,2176]{1,0:T(8,128)(2,1)S(1)}, bf16[72,2176]{1,0:T(8,128)(2,1)}, u32[]{:S(2)}, u32[]{:S(2)}) %collective-permute-start.5) | collective-permute-done | bytes 313376 | tf_op jit(solution)/shard_map/ppermute | solution.py:380
  21.7 2.0 %collective-permute-start.8 = (bf16[72,2048]{1,0:T(8,128)(2,1)}, bf16[72,2048]{1,0:T(8,128)(2,1)}, u32[]{:S(2)}, u32[]{:S(2)}) collective-permute-start(bf16[72,2048]{1,0:T(8,128)(2,1)} %collective-permute-done.4.rest_6_), channel_id=1, source_target_pairs={{0,8},{8,16},{16,24},{24,28},{28,20},{20,12},{12,4},{4,0},{1,9},{9... | collective-permute-start | bytes 884744 | tf_op jit(solution)/shard_map/ppermute | solution.py:376
  23.7 4.5 %dft.4.rest_0_ = bf16[128,4224]{1,0:T(8,128)(2,1)S(1)} custom-call(bf16[328,256]{1,0:T(8,128)(2,1)S(1)} %copy-done, bf16[512,128,128]{2,1,0:T(8,128)(2,1)} %img_ref.5), custom_call_target="tpu_custom_call" | custom-call | flops 855638016 | bytes 5275648 | tf_op jit(solution)/shard_map/dft/pallas_call | solution.py:222
  30.4 2.2 %collective-permute-done.8.rest_10_ = bf16[72,2048]{1,0:T(8,128)(2,1)} collective-permute-done((bf16[72,2048]{1,0:T(8,128)(2,1)}, bf16[72,2048]{1,0:T(8,128)(2,1)}, u32[]{:S(2)}, u32[]{:S(2)}) %collective-permute-start.8) | collective-permute-done | bytes 294944 | tf_op jit(solution)/shard_map/ppermute | solution.py:376
  32.5 2.2 %collective-permute-done.9.rest_9_ = bf16[72,2176]{1,0:T(8,128)(2,1)} collective-permute-done((bf16[72,2176]{1,0:T(8,128)(2,1)}, bf16[72,2176]{1,0:T(8,128)(2,1)}, u32[]{:S(2)}, u32[]{:S(2)}) %collective-permute-start.9) | collective-permute-done | bytes 313376 | tf_op jit(solution)/shard_map/ppermute | solution.py:380
  36.8 4.5 %dft.5.rest_1_ = bf16[256,4224]{1,0:T(8,128)(2,1)S(1)} custom-call(bf16[328,256]{1,0:T(8,128)(2,1)S(1)} %copy-done.1, bf16[512,128,128]{2,1,0:T(8,128)(2,1)} %img_ref.5, bf16[128,4224]{1,0:T(8,128)(2,1)S(1)} %dft.4.rest_0_), custom_call_target="tpu_custom_call" | custom-call | flops 855638016 | bytes 5275648 | tf_op jit(solution)/shard_map/dft/pallas_call | solution.py:222
  41.3 2.0 %collective-permute-start.11 = (bf16[72,2176]{1,0:T(8,128)(2,1)}, bf16[72,2176]{1,0:T(8,128)(2,1)S(1)}, u32[]{:S(2)}, u32[]{:S(2)}) collective-permute-start(bf16[72,2176]{1,0:T(8,128)(2,1)} %collective-permute-done.6.rest_2_), channel_id=1, source_target_pairs={{0,8},{8,16},{16,24},{24,28},{28,20},{20,12},{12,4},{4,0},{1,9},{9... | collective-permute-start | bytes 940040 | tf_op jit(solution)/shard_map/ppermute | solution.py:376
  44.1 4.3 %score.4.before_ref = f32[4,512]{1,0:T(4,128)S(1)} custom-call(s32[8]{0:T(128)S(1)} %multiply_bitcast_fusion.base_ref, s32[4,512]{1,0:T(4,128)S(1)} %add_bitcast_fusion.panel_ref, f32[4,512]{1,0:T(4,128)S(1)} %broadcast_in_dim.6.before_ref, bf16[256,4224]{1,0:T(8,128)(2,1)S(1)} %dft.3.rest_0_, bf16[256,4224]{1,0:T(8,128)(2,1)S(1)} %dft.5.rest_1_, ...), custom_call_target="tpu_custom_call" | custom-call | flops 1557135360 | bytes 3041280 | tf_op jit(solution)/shard_map/score/pallas_call | solution.py:290
  48.4 2.5 %score.5.before_ref = f32[4,512]{1,0:T(4,128)S(1)} custom-call(s32[8]{0:T(128)S(1)} %multiply_bitcast_fusion.base_ref, s32[4,512]{1,0:T(4,128)S(1)} %add_bitcast_fusion.panel_ref, f32[4,512]{1,0:T(4,128)S(1)} %score.4.before_ref, bf16[256,4224]{1,0:T(8,128)(2,1)S(1)} %dft.3.rest_0_, bf16[256,4224]{1,0:T(8,128)(2,1)S(1)} %dft.5.rest_1_, ...), custom_call_target="tpu_custom_call" | custom-call | flops 622854144 | bytes 1216512 | tf_op jit(solution)/shard_map/score/pallas_call | solution.py:290
  59.7 1.7 %collective-permute-start.17 = (bf16[72,2176]{1,0:T(8,128)(2,1)S(1)}, bf16[72,2176]{1,0:T(8,128)(2,1)S(1)}, u32[]{:S(2)}, u32[]{:S(2)}) collective-permute-start(bf16[72,2176]{1,0:T(8,128)(2,1)S(1)} %get-tuple-element.99), channel_id=1, source_target_pairs={{0,8},{8,16},{16,24},{24,28},{28,20},{20,12},{12,4},{4,0},{1,9},{9... | collective-permute-start | bytes 940040 | tf_op jit(solution)/shard_map/ppermute | solution.py:376
  65.1 6.1 %collective-permute-done.18 = bf16[72,2048]{1,0:T(8,128)(2,1)S(1)} collective-permute-done((bf16[72,2048]{1,0:T(8,128)(2,1)S(1)}, bf16[72,2048]{1,0:T(8,128)(2,1)S(1)}, u32[]{:S(2)}, u32[]{:S(2)}) %collective-permute-start.18) | collective-permute-done | bytes 294944 | tf_op jit(solution)/shard_map/ppermute | solution.py:380
  76.2 1.7 %collective-permute-done.22 = bf16[72,2176]{1,0:T(8,128)(2,1)S(1)} collective-permute-done((bf16[72,2176]{1,0:T(8,128)(2,1)S(1)}, bf16[72,2176]{1,0:T(8,128)(2,1)S(1)}, u32[]{:S(2)}, u32[]{:S(2)}) %collective-permute-start.22) | collective-permute-done | bytes 313376 | tf_op jit(solution)/shard_map/ppermute | solution.py:380
  81.5 2.7 %collective-permute-done.20 = bf16[72,2048]{1,0:T(8,128)(2,1)S(1)} collective-permute-done((bf16[72,2048]{1,0:T(8,128)(2,1)S(1)}, bf16[72,2048]{1,0:T(8,128)(2,1)S(1)}, u32[]{:S(2)}, u32[]{:S(2)}) %collective-permute-start.20) | collective-permute-done | bytes 294944 | tf_op jit(solution)/shard_map/ppermute | solution.py:380
  89.3 1.7 %collective-permute-done.26 = bf16[72,2176]{1,0:T(8,128)(2,1)S(1)} collective-permute-done((bf16[72,2176]{1,0:T(8,128)(2,1)S(1)}, bf16[72,2176]{1,0:T(8,128)(2,1)S(1)}, u32[]{:S(2)}, u32[]{:S(2)}) %collective-permute-start.26) | collective-permute-done | bytes 313376 | tf_op jit(solution)/shard_map/ppermute | solution.py:380
  91.5 1.7 %collective-permute-start.29 = (bf16[72,2048]{1,0:T(8,128)(2,1)S(1)}, bf16[72,2048]{1,0:T(8,128)(2,1)S(1)}, u32[]{:S(2)}, u32[]{:S(2)}) collective-permute-start(bf16[72,2048]{1,0:T(8,128)(2,1)S(1)} %add_convert_fusion.6), channel_id=1, source_target_pairs={{0,8},{8,16},{16,24},{24,28},{28,20},{20,12},{12,4},{4,0},{1,9},{9... | collective-permute-start | bytes 884744 | tf_op jit(solution)/shard_map/ppermute | solution.py:376
  94.6 2.7 %collective-permute-done.24 = bf16[72,2048]{1,0:T(8,128)(2,1)S(1)} collective-permute-done((bf16[72,2048]{1,0:T(8,128)(2,1)S(1)}, bf16[72,2048]{1,0:T(8,128)(2,1)S(1)}, u32[]{:S(2)}, u32[]{:S(2)}) %collective-permute-start.24) | collective-permute-done | bytes 294944 | tf_op jit(solution)/shard_map/ppermute | solution.py:380
  102.3 1.7 %collective-permute-done.28.rest_2_ = bf16[72,2176]{1,0:T(8,128)(2,1)S(1)} collective-permute-done((bf16[72,2176]{1,0:T(8,128)(2,1)S(1)}, bf16[72,2176]{1,0:T(8,128)(2,1)S(1)}, u32[]{:S(2)}, u32[]{:S(2)}) %collective-permute-start.28) | collective-permute-done | bytes 313376 | tf_op jit(solution)/shard_map/ppermute | solution.py:380
  104.0 5.5 %collective-permute-done.30.rest_5_ = bf16[72,2048]{1,0:T(8,128)(2,1)S(1)} collective-permute-done((bf16[72,2048]{1,0:T(8,128)(2,1)S(1)}, bf16[72,2048]{1,0:T(8,128)(2,1)S(1)}, u32[]{:S(2)}, u32[]{:S(2)}) %collective-permute-start.30) | collective-permute-done | bytes 294944 | tf_op jit(solution)/shard_map/ppermute | solution.py:380
  109.4 1.8 %unfold.1 = f32[72,8192]{1,0:T(8,128)} custom-call(f32[72,2176]{1,0:T(8,128)S(1)} %get-tuple-element.131.rest_0_, bf16[72,2176]{1,0:T(8,128)(2,1)S(1)} %collective-permute-done.27.rest_1_, bf16[72,2176]{1,0:T(8,128)(2,1)S(1)} %collective-permute-done.28.rest_2_, f32[72,2048]{1,0:T(8,128)S(1)} %get-tuple-element.136.rest_3_, ...), custom_call_target="tpu_custom_call" | custom-call | tf_op jit(solution)/shard_map/unfold/pallas_call | solution.py:150
  (97 shorter events, 40.9 us)
Async XLA Ops:
  1.9 13.5 %collective-permute-start = (bf16[72,2176]{1,0:T(8,128)(2,1)S(1)}, bf16[72,2176]{1,0:T(8,128)(2,1)S(1)}, u32[]{:S(2)}, u32[]{:S(2)}) collective-permute-start(bf16[72,2176]{1,0:T(8,128)(2,1)S(1)} %get-tuple-element.73.rest_2_), channel_id=1, source_target_pairs={{0,8},{8,16},{16,24},{24,28},{28,20},{20,12},{12,4},{4,0},{1,9},{9... | collective-permute-start | bytes 940040 | tf_op jit(solution)/shard_map/ppermute | solution.py:376
  4.9 14.6 %collective-permute-start.4 = (bf16[72,2048]{1,0:T(8,128)(2,1)S(1)}, bf16[72,2048]{1,0:T(8,128)(2,1)}, u32[]{:S(2)}, u32[]{:S(2)}) collective-permute-start(bf16[72,2048]{1,0:T(8,128)(2,1)S(1)} %get-tuple-element.74.rest_5_), channel_id=1, source_target_pairs={{0,8},{8,16},{16,24},{24,28},{28,20},{20,12},{12,4},{4,0},{1,9},{9... | collective-permute-start | bytes 884744 | tf_op jit(solution)/shard_map/ppermute | solution.py:376
  7.0 14.7 %collective-permute-start.5 = (bf16[72,2176]{1,0:T(8,128)(2,1)S(1)}, bf16[72,2176]{1,0:T(8,128)(2,1)}, u32[]{:S(2)}, u32[]{:S(2)}) collective-permute-start(bf16[72,2176]{1,0:T(8,128)(2,1)S(1)} %get-tuple-element.73.rest_2_), channel_id=1, source_target_pairs={{8,0},{16,8},{24,16},{28,24},{20,28},{12,20},{4,12},{0,4},{9,1},{1... | collective-permute-start | bytes 940040 | tf_op jit(solution)/shard_map/ppermute | solution.py:380
  15.4 12.9 %collective-permute-start.2 = (bf16[72,2176]{1,0:T(8,128)(2,1)S(1)}, bf16[72,2176]{1,0:T(8,128)(2,1)}, u32[]{:S(2)}, u32[]{:S(2)}) collective-permute-start(bf16[72,2176]{1,0:T(8,128)(2,1)S(1)} %collective-permute-done.rest_3_), channel_id=1, source_target_pairs={{0,8},{8,16},{16,24},{24,28},{28,20},{20,12},{12,4},{4,0},{1,9},{9... | collective-permute-start | bytes 940040 | tf_op jit(solution)/shard_map/ppermute | solution.py:376
  17.4 10.8 %collective-permute-start.3 = (bf16[72,2048]{1,0:T(8,128)(2,1)S(1)}, bf16[72,2048]{1,0:T(8,128)(2,1)}, u32[]{:S(2)}, u32[]{:S(2)}) collective-permute-start(bf16[72,2048]{1,0:T(8,128)(2,1)S(1)} %collective-permute-done.1.rest_7_), channel_id=1, source_target_pairs={{8,0},{16,8},{24,16},{28,24},{20,28},{12,20},{4,12},{0,4},{9,1},{1... | collective-permute-start | bytes 884744 | tf_op jit(solution)/shard_map/ppermute | solution.py:380
  21.7 13.0 %collective-permute-start.9 = (bf16[72,2176]{1,0:T(8,128)(2,1)}, bf16[72,2176]{1,0:T(8,128)(2,1)}, u32[]{:S(2)}, u32[]{:S(2)}) collective-permute-start(bf16[72,2176]{1,0:T(8,128)(2,1)} %collective-permute-done.5.rest_4_), channel_id=1, source_target_pairs={{8,0},{16,8},{24,16},{28,24},{20,28},{12,20},{4,12},{0,4},{9,1},{1... | collective-permute-start | bytes 940040 | tf_op jit(solution)/shard_map/ppermute | solution.py:380
  21.7 10.8 %collective-permute-start.8 = (bf16[72,2048]{1,0:T(8,128)(2,1)}, bf16[72,2048]{1,0:T(8,128)(2,1)}, u32[]{:S(2)}, u32[]{:S(2)}) collective-permute-start(bf16[72,2048]{1,0:T(8,128)(2,1)} %collective-permute-done.4.rest_6_), channel_id=1, source_target_pairs={{0,8},{8,16},{16,24},{24,28},{28,20},{20,12},{12,4},{4,0},{1,9},{9... | collective-permute-start | bytes 884744 | tf_op jit(solution)/shard_map/ppermute | solution.py:376
  28.2 13.0 %collective-permute-start.6 = (bf16[72,2176]{1,0:T(8,128)(2,1)}, bf16[72,2176]{1,0:T(8,128)(2,1)}, u32[]{:S(2)}, u32[]{:S(2)}) collective-permute-start(bf16[72,2176]{1,0:T(8,128)(2,1)} %collective-permute-done.2.rest_8_), channel_id=1, source_target_pairs={{0,8},{8,16},{16,24},{24,28},{28,20},{20,12},{12,4},{4,0},{1,9},{9... | collective-permute-start | bytes 940040 | tf_op jit(solution)/shard_map/ppermute | solution.py:376
  29.9 11.4 %collective-permute-start.7 = (bf16[72,2048]{1,0:T(8,128)(2,1)}, bf16[72,2048]{1,0:T(8,128)(2,1)S(1)}, u32[]{:S(2)}, u32[]{:S(2)}) collective-permute-start(bf16[72,2048]{1,0:T(8,128)(2,1)} %collective-permute-done.3.rest_11_), channel_id=1, source_target_pairs={{8,0},{16,8},{24,16},{28,24},{20,28},{12,20},{4,12},{0,4},{9,1},{1... | collective-permute-start | bytes 884744 | tf_op jit(solution)/shard_map/ppermute | solution.py:380
  34.7 13.6 %collective-permute-start.12 = (bf16[72,2048]{1,0:T(8,128)(2,1)}, bf16[72,2048]{1,0:T(8,128)(2,1)S(1)}, u32[]{:S(2)}, u32[]{:S(2)}) collective-permute-start(bf16[72,2048]{1,0:T(8,128)(2,1)} %collective-permute-done.8.rest_10_), channel_id=1, source_target_pairs={{0,8},{8,16},{16,24},{24,28},{28,20},{20,12},{12,4},{4,0},{1,9},{9... | collective-permute-start | bytes 884744 | tf_op jit(solution)/shard_map/ppermute | solution.py:376
  36.3 12.1 %collective-permute-start.13 = (bf16[72,2176]{1,0:T(8,128)(2,1)}, bf16[72,2176]{1,0:T(8,128)(2,1)S(1)}, u32[]{:S(2)}, u32[]{:S(2)}) collective-permute-start(bf16[72,2176]{1,0:T(8,128)(2,1)} %collective-permute-done.9.rest_9_), channel_id=1, source_target_pairs={{8,0},{16,8},{24,16},{28,24},{20,28},{12,20},{4,12},{0,4},{9,1},{1... | collective-permute-start | bytes 940040 | tf_op jit(solution)/shard_map/ppermute | solution.py:380
  41.3 11.5 %collective-permute-start.10 = (bf16[72,2048]{1,0:T(8,128)(2,1)S(1)}, bf16[72,2048]{1,0:T(8,128)(2,1)S(1)}, u32[]{:S(2)}, u32[]{:S(2)}) collective-permute-start(bf16[72,2048]{1,0:T(8,128)(2,1)S(1)} %collective-permute-done.7.rest_5_), channel_id=1, source_target_pairs={{8,0},{16,8},{24,16},{28,24},{20,28},{12,20},{4,12},{0,4},{9,1},{1... | collective-permute-start | bytes 884744 | tf_op jit(solution)/shard_map/ppermute | solution.py:380
  59.7 11.5 %collective-permute-start.17 = (bf16[72,2176]{1,0:T(8,128)(2,1)S(1)}, bf16[72,2176]{1,0:T(8,128)(2,1)S(1)}, u32[]{:S(2)}, u32[]{:S(2)}) collective-permute-start(bf16[72,2176]{1,0:T(8,128)(2,1)S(1)} %get-tuple-element.99), channel_id=1, source_target_pairs={{0,8},{8,16},{16,24},{24,28},{28,20},{20,12},{12,4},{4,0},{1,9},{9... | collective-permute-start | bytes 940040 | tf_op jit(solution)/shard_map/ppermute | solution.py:376
  61.7 14.5 %collective-permute-start.21 = (bf16[72,2048]{1,0:T(8,128)(2,1)S(1)}, bf16[72,2048]{1,0:T(8,128)(2,1)S(1)}, u32[]{:S(2)}, u32[]{:S(2)}) collective-permute-start(bf16[72,2048]{1,0:T(8,128)(2,1)S(1)} %get-tuple-element.108), channel_id=1, source_target_pairs={{0,8},{8,16},{16,24},{24,28},{28,20},{20,12},{12,4},{4,0},{1,9},{9... | collective-permute-start | bytes 884744 | tf_op jit(solution)/shard_map/ppermute | solution.py:376
  63.3 14.6 %collective-permute-start.22 = (bf16[72,2176]{1,0:T(8,128)(2,1)S(1)}, bf16[72,2176]{1,0:T(8,128)(2,1)S(1)}, u32[]{:S(2)}, u32[]{:S(2)}) collective-permute-start(bf16[72,2176]{1,0:T(8,128)(2,1)S(1)} %get-tuple-element.109), channel_id=1, source_target_pairs={{8,0},{16,8},{24,16},{28,24},{20,28},{12,20},{4,12},{0,4},{9,1},{1... | collective-permute-start | bytes 940040 | tf_op jit(solution)/shard_map/ppermute | solution.py:380
  71.2 13.0 %collective-permute-start.19 = (bf16[72,2176]{1,0:T(8,128)(2,1)S(1)}, bf16[72,2176]{1,0:T(8,128)(2,1)S(1)}, u32[]{:S(2)}, u32[]{:S(2)}) collective-permute-start(bf16[72,2176]{1,0:T(8,128)(2,1)S(1)} %add_convert_fusion.4), channel_id=1, source_target_pairs={{0,8},{8,16},{16,24},{24,28},{28,20},{20,12},{12,4},{4,0},{1,9},{9... | collective-permute-start | bytes 940040 | tf_op jit(solution)/shard_map/ppermute | solution.py:376
  72.9 11.3 %collective-permute-start.20 = (bf16[72,2048]{1,0:T(8,128)(2,1)S(1)}, bf16[72,2048]{1,0:T(8,128)(2,1)S(1)}, u32[]{:S(2)}, u32[]{:S(2)}) collective-permute-start(bf16[72,2048]{1,0:T(8,128)(2,1)S(1)} %add_convert_fusion.9), channel_id=1, source_target_pairs={{8,0},{16,8},{24,16},{28,24},{20,28},{12,20},{4,12},{0,4},{9,1},{1... | collective-permute-start | bytes 884744 | tf_op jit(solution)/shard_map/ppermute | solution.py:380
  78.0 11.3 %collective-permute-start.25 = (bf16[72,2048]{1,0:T(8,128)(2,1)S(1)}, bf16[72,2048]{1,0:T(8,128)(2,1)S(1)}, u32[]{:S(2)}, u32[]{:S(2)}) collective-permute-start(bf16[72,2048]{1,0:T(8,128)(2,1)S(1)} %add_convert_fusion.7), channel_id=1, source_target_pairs={{0,8},{8,16},{16,24},{24,28},{28,20},{20,12},{12,4},{4,0},{1,9},{9... | collective-permute-start | bytes 884744 | tf_op jit(solution)/shard_map/ppermute | solution.py:376
  79.7 11.3 %collective-permute-start.26 = (bf16[72,2176]{1,0:T(8,128)(2,1)S(1)}, bf16[72,2176]{1,0:T(8,128)(2,1)S(1)}, u32[]{:S(2)}, u32[]{:S(2)}) collective-permute-start(bf16[72,2176]{1,0:T(8,128)(2,1)S(1)} %add_convert_fusion.2), channel_id=1, source_target_pairs={{8,0},{16,8},{24,16},{28,24},{20,28},{12,20},{4,12},{0,4},{9,1},{1... | collective-permute-start | bytes 940040 | tf_op jit(solution)/shard_map/ppermute | solution.py:380
  84.3 13.0 %collective-permute-start.23 = (bf16[72,2176]{1,0:T(8,128)(2,1)S(1)}, bf16[72,2176]{1,0:T(8,128)(2,1)S(1)}, u32[]{:S(2)}, u32[]{:S(2)}) collective-permute-start(bf16[72,2176]{1,0:T(8,128)(2,1)S(1)} %add_convert_fusion.3), channel_id=1, source_target_pairs={{0,8},{8,16},{16,24},{24,28},{28,20},{20,12},{12,4},{4,0},{1,9},{9... | collective-permute-start | bytes 940040 | tf_op jit(solution)/shard_map/ppermute | solution.py:376
  86.0 11.3 %collective-permute-start.24 = (bf16[72,2048]{1,0:T(8,128)(2,1)S(1)}, bf16[72,2048]{1,0:T(8,128)(2,1)S(1)}, u32[]{:S(2)}, u32[]{:S(2)}) collective-permute-start(bf16[72,2048]{1,0:T(8,128)(2,1)S(1)} %add_convert_fusion.8), channel_id=1, source_target_pairs={{8,0},{16,8},{24,16},{28,24},{20,28},{12,20},{4,12},{0,4},{9,1},{1... | collective-permute-start | bytes 884744 | tf_op jit(solution)/shard_map/ppermute | solution.py:380
  91.0 13.0 %collective-permute-start.28 = (bf16[72,2176]{1,0:T(8,128)(2,1)S(1)}, bf16[72,2176]{1,0:T(8,128)(2,1)S(1)}, u32[]{:S(2)}, u32[]{:S(2)}) collective-permute-start(bf16[72,2176]{1,0:T(8,128)(2,1)S(1)} %add_convert_fusion), channel_id=1, source_target_pairs={{8,0},{16,8},{24,16},{28,24},{20,28},{12,20},{4,12},{0,4},{9,1},{1... | collective-permute-start | bytes 940040 | tf_op jit(solution)/shard_map/ppermute | solution.py:380
  91.5 10.8 %collective-permute-start.29 = (bf16[72,2048]{1,0:T(8,128)(2,1)S(1)}, bf16[72,2048]{1,0:T(8,128)(2,1)S(1)}, u32[]{:S(2)}, u32[]{:S(2)}) collective-permute-start(bf16[72,2048]{1,0:T(8,128)(2,1)S(1)} %add_convert_fusion.6), channel_id=1, source_target_pairs={{0,8},{8,16},{16,24},{24,28},{28,20},{20,12},{12,4},{4,0},{1,9},{9... | collective-permute-start | bytes 884744 | tf_op jit(solution)/shard_map/ppermute | solution.py:376
  97.3 12.1 %collective-permute-start.27 = (bf16[72,2176]{1,0:T(8,128)(2,1)S(1)}, bf16[72,2176]{1,0:T(8,128)(2,1)S(1)}, u32[]{:S(2)}, u32[]{:S(2)}) collective-permute-start(bf16[72,2176]{1,0:T(8,128)(2,1)S(1)} %add_convert_fusion.1), channel_id=1, source_target_pairs={{0,8},{8,16},{16,24},{24,28},{28,20},{20,12},{12,4},{4,0},{1,9},{9... | collective-permute-start | bytes 940040 | tf_op jit(solution)/shard_map/ppermute | solution.py:376
  (22 other events, 221.7 us)

commit v6 on v5

--- a/solution.py
+++ b/solution.py
@@ -426,7 +426,7 @@
         arrived, picked = tie(p4[piece], picked)
         picked = score(bases, spectra, panel, picked, [((4,), starts[piece], [arrived])])
 
-    turns = [[(c, c ^ n) for c in range(cls_count)] for n in range(cls_count - 1, 0, -1)]
+    turns = [[(c, c ^ n) for c in range(cls_count)] for n in (*range(2, cls_count), 1)]
     weight = [picked] + [lax.ppermute(picked, "cls", turn) for turn in turns] + [prior, precision]
 
     narrow, wide = jnp.bfloat16, jnp.float32

time: 112 us -> 111 us (level)
    ppermute x14, waiting for transfers between devices: 26.2 us -> 24.8 us  [backward(): return lax.ppermute(value, 'dp', list(zip(RING[1:] + RING[:1], RING)))]
where the time goes in v6:
time: 111 us
  Pallas kernels  37.9 us (34%)
  waiting for transfers between devices  36.5 us (33%)
  starting transfers between devices  32.5 us (29%)
  local copies, waits for them, and re-layouts  2.26 us (2%)
  other arithmetic  1.31 us (1%)
    ppermute x14, starting transfers between devices, onward(): return lax.ppermute(value, 'dp', list(zip(RING, RING[1:] + RING[:1])))  25.8 us
    ppermute x14, waiting for transfers between devices, backward(): return lax.ppermute(value, 'dp', list(zip(RING[1:] + RING[:1], RING)))  24.8 us
    pallas_call x3, Pallas kernels, dft(): pl.pallas_call(functools.partial(dft_kernel, tile, first), in_specs=[pl.B...  16.3 us
    pallas_call x7, Pallas kernels, sums(): pl.pallas_call(functools.partial(sums_kernel, [(at, first) for at, first,...  9.62 us
    pallas_call x4, Pallas kernels, score(): pl.pallas_call(functools.partial(score_kernel, shapes, len(spectra)), in_...  9.54 us
    ppermute x14, waiting for transfers between devices, onward(): return lax.ppermute(value, 'dp', list(zip(RING, RING[1:] + RING[:1])))  9.02 us
    ppermute x14, starting transfers between devices, backward(): return lax.ppermute(value, 'dp', list(zip(RING[1:] + RING[:1], RING)))  4.52 us
    ppermute x3, waiting for transfers between devices, by_ring(): lax.ppermute(picked, 'cls', turn)  2.7 us
  transfers between devices with their start and end apart: 31, of which 17 were waited for; matrix products, arithmetic and copies ran while one was open for 1% of the time, Pallas kernels for 29%

profile of v6, /device:TPU:0, one launch (start us, length us, event | category | flops | bytes accessed | tf_op | source)
XLA Modules:
  0.0 111.0 jit_solution(15127174994685443549)
XLA Ops:
  1.9 3.1 %collective-permute-start = (bf16[72,2176]{1,0:T(8,128)(2,1)S(1)}, bf16[72,2176]{1,0:T(8,128)(2,1)S(1)}, u32[]{:S(2)}, u32[]{:S(2)}) collective-permute-start(bf16[72,2176]{1,0:T(8,128)(2,1)S(1)} %get-tuple-element.73.rest_2_), channel_id=1, source_target_pairs={{0,8},{8,16},{16,24},{24,28},{28,20},{20,12},{12,4},{4,0},{1,9},{9... | collective-permute-start | bytes 940040 | tf_op jit(solution)/shard_map/ppermute | solution.py:376
  4.9 2.0 %collective-permute-start.4 = (bf16[72,2048]{1,0:T(8,128)(2,1)S(1)}, bf16[72,2048]{1,0:T(8,128)(2,1)}, u32[]{:S(2)}, u32[]{:S(2)}) collective-permute-start(bf16[72,2048]{1,0:T(8,128)(2,1)S(1)} %get-tuple-element.74.rest_5_), channel_id=1, source_target_pairs={{0,8},{8,16},{16,24},{24,28},{28,20},{20,12},{12,4},{4,0},{1,9},{9... | collective-permute-start | bytes 884744 | tf_op jit(solution)/shard_map/ppermute | solution.py:376
  7.9 7.4 %dft.3.rest_0_ = bf16[256,4224]{1,0:T(8,128)(2,1)S(1)} custom-call(bf16[328,256]{1,0:T(8,128)(2,1)S(1)} %copy-done, bf16[512,128,128]{2,1,0:T(8,128)(2,1)} %img_ref.5), custom_call_target="tpu_custom_call" | custom-call | flops 1711276032 | bytes 10551296 | tf_op jit(solution)/shard_map/dft/pallas_call | solution.py:222
  15.4 2.1 %collective-permute-start.2 = (bf16[72,2176]{1,0:T(8,128)(2,1)S(1)}, bf16[72,2176]{1,0:T(8,128)(2,1)}, u32[]{:S(2)}, u32[]{:S(2)}) collective-permute-start(bf16[72,2176]{1,0:T(8,128)(2,1)S(1)} %collective-permute-done.rest_3_), channel_id=1, source_target_pairs={{0,8},{8,16},{16,24},{24,28},{28,20},{20,12},{12,4},{4,0},{1,9},{9... | collective-permute-start | bytes 940040 | tf_op jit(solution)/shard_map/ppermute | solution.py:376
  17.4 2.1 %collective-permute-done.4.rest_6_ = bf16[72,2048]{1,0:T(8,128)(2,1)} collective-permute-done((bf16[72,2048]{1,0:T(8,128)(2,1)S(1)}, bf16[72,2048]{1,0:T(8,128)(2,1)}, u32[]{:S(2)}, u32[]{:S(2)}) %collective-permute-start.4) | collective-permute-done | bytes 294944 | tf_op jit(solution)/shard_map/ppermute | solution.py:376
  19.5 2.2 %collective-permute-done.5.rest_4_ = bf16[72,2176]{1,0:T(8,128)(2,1)} collective-permute-done((bf16[72,2176]{1,0:T(8,128)(2,1)S(1)}, bf16[72,2176]{1,0:T(8,128)(2,1)}, u32[]{:S(2)}, u32[]{:S(2)}) %collective-permute-start.5) | collective-permute-done | bytes 313376 | tf_op jit(solution)/shard_map/ppermute | solution.py:380
  21.7 2.0 %collective-permute-start.8 = (bf16[72,2048]{1,0:T(8,128)(2,1)}, bf16[72,2048]{1,0:T(8,128)(2,1)}, u32[]{:S(2)}, u32[]{:S(2)}) collective-permute-start(bf16[72,2048]{1,0:T(8,128)(2,1)} %collective-permute-done.4.rest_6_), channel_id=1, source_target_pairs={{0,8},{8,16},{16,24},{24,28},{28,20},{20,12},{12,4},{4,0},{1,9},{9... | collective-permute-start | bytes 884744 | tf_op jit(solution)/shard_map/ppermute | solution.py:376
  23.7 4.5 %dft.4.rest_0_ = bf16[128,4224]{1,0:T(8,128)(2,1)S(1)} custom-call(bf16[328,256]{1,0:T(8,128)(2,1)S(1)} %copy-done, bf16[512,128,128]{2,1,0:T(8,128)(2,1)} %img_ref.5), custom_call_target="tpu_custom_call" | custom-call | flops 855638016 | bytes 5275648 | tf_op jit(solution)/shard_map/dft/pallas_call | solution.py:222
  30.4 2.2 %collective-permute-done.8.rest_10_ = bf16[72,2048]{1,0:T(8,128)(2,1)} collective-permute-done((bf16[72,2048]{1,0:T(8,128)(2,1)}, bf16[72,2048]{1,0:T(8,128)(2,1)}, u32[]{:S(2)}, u32[]{:S(2)}) %collective-permute-start.8) | collective-permute-done | bytes 294944 | tf_op jit(solution)/shard_map/ppermute | solution.py:376
  32.5 2.2 %collective-permute-done.9.rest_9_ = bf16[72,2176]{1,0:T(8,128)(2,1)} collective-permute-done((bf16[72,2176]{1,0:T(8,128)(2,1)}, bf16[72,2176]{1,0:T(8,128)(2,1)}, u32[]{:S(2)}, u32[]{:S(2)}) %collective-permute-start.9) | collective-permute-done | bytes 313376 | tf_op jit(solution)/shard_map/ppermute | solution.py:380
  36.8 4.5 %dft.5.rest_1_ = bf16[256,4224]{1,0:T(8,128)(2,1)S(1)} custom-call(bf16[328,256]{1,0:T(8,128)(2,1)S(1)} %copy-done.1, bf16[512,128,128]{2,1,0:T(8,128)(2,1)} %img_ref.5, bf16[128,4224]{1,0:T(8,128)(2,1)S(1)} %dft.4.rest_0_), custom_call_target="tpu_custom_call" | custom-call | flops 855638016 | bytes 5275648 | tf_op jit(solution)/shard_map/dft/pallas_call | solution.py:222
  41.3 2.0 %collective-permute-start.11 = (bf16[72,2176]{1,0:T(8,128)(2,1)}, bf16[72,2176]{1,0:T(8,128)(2,1)S(1)}, u32[]{:S(2)}, u32[]{:S(2)}) collective-permute-start(bf16[72,2176]{1,0:T(8,128)(2,1)} %collective-permute-done.6.rest_2_), channel_id=1, source_target_pairs={{0,8},{8,16},{16,24},{24,28},{28,20},{20,12},{12,4},{4,0},{1,9},{9... | collective-permute-start | bytes 940040 | tf_op jit(solution)/shard_map/ppermute | solution.py:376
  44.1 4.3 %score.4.before_ref = f32[4,512]{1,0:T(4,128)S(1)} custom-call(s32[8]{0:T(128)S(1)} %multiply_bitcast_fusion.base_ref, s32[4,512]{1,0:T(4,128)S(1)} %add_bitcast_fusion.panel_ref, f32[4,512]{1,0:T(4,128)S(1)} %broadcast_in_dim.6.before_ref, bf16[256,4224]{1,0:T(8,128)(2,1)S(1)} %dft.3.rest_0_, bf16[256,4224]{1,0:T(8,128)(2,1)S(1)} %dft.5.rest_1_, ...), custom_call_target="tpu_custom_call" | custom-call | flops 1557135360 | bytes 3041280 | tf_op jit(solution)/shard_map/score/pallas_call | solution.py:290
  48.4 2.5 %score.5.before_ref = f32[4,512]{1,0:T(4,128)S(1)} custom-call(s32[8]{0:T(128)S(1)} %multiply_bitcast_fusion.base_ref, s32[4,512]{1,0:T(4,128)S(1)} %add_bitcast_fusion.panel_ref, f32[4,512]{1,0:T(4,128)S(1)} %score.4.before_ref, bf16[256,4224]{1,0:T(8,128)(2,1)S(1)} %dft.3.rest_0_, bf16[256,4224]{1,0:T(8,128)(2,1)S(1)} %dft.5.rest_1_, ...), custom_call_target="tpu_custom_call" | custom-call | flops 622854144 | bytes 1216512 | tf_op jit(solution)/shard_map/score/pallas_call | solution.py:290
  54.2 1.8 %collective-permute-start.14 = (f32[4,512]{1,0:T(4,128)S(1)}, f32[4,512]{1,0:T(4,128)S(1)}, u32[]{:S(2)}, u32[]{:S(2)}) collective-permute-start(f32[4,512]{1,0:T(4,128)S(1)} %score.7.rest_2_), channel_id=1, source_target_pairs={{0,2},{1,3},{2,0},{3,1},{4,6},{5,7},{6,4},{7,5},{8,10},{9,11},{10,... | collective-permute-start | bytes 24584 | tf_op jit(solution)/shard_map/ppermute | solution.py:430
  66.0 6.1 %collective-permute-done.18 = bf16[72,2048]{1,0:T(8,128)(2,1)S(1)} collective-permute-done((bf16[72,2048]{1,0:T(8,128)(2,1)S(1)}, bf16[72,2048]{1,0:T(8,128)(2,1)S(1)}, u32[]{:S(2)}, u32[]{:S(2)}) %collective-permute-start.18) | collective-permute-done | bytes 294944 | tf_op jit(solution)/shard_map/ppermute | solution.py:380
  72.2 1.6 %collective-permute-start.19 = (bf16[72,2176]{1,0:T(8,128)(2,1)S(1)}, bf16[72,2176]{1,0:T(8,128)(2,1)S(1)}, u32[]{:S(2)}, u32[]{:S(2)}) collective-permute-start(bf16[72,2176]{1,0:T(8,128)(2,1)S(1)} %add_convert_fusion.4), channel_id=1, source_target_pairs={{0,8},{8,16},{16,24},{24,28},{28,20},{20,12},{12,4},{4,0},{1,9},{9... | collective-permute-start | bytes 940040 | tf_op jit(solution)/shard_map/ppermute | solution.py:376
  78.9 1.6 %collective-permute-start.25 = (bf16[72,2048]{1,0:T(8,128)(2,1)S(1)}, bf16[72,2048]{1,0:T(8,128)(2,1)S(1)}, u32[]{:S(2)}, u32[]{:S(2)}) collective-permute-start(bf16[72,2048]{1,0:T(8,128)(2,1)S(1)} %add_convert_fusion.7), channel_id=1, source_target_pairs={{0,8},{8,16},{16,24},{24,28},{28,20},{20,12},{12,4},{4,0},{1,9},{9... | collective-permute-start | bytes 884744 | tf_op jit(solution)/shard_map/ppermute | solution.py:376
  82.4 2.7 %collective-permute-done.20 = bf16[72,2048]{1,0:T(8,128)(2,1)S(1)} collective-permute-done((bf16[72,2048]{1,0:T(8,128)(2,1)S(1)}, bf16[72,2048]{1,0:T(8,128)(2,1)S(1)}, u32[]{:S(2)}, u32[]{:S(2)}) %collective-permute-start.20) | collective-permute-done | bytes 294944 | tf_op jit(solution)/shard_map/ppermute | solution.py:380
  85.2 1.6 %collective-permute-start.23 = (bf16[72,2176]{1,0:T(8,128)(2,1)S(1)}, bf16[72,2176]{1,0:T(8,128)(2,1)S(1)}, u32[]{:S(2)}, u32[]{:S(2)}) collective-permute-start(bf16[72,2176]{1,0:T(8,128)(2,1)S(1)} %add_convert_fusion.3), channel_id=1, source_target_pairs={{0,8},{8,16},{16,24},{24,28},{28,20},{20,12},{12,4},{4,0},{1,9},{9... | collective-permute-start | bytes 940040 | tf_op jit(solution)/shard_map/ppermute | solution.py:376
  92.5 1.6 %collective-permute-start.29 = (bf16[72,2048]{1,0:T(8,128)(2,1)S(1)}, bf16[72,2048]{1,0:T(8,128)(2,1)S(1)}, u32[]{:S(2)}, u32[]{:S(2)}) collective-permute-start(bf16[72,2048]{1,0:T(8,128)(2,1)S(1)} %add_convert_fusion.6), channel_id=1, source_target_pairs={{0,8},{8,16},{16,24},{24,28},{28,20},{20,12},{12,4},{4,0},{1,9},{9... | collective-permute-start | bytes 884744 | tf_op jit(solution)/shard_map/ppermute | solution.py:376
  95.5 2.7 %collective-permute-done.24 = bf16[72,2048]{1,0:T(8,128)(2,1)S(1)} collective-permute-done((bf16[72,2048]{1,0:T(8,128)(2,1)S(1)}, bf16[72,2048]{1,0:T(8,128)(2,1)S(1)}, u32[]{:S(2)}, u32[]{:S(2)}) %collective-permute-start.24) | collective-permute-done | bytes 294944 | tf_op jit(solution)/shard_map/ppermute | solution.py:380
  104.9 4.2 %collective-permute-done.30.rest_5_ = bf16[72,2048]{1,0:T(8,128)(2,1)S(1)} collective-permute-done((bf16[72,2048]{1,0:T(8,128)(2,1)S(1)}, bf16[72,2048]{1,0:T(8,128)(2,1)S(1)}, u32[]{:S(2)}, u32[]{:S(2)}) %collective-permute-start.30) | collective-permute-done | bytes 294944 | tf_op jit(solution)/shard_map/ppermute | solution.py:380
  109.0 1.8 %unfold.1 = f32[72,8192]{1,0:T(8,128)} custom-call(f32[72,2176]{1,0:T(8,128)S(1)} %get-tuple-element.131.rest_0_, bf16[72,2176]{1,0:T(8,128)(2,1)S(1)} %collective-permute-done.27.rest_1_, bf16[72,2176]{1,0:T(8,128)(2,1)S(1)} %collective-permute-done.28.rest_2_, f32[72,2048]{1,0:T(8,128)S(1)} %get-tuple-element.136.rest_3_, ...), custom_call_target="tpu_custom_call" | custom-call | tf_op jit(solution)/shard_map/unfold/pallas_call | solution.py:150
  (97 shorter events, 41.7 us)
Async XLA Ops:
  1.9 13.5 %collective-permute-start = (bf16[72,2176]{1,0:T(8,128)(2,1)S(1)}, bf16[72,2176]{1,0:T(8,128)(2,1)S(1)}, u32[]{:S(2)}, u32[]{:S(2)}) collective-permute-start(bf16[72,2176]{1,0:T(8,128)(2,1)S(1)} %get-tuple-element.73.rest_2_), channel_id=1, source_target_pairs={{0,8},{8,16},{16,24},{24,28},{28,20},{20,12},{12,4},{4,0},{1,9},{9... | collective-permute-start | bytes 940040 | tf_op jit(solution)/shard_map/ppermute | solution.py:376
  4.9 14.6 %collective-permute-start.4 = (bf16[72,2048]{1,0:T(8,128)(2,1)S(1)}, bf16[72,2048]{1,0:T(8,128)(2,1)}, u32[]{:S(2)}, u32[]{:S(2)}) collective-permute-start(bf16[72,2048]{1,0:T(8,128)(2,1)S(1)} %get-tuple-element.74.rest_5_), channel_id=1, source_target_pairs={{0,8},{8,16},{16,24},{24,28},{28,20},{20,12},{12,4},{4,0},{1,9},{9... | collective-permute-start | bytes 884744 | tf_op jit(solution)/shard_map/ppermute | solution.py:376
  7.0 14.7 %collective-permute-start.5 = (bf16[72,2176]{1,0:T(8,128)(2,1)S(1)}, bf16[72,2176]{1,0:T(8,128)(2,1)}, u32[]{:S(2)}, u32[]{:S(2)}) collective-permute-start(bf16[72,2176]{1,0:T(8,128)(2,1)S(1)} %get-tuple-element.73.rest_2_), channel_id=1, source_target_pairs={{8,0},{16,8},{24,16},{28,24},{20,28},{12,20},{4,12},{0,4},{9,1},{1... | collective-permute-start | bytes 940040 | tf_op jit(solution)/shard_map/ppermute | solution.py:380
  15.4 12.9 %collective-permute-start.2 = (bf16[72,2176]{1,0:T(8,128)(2,1)S(1)}, bf16[72,2176]{1,0:T(8,128)(2,1)}, u32[]{:S(2)}, u32[]{:S(2)}) collective-permute-start(bf16[72,2176]{1,0:T(8,128)(2,1)S(1)} %collective-permute-done.rest_3_), channel_id=1, source_target_pairs={{0,8},{8,16},{16,24},{24,28},{28,20},{20,12},{12,4},{4,0},{1,9},{9... | collective-permute-start | bytes 940040 | tf_op jit(solution)/shard_map/ppermute | solution.py:376
  17.4 10.8 %collective-permute-start.3 = (bf16[72,2048]{1,0:T(8,128)(2,1)S(1)}, bf16[72,2048]{1,0:T(8,128)(2,1)}, u32[]{:S(2)}, u32[]{:S(2)}) collective-permute-start(bf16[72,2048]{1,0:T(8,128)(2,1)S(1)} %collective-permute-done.1.rest_7_), channel_id=1, source_target_pairs={{8,0},{16,8},{24,16},{28,24},{20,28},{12,20},{4,12},{0,4},{9,1},{1... | collective-permute-start | bytes 884744 | tf_op jit(solution)/shard_map/ppermute | solution.py:380
  21.7 13.0 %collective-permute-start.9 = (bf16[72,2176]{1,0:T(8,128)(2,1)}, bf16[72,2176]{1,0:T(8,128)(2,1)}, u32[]{:S(2)}, u32[]{:S(2)}) collective-permute-start(bf16[72,2176]{1,0:T(8,128)(2,1)} %collective-permute-done.5.rest_4_), channel_id=1, source_target_pairs={{8,0},{16,8},{24,16},{28,24},{20,28},{12,20},{4,12},{0,4},{9,1},{1... | collective-permute-start | bytes 940040 | tf_op jit(solution)/shard_map/ppermute | solution.py:380
  21.7 10.8 %collective-permute-start.8 = (bf16[72,2048]{1,0:T(8,128)(2,1)}, bf16[72,2048]{1,0:T(8,128)(2,1)}, u32[]{:S(2)}, u32[]{:S(2)}) collective-permute-start(bf16[72,2048]{1,0:T(8,128)(2,1)} %collective-permute-done.4.rest_6_), channel_id=1, source_target_pairs={{0,8},{8,16},{16,24},{24,28},{28,20},{20,12},{12,4},{4,0},{1,9},{9... | collective-permute-start | bytes 884744 | tf_op jit(solution)/shard_map/ppermute | solution.py:376
  28.2 13.0 %collective-permute-start.6 = (bf16[72,2176]{1,0:T(8,128)(2,1)}, bf16[72,2176]{1,0:T(8,128)(2,1)}, u32[]{:S(2)}, u32[]{:S(2)}) collective-permute-start(bf16[72,2176]{1,0:T(8,128)(2,1)} %collective-permute-done.2.rest_8_), channel_id=1, source_target_pairs={{0,8},{8,16},{16,24},{24,28},{28,20},{20,12},{12,4},{4,0},{1,9},{9... | collective-permute-start | bytes 940040 | tf_op jit(solution)/shard_map/ppermute | solution.py:376
  29.9 11.4 %collective-permute-start.7 = (bf16[72,2048]{1,0:T(8,128)(2,1)}, bf16[72,2048]{1,0:T(8,128)(2,1)S(1)}, u32[]{:S(2)}, u32[]{:S(2)}) collective-permute-start(bf16[72,2048]{1,0:T(8,128)(2,1)} %collective-permute-done.3.rest_11_), channel_id=1, source_target_pairs={{8,0},{16,8},{24,16},{28,24},{20,28},{12,20},{4,12},{0,4},{9,1},{1... | collective-permute-start | bytes 884744 | tf_op jit(solution)/shard_map/ppermute | solution.py:380
  34.7 13.6 %collective-permute-start.12 = (bf16[72,2048]{1,0:T(8,128)(2,1)}, bf16[72,2048]{1,0:T(8,128)(2,1)S(1)}, u32[]{:S(2)}, u32[]{:S(2)}) collective-permute-start(bf16[72,2048]{1,0:T(8,128)(2,1)} %collective-permute-done.8.rest_10_), channel_id=1, source_target_pairs={{0,8},{8,16},{16,24},{24,28},{28,20},{20,12},{12,4},{4,0},{1,9},{9... | collective-permute-start | bytes 884744 | tf_op jit(solution)/shard_map/ppermute | solution.py:376
  36.3 12.1 %collective-permute-start.13 = (bf16[72,2176]{1,0:T(8,128)(2,1)}, bf16[72,2176]{1,0:T(8,128)(2,1)S(1)}, u32[]{:S(2)}, u32[]{:S(2)}) collective-permute-start(bf16[72,2176]{1,0:T(8,128)(2,1)} %collective-permute-done.9.rest_9_), channel_id=1, source_target_pairs={{8,0},{16,8},{24,16},{28,24},{20,28},{12,20},{4,12},{0,4},{9,1},{1... | collective-permute-start | bytes 940040 | tf_op jit(solution)/shard_map/ppermute | solution.py:380
  41.3 11.5 %collective-permute-start.10 = (bf16[72,2048]{1,0:T(8,128)(2,1)S(1)}, bf16[72,2048]{1,0:T(8,128)(2,1)S(1)}, u32[]{:S(2)}, u32[]{:S(2)}) collective-permute-start(bf16[72,2048]{1,0:T(8,128)(2,1)S(1)} %collective-permute-done.7.rest_5_), channel_id=1, source_target_pairs={{8,0},{16,8},{24,16},{28,24},{20,28},{12,20},{4,12},{0,4},{9,1},{1... | collective-permute-start | bytes 884744 | tf_op jit(solution)/shard_map/ppermute | solution.py:380
  60.5 11.6 %collective-permute-start.17 = (bf16[72,2176]{1,0:T(8,128)(2,1)S(1)}, bf16[72,2176]{1,0:T(8,128)(2,1)S(1)}, u32[]{:S(2)}, u32[]{:S(2)}) collective-permute-start(bf16[72,2176]{1,0:T(8,128)(2,1)S(1)} %get-tuple-element.99), channel_id=1, source_target_pairs={{0,8},{8,16},{16,24},{24,28},{28,20},{20,12},{12,4},{4,0},{1,9},{9... | collective-permute-start | bytes 940040 | tf_op jit(solution)/shard_map/ppermute | solution.py:376
  62.6 14.6 %collective-permute-start.21 = (bf16[72,2048]{1,0:T(8,128)(2,1)S(1)}, bf16[72,2048]{1,0:T(8,128)(2,1)S(1)}, u32[]{:S(2)}, u32[]{:S(2)}) collective-permute-start(bf16[72,2048]{1,0:T(8,128)(2,1)S(1)} %get-tuple-element.108), channel_id=1, source_target_pairs={{0,8},{8,16},{16,24},{24,28},{28,20},{20,12},{12,4},{4,0},{1,9},{9... | collective-permute-start | bytes 884744 | tf_op jit(solution)/shard_map/ppermute | solution.py:376
  64.2 14.6 %collective-permute-start.22 = (bf16[72,2176]{1,0:T(8,128)(2,1)S(1)}, bf16[72,2176]{1,0:T(8,128)(2,1)S(1)}, u32[]{:S(2)}, u32[]{:S(2)}) collective-permute-start(bf16[72,2176]{1,0:T(8,128)(2,1)S(1)} %get-tuple-element.109), channel_id=1, source_target_pairs={{8,0},{16,8},{24,16},{28,24},{20,28},{12,20},{4,12},{0,4},{9,1},{1... | collective-permute-start | bytes 940040 | tf_op jit(solution)/shard_map/ppermute | solution.py:380
  72.2 13.0 %collective-permute-start.19 = (bf16[72,2176]{1,0:T(8,128)(2,1)S(1)}, bf16[72,2176]{1,0:T(8,128)(2,1)S(1)}, u32[]{:S(2)}, u32[]{:S(2)}) collective-permute-start(bf16[72,2176]{1,0:T(8,128)(2,1)S(1)} %add_convert_fusion.4), channel_id=1, source_target_pairs={{0,8},{8,16},{16,24},{24,28},{28,20},{20,12},{12,4},{4,0},{1,9},{9... | collective-permute-start | bytes 940040 | tf_op jit(solution)/shard_map/ppermute | solution.py:376
  73.8 11.3 %collective-permute-start.20 = (bf16[72,2048]{1,0:T(8,128)(2,1)S(1)}, bf16[72,2048]{1,0:T(8,128)(2,1)S(1)}, u32[]{:S(2)}, u32[]{:S(2)}) collective-permute-start(bf16[72,2048]{1,0:T(8,128)(2,1)S(1)} %add_convert_fusion.9), channel_id=1, source_target_pairs={{8,0},{16,8},{24,16},{28,24},{20,28},{12,20},{4,12},{0,4},{9,1},{1... | collective-permute-start | bytes 884744 | tf_op jit(solution)/shard_map/ppermute | solution.py:380
  78.9 11.4 %collective-permute-start.25 = (bf16[72,2048]{1,0:T(8,128)(2,1)S(1)}, bf16[72,2048]{1,0:T(8,128)(2,1)S(1)}, u32[]{:S(2)}, u32[]{:S(2)}) collective-permute-start(bf16[72,2048]{1,0:T(8,128)(2,1)S(1)} %add_convert_fusion.7), channel_id=1, source_target_pairs={{0,8},{8,16},{16,24},{24,28},{28,20},{20,12},{12,4},{4,0},{1,9},{9... | collective-permute-start | bytes 884744 | tf_op jit(solution)/shard_map/ppermute | solution.py:376
  80.6 11.3 %collective-permute-start.26 = (bf16[72,2176]{1,0:T(8,128)(2,1)S(1)}, bf16[72,2176]{1,0:T(8,128)(2,1)S(1)}, u32[]{:S(2)}, u32[]{:S(2)}) collective-permute-start(bf16[72,2176]{1,0:T(8,128)(2,1)S(1)} %add_convert_fusion.2), channel_id=1, source_target_pairs={{8,0},{16,8},{24,16},{28,24},{20,28},{12,20},{4,12},{0,4},{9,1},{1... | collective-permute-start | bytes 940040 | tf_op jit(solution)/shard_map/ppermute | solution.py:380
  85.2 13.0 %collective-permute-start.23 = (bf16[72,2176]{1,0:T(8,128)(2,1)S(1)}, bf16[72,2176]{1,0:T(8,128)(2,1)S(1)}, u32[]{:S(2)}, u32[]{:S(2)}) collective-permute-start(bf16[72,2176]{1,0:T(8,128)(2,1)S(1)} %add_convert_fusion.3), channel_id=1, source_target_pairs={{0,8},{8,16},{16,24},{24,28},{28,20},{20,12},{12,4},{4,0},{1,9},{9... | collective-permute-start | bytes 940040 | tf_op jit(solution)/shard_map/ppermute | solution.py:376
  86.9 11.3 %collective-permute-start.24 = (bf16[72,2048]{1,0:T(8,128)(2,1)S(1)}, bf16[72,2048]{1,0:T(8,128)(2,1)S(1)}, u32[]{:S(2)}, u32[]{:S(2)}) collective-permute-start(bf16[72,2048]{1,0:T(8,128)(2,1)S(1)} %add_convert_fusion.8), channel_id=1, source_target_pairs={{8,0},{16,8},{24,16},{28,24},{20,28},{12,20},{4,12},{0,4},{9,1},{1... | collective-permute-start | bytes 884744 | tf_op jit(solution)/shard_map/ppermute | solution.py:380
  91.9 13.0 %collective-permute-start.28 = (bf16[72,2176]{1,0:T(8,128)(2,1)S(1)}, bf16[72,2176]{1,0:T(8,128)(2,1)S(1)}, u32[]{:S(2)}, u32[]{:S(2)}) collective-permute-start(bf16[72,2176]{1,0:T(8,128)(2,1)S(1)} %add_convert_fusion), channel_id=1, source_target_pairs={{8,0},{16,8},{24,16},{28,24},{20,28},{12,20},{4,12},{0,4},{9,1},{1... | collective-permute-start | bytes 940040 | tf_op jit(solution)/shard_map/ppermute | solution.py:380
  92.5 10.8 %collective-permute-start.29 = (bf16[72,2048]{1,0:T(8,128)(2,1)S(1)}, bf16[72,2048]{1,0:T(8,128)(2,1)S(1)}, u32[]{:S(2)}, u32[]{:S(2)}) collective-permute-start(bf16[72,2048]{1,0:T(8,128)(2,1)S(1)} %add_convert_fusion.6), channel_id=1, source_target_pairs={{0,8},{8,16},{16,24},{24,28},{28,20},{20,12},{12,4},{4,0},{1,9},{9... | collective-permute-start | bytes 884744 | tf_op jit(solution)/shard_map/ppermute | solution.py:376
  98.2 10.8 %collective-permute-start.27 = (bf16[72,2176]{1,0:T(8,128)(2,1)S(1)}, bf16[72,2176]{1,0:T(8,128)(2,1)S(1)}, u32[]{:S(2)}, u32[]{:S(2)}) collective-permute-start(bf16[72,2176]{1,0:T(8,128)(2,1)S(1)} %add_convert_fusion.1), channel_id=1, source_target_pairs={{0,8},{8,16},{16,24},{24,28},{28,20},{20,12},{12,4},{4,0},{1,9},{9... | collective-permute-start | bytes 940040 | tf_op jit(solution)/shard_map/ppermute | solution.py:376
  (22 other events, 223.1 us)
